TPU v7x, 32 devices: a whole 2x2x4 slice. The times are simulated.
32 devices in a mesh: sp: 8 (over y, x, core), tp: 4 (over z).
Axes of the slice: x: 2, y: 2, z: 4, core: 2. Of those that a mesh axis runs over, the one named last changes fastest.
Arguments:
- state: bfloat16 [10, 96, 138240], P(None, 'sp', 'tp'), may hold values from -6 to 6
- cotangent: bfloat16 [10, 96, 138240], P(None, 'sp', 'tp'), may hold values from -6 to 6
- rollout_lengths: int32 [2], replicated, may hold values from 1 to 5, as said below
- channel_sizes: int32 [4], replicated, may hold values from 160 to 161, as said below
- owner_slots: int32 [94], replicated, may hold values from 0 to 95, as said below
- master: float32 [96, 768, 768], P('sp', 'tp')
- first_moment: float32 [96, 768, 768], P('sp', 'tp')
- second_moment: float32 [96, 768, 768], P('sp', 'tp'), as said below
- gains: float32 [2, 768], P(None, 'tp'), may hold values from 0.5 to 1.5
- gain_first: float32 [2, 768], P(None, 'tp'), may hold values from -2048 to 2048
- gain_second: float32 [2, 768], P(None, 'tp'), may hold values from 103680 to 414720
Outputs:
- block_out: bfloat16 [10, 96, 138240], P(None, 'sp', 'tp')
- grad_state: bfloat16 [10, 96, 138240], P(None, 'sp', 'tp')
- new_master: float32 [96, 768, 768], P('sp', 'tp')
- new_copy: bfloat16 [96, 768, 768], P('sp', 'tp')
- new_first: float32 [96, 768, 768], P('sp', 'tp')
- new_second: float32 [96, 768, 768], P('sp', 'tp')
- new_gains: float32 [2, 768], P(None, 'tp')
- new_gain_first: float32 [2, 768], P(None, 'tp')
- new_gain_second: float32 [2, 768], P(None, 'tp')
Inputs may be any that keep to these rules, and one draw needn't show every extreme that they name: `rollout_lengths`: some sample has exactly 5 steps. `channel_sizes`: they sum to 641. `owner_slots`: distinct; slot q lies on sp index q div 12; some sp index owns 12 pieces. `second_moment`: positive.
All inputs are finite; a program needn't handle non-finite values.
Results may differ from a plain program's by a relative error of at most 0.015.
Values may be sent and summed in bfloat16 or wider, within the bound.
No kernel may reach another device: no remote copies, remote signals or barrier semaphores. Data moves between devices by JAX's collectives and lax.ppermute only.
A program may use at most 832 MiB of HBM per device.

v0:
```python
import math

import jax
import jax.numpy as jnp
from jax import lax
from jax.sharding import PartitionSpec as P

CH = 641
NLAT = 90
ROLL = 5


EPS = 1e-05
ADAM_EPS = 1e-08
BIAS_FIX = 1.0 - 0.5**5


def gelu_tanh(value):
    return jax.nn.gelu(value, approximate=True)


def tables(nlat, nlatp, nlon, mmax, mpad):
    rows = jnp.arange(nlat).astype(jnp.float32)
    theta = (rows + 0.5) * (math.pi / nlat)
    cosine = jnp.cos(theta)
    sine = jnp.sin(theta)
    orders = jnp.arange(mmax).astype(jnp.float32)
    steps = jnp.arange(1, mmax).astype(jnp.float32)
    logs = 0.5 * jnp.log((2.0 * steps + 1.0) / (2.0 * steps))
    logcum = jnp.concatenate([jnp.zeros((1,), jnp.float32), jnp.cumsum(logs)])
    diagonal = jnp.exp(
        0.5 * math.log(0.5) + logcum[:, None] + orders[:, None] * jnp.log(sine)[None, :]
    )
    col = orders[:, None]

    def degree_step(carry, degree):
        prev_one, prev_two = carry
        sq = degree * degree
        coef_a = jnp.sqrt(jnp.maximum(4.0 * sq - 1.0, 0.0) / jnp.maximum(sq - col * col, 1.0))
        coef_b = jnp.sqrt(
            jnp.maximum((degree - 1.0) ** 2 - col * col, 0.0)
            / jnp.maximum(4.0 * (degree - 1.0) ** 2 - 1.0, 1.0)
        )
        general = coef_a * (cosine[None, :] * prev_one - coef_b * prev_two)
        current = jnp.where(
            degree == col,
            diagonal,
            jnp.where(
                degree == col + 1.0,
                jnp.sqrt(2.0 * col + 3.0) * cosine[None, :] * prev_one,
                jnp.where(degree > col + 1.0, general, 0.0),
            ),
        )
        return ((current, prev_one), current)

    start = jnp.zeros((mmax, nlat), jnp.float32)
    _, legendre = lax.scan(degree_step, (start, start), orders)
    weights = sine * (math.pi / nlat)
    analysis = jnp.transpose(legendre, (1, 2, 0)) * weights[None, :, None]
    synthesis = jnp.transpose(legendre, (1, 0, 2))
    analysis = jnp.pad(analysis, ((0, mpad - mmax), (0, nlatp - nlat), (0, 0)))
    synthesis = jnp.pad(synthesis, ((0, mpad - mmax), (0, 0), (0, nlatp - nlat)))
    lon = jnp.arange(nlon)
    order_ids = jnp.arange(mmax)
    angle = (lon[:, None] * order_ids[None, :] % nlon).astype(jnp.float32) * (2.0 * math.pi / nlon)
    scale = math.sqrt(2.0 / nlon)
    fwd_basis = jnp.stack([jnp.cos(angle) * scale, -jnp.sin(angle) * scale], axis=1)
    half = jnp.where(order_ids == 0, 0.5, 1.0).astype(jnp.float32)
    inv_basis = jnp.transpose(fwd_basis, (1, 2, 0)) * half[None, :, None]
    fwd_basis = jnp.pad(fwd_basis, ((0, 0), (0, 0), (0, mpad - mmax)))
    inv_basis = jnp.pad(inv_basis, ((0, 0), (0, mpad - mmax), (0, 0)))
    return (
        fwd_basis.astype(jnp.bfloat16),
        analysis.astype(jnp.bfloat16),
        synthesis.astype(jnp.bfloat16),
        inv_basis.astype(jnp.bfloat16),
    )


def channel_sum(value):
    return lax.psum(value, "tp")


def channel_gather(value):
    return lax.all_gather(value, "tp", axis=2, tiled=True)


def channel_partials(value):
    return lax.psum_scatter(
        value.astype(jnp.bfloat16), "tp", scatter_dimension=2, tiled=True
    ).astype(jnp.float32)


def to_pairs(value):
    return lax.all_to_all(value, "sp", split_axis=0, concat_axis=1, tiled=True)


def to_bands(value):
    return lax.all_to_all(value, "sp", split_axis=1, concat_axis=0, tiled=True)


def adamw(param, grad, first, second, rate, decay):
    new_first = 0.5 * first + 0.5 * grad
    new_second = 0.5 * second + 0.5 * grad * grad
    update = new_first / BIAS_FIX / (jnp.sqrt(new_second / BIAS_FIX) + ADAM_EPS)
    return (param - rate * (update + decay * param), new_first, new_second)


def local(
    state,
    cotangent,
    rollout_lengths,
    channel_sizes,
    owner_slots,
    master,
    first_moment,
    second_moment,
    gains,
    gain_first,
    gain_second,
):
    slots, latd, flat = state.shape
    csh = master.shape[1]
    cp = master.shape[2]
    nlon = flat // csh
    n_sp = lax.axis_size("sp")
    sp_index = lax.axis_index("sp")
    tp_index = lax.axis_index("tp")
    degrees = owner_slots.shape[0] - 4
    mpad = (degrees + 31) // 32 * 32
    nlatp = latd * n_sp
    pairs = slots * mpad // n_sp
    owned_count = master.shape[0]
    fwd_basis, analysis, synthesis, inv_basis = tables(NLAT, nlatp, nlon, degrees, mpad)
    chan = jnp.arange(cp)
    chan_mask = (chan % csh < channel_sizes[chan // csh]).astype(jnp.float32)
    local_mask = (jnp.arange(csh) < channel_sizes[tp_index]).astype(jnp.float32)
    hidden_mask = (jnp.arange(2 * csh) < 2 * channel_sizes[tp_index]).astype(jnp.float32)
    lat_mask = (sp_index * latd + jnp.arange(latd) < NLAT).astype(jnp.float32)
    slot_numbers = jnp.arange(slots)
    slot_mask = (slot_numbers % ROLL < rollout_lengths[slot_numbers // ROLL]).astype(jnp.float32)
    spec_mask = local_mask[:, None] * chan_mask[None, :]
    dense_mask = hidden_mask[:, None] * chan_mask[None, :]
    grid_mask = lat_mask[None, :, None, None] * local_mask[None, None, :, None]
    copies = lax.all_gather(master.astype(jnp.bfloat16), "sp", axis=0, tiled=True)
    pieces = copies[owner_slots]
    spec_w = pieces[:degrees] * spec_mask.astype(jnp.bfloat16)[None]
    w_in = jnp.concatenate([pieces[degrees], pieces[degrees + 1]], axis=0) * dense_mask.astype(
        jnp.bfloat16
    )
    w_out = jnp.concatenate([pieces[degrees + 2], pieces[degrees + 3]], axis=0) * dense_mask.astype(
        jnp.bfloat16
    )
    gain_a = gains[0][None, None, :, None]
    gain_b = gains[1][None, None, :, None]
    x_val = state.reshape(slots, latd, csh, nlon).astype(jnp.float32) * grid_mask
    inv_one = lax.rsqrt(channel_sum(jnp.sum(x_val * x_val, axis=2)) / CH + EPS)[:, :, None, :]
    normed = (x_val * inv_one * gain_a).astype(jnp.bfloat16)
    fourier = jnp.einsum("sjcn,nkm->smjkc", normed, fwd_basis, preferred_element_type=jnp.float32)
    fourier = fourier.astype(jnp.bfloat16).reshape(slots * mpad, latd, 2, csh)
    spectral = to_pairs(fourier)
    order_of_pair = (sp_index * pairs + jnp.arange(pairs)) % mpad
    analysis_pairs = analysis[order_of_pair]
    synthesis_pairs = synthesis[order_of_pair]
    coef = jnp.einsum(
        "pjkc,pjl->pkcl", spectral, analysis_pairs, preferred_element_type=jnp.float32
    ).astype(jnp.bfloat16)
    coef_full = channel_gather(coef)
    mixed = jnp.einsum(
        "pkcl,loc->pkol", coef_full, spec_w, preferred_element_type=jnp.float32
    ).astype(jnp.bfloat16)
    synth = jnp.einsum(
        "pkol,plj->pjko", mixed, synthesis_pairs, preferred_element_type=jnp.float32
    ).astype(jnp.bfloat16)
    bands = to_bands(synth).reshape(slots, mpad, latd, 2, csh)
    spec_out = jnp.einsum("smjko,kmn->sjon", bands, inv_basis, preferred_element_type=jnp.float32)
    resid = x_val + spec_out
    inv_two = lax.rsqrt(channel_sum(jnp.sum(resid * resid, axis=2)) / CH + EPS)[:, :, None, :]
    normed_two = (resid * inv_two * gain_b).astype(jnp.bfloat16)
    grad_out = (
        cotangent.reshape(slots, latd, csh, nlon).astype(jnp.float32)
        * slot_mask[:, None, None, None]
        * grid_mask
    )
    mlp_in = channel_gather(normed_two)
    pre_act = jnp.einsum("sjcn,hc->sjhn", mlp_in, w_in, preferred_element_type=jnp.float32)
    act_val, gelu_pull = jax.vjp(gelu_tanh, pre_act)
    act = act_val.astype(jnp.bfloat16)
    mlp_out = channel_partials(
        jnp.einsum("sjhn,hc->sjcn", act, w_out, preferred_element_type=jnp.float32)
    )
    result = resid + mlp_out
    grad_full = channel_gather(grad_out.astype(jnp.bfloat16))
    grad_act = jnp.einsum("sjcn,hc->sjhn", grad_full, w_out, preferred_element_type=jnp.float32)
    grad_w_out = jnp.einsum("sjcn,sjhn->hc", grad_full, act, preferred_element_type=jnp.float32)
    grad_pre = gelu_pull(grad_act)[0].astype(jnp.bfloat16)
    grad_w_in = jnp.einsum("sjcn,sjhn->hc", mlp_in, grad_pre, preferred_element_type=jnp.float32)
    grad_two = channel_partials(
        jnp.einsum("sjhn,hc->sjcn", grad_pre, w_in, preferred_element_type=jnp.float32)
    )
    proj_two = channel_sum(jnp.sum(resid * gain_b * grad_two, axis=2))[:, :, None, :]
    grad_resid = grad_out + inv_two * gain_b * grad_two - resid * inv_two**3 * proj_two / CH
    gain_grad_two = jnp.sum(grad_two * resid * inv_two, axis=(0, 1, 3))
    grad_bands = jnp.einsum(
        "sjon,kmn->smjko",
        grad_resid.astype(jnp.bfloat16),
        inv_basis,
        preferred_element_type=jnp.float32,
    )
    grad_bands = grad_bands.astype(jnp.bfloat16).reshape(slots * mpad, latd, 2, csh)
    grad_synth = to_pairs(grad_bands)
    grad_mixed = jnp.einsum(
        "pjko,plj->pkol", grad_synth, synthesis_pairs, preferred_element_type=jnp.float32
    ).astype(jnp.bfloat16)
    grad_spec_w = jnp.einsum(
        "pkcl,pkol->loc", coef_full, grad_mixed, preferred_element_type=jnp.float32
    )
    grad_coef = channel_partials(
        jnp.einsum("pkol,loc->pkcl", grad_mixed, spec_w, preferred_element_type=jnp.float32)
    ).astype(jnp.bfloat16)
    grad_spectral = jnp.einsum(
        "pkcl,pjl->pjkc", grad_coef, analysis_pairs, preferred_element_type=jnp.float32
    ).astype(jnp.bfloat16)
    grad_fourier = to_bands(grad_spectral).reshape(slots, mpad, latd, 2, csh)
    grad_normed = jnp.einsum(
        "smjkc,nkm->sjcn", grad_fourier, fwd_basis, preferred_element_type=jnp.float32
    )
    proj_one = channel_sum(jnp.sum(x_val * gain_a * grad_normed, axis=2))[:, :, None, :]
    grad_in = (
        grad_resid + inv_one * gain_a * grad_normed - x_val * inv_one**3 * proj_one / CH
    ) * grid_mask
    gain_grad_one = jnp.sum(grad_normed * x_val * inv_one, axis=(0, 1, 3))
    gain_grads = lax.psum(jnp.stack([gain_grad_one, gain_grad_two]), "sp")
    grad_spec_w = grad_spec_w * spec_mask[None]
    grad_w_in = grad_w_in * dense_mask
    grad_w_out = grad_w_out * dense_mask
    piece_grads = jnp.concatenate(
        [
            grad_spec_w,
            grad_w_in[None, :csh],
            grad_w_in[None, csh:],
            grad_w_out[None, :csh],
            grad_w_out[None, csh:],
        ],
        axis=0,
    )
    slot_grads = (
        jnp.zeros((owned_count * n_sp, csh, cp), jnp.float32).at[owner_slots].set(piece_grads)
    )
    owned_grads = lax.psum_scatter(slot_grads, "sp", scatter_dimension=0, tiled=True)
    new_master, new_first, new_second = adamw(
        master, owned_grads, first_moment, second_moment, 0.03, 0.01
    )
    new_gains, gain_one, gain_two = adamw(gains, gain_grads, gain_first, gain_second, 0.5, 0.0)
    return (
        result.reshape(slots, latd, flat).astype(jnp.bfloat16),
        grad_in.reshape(slots, latd, flat).astype(jnp.bfloat16),
        new_master,
        new_master.astype(jnp.bfloat16),
        new_first,
        new_second,
        new_gains,
        gain_one,
        gain_two,
    )


def solution(mesh):
    return jax.shard_map(
        local,
        mesh=mesh,
        in_specs=(
            P(None, "sp", "tp"),
            P(None, "sp", "tp"),
            P(),
            P(),
            P(),
            P("sp", "tp", None),
            P("sp", "tp", None),
            P("sp", "tp", None),
            P(None, "tp"),
            P(None, "tp"),
            P(None, "tp"),
        ),
        out_specs=(
            P(None, "sp", "tp"),
            P(None, "sp", "tp"),
            P("sp", "tp", None),
            P("sp", "tp", None),
            P("sp", "tp", None),
            P("sp", "tp", None),
            P(None, "tp"),
            P(None, "tp"),
            P(None, "tp"),
        ),
        check_vma=False,
    )
```

profile of v0, /device:TPU:0, one launch (start us, length us, event | category | flops | bytes accessed | tf_op | source)
XLA Modules:
  0.0 7296.9 jit_solution(5134488554415538168)
XLA Ops:
  11.5 36.9 reshape.556
  48.4 24.8 copy.132
  73.2 36.9 reshape.557
  110.2 24.8 copy.149
  163.0 30.8 all-reduce.11.cloned.1.call-done
  207.6 32.3 copy.135
  245.7 426.1 %while.21 = (s32[]{:T(128)}, f32[90,90]{1,0:T(8,128)S(1)}, f32[90,90]{1,0:T(8,128)S(1)}, f32[90,90,90]{2,1,0:T(8,128)}, f32[90]{0:T(128)S(1)}, /*index=5*/f32[90...) while((s32[]{:T(128)}, f32[90,90]{1,0:T(8,128)S(1)}, ...), condition=%wide.region_2.3_spmd.clone.clone.clone.clone, body=%wide.region_1.2_spmd.clone.clone.clone.clone.sunk | while | flops 99012 | bytes 183543 | solution.py:57
  685.8 31.2 copy.190
  757.4 25.9 gather_fusion.1
  783.3 744.1 %all-gather.7.cloned.1.call-done = bf16[120,2,768,90]{3,2,1,0:T(8,128)(2,1)} async-done(((bf16[120,2,192,90]{3,2,1,0:T(8,128)(2,1)}), bf16[120,2,768,90]{3,2,1,0:T(8,128)(2,1)}) %all-gather.7.cloned.1.call-update) | async-done | bytes 33177616 | tf_op jit(solution)/shard_map/all_gather | solution.py:85
  1527.4 64.6 copy.140
  1591.9 25.8 convert_bitcast_fusion.5
  1668.6 105.2 %all-to-all-done.1 = bf16[120,96,2,192]{0,3,2,1:T(8,128)(2,1)} async-done(((bf16[120,96,2,192]{0,3,2,1:T(8,128)(2,1)}), bf16[120,96,2,192]{0,3,2,1:T(8,128)(2,1)}, u32[]{:S(2)}, u32[]{:S(2)}) %all-to-all-start.1) | async-done | bytes 8847392 | tf_op jit(solution)/shard_map/all_to_all | solution.py:99
  1788.4 23.1 multiply_reduce_fusion
  1811.5 31.2 all-reduce.13.cloned.1.call-done
  1880.3 24.4 copy.150
  1907.1 1015.4 %all-gather.9.cloned.1.call-done = bf16[10,12,768,180]{3,1,0,2:T(8,128)(2,1)} async-done(((bf16[10,12,192,180]{3,1,0,2:T(8,128)(2,1)}), bf16[10,12,768,180]{3,1,0,2:T(8,128)(2,1)}) %all-gather.9.cloned.1.call-update) | async-done | bytes 33177616 | tf_op jit(solution)/shard_map/all_gather | solution.py:85
  2922.5 83.0 %fusion.40 = (bf16[10,12,384,180]{2,3,1,0:T(8,128)(2,1)}, f32[384,10,12,180]{0,3,2,1:T(8,128)}) fusion(bf16[10,12,768,180]{3,1,0,2:T(8,128)(2,1)} %all-gather.9.cloned.1.call-done, bf16[192,768]{1,0:T(8,128)(2,1)S(1)} %get-tuple-element.304, bf16[192,768]{1,0:T(8,128)(2,1)S(1)} %get-tuple-element.302, f32[768]{0:T(1024)S(1)} %copy-done.37, f32[384]{0:T(512)S(1)} %fusion.149), kind=kOutput, calls=%fused_computation.56 | convolution fusion | flops 12817207296 | bytes 83538432 | tf_op jit(solution)/shard_map/sjcn,hc->sjhn/dot_general | solution.py:186
  3005.5 959.0 %all-gather.11.cloned.1.call-done = bf16[10,12,768,180]{3,1,0,2:T(8,128)(2,1)} async-done(((bf16[10,12,192,180]{3,1,0,2:T(8,128)(2,1)}), bf16[10,12,768,180]{3,1,0,2:T(8,128)(2,1)}) %all-gather.11.cloned.1.call-update) | async-done | bytes 33177616 | tf_op jit(solution)/shard_map/all_gather | solution.py:85
  3964.5 57.5 fusion.36
  4022.0 29.4 convert_bitcast_fusion
  4051.4 74.8 %copy.196 = bf16[10,12,768,180]{3,1,0,2:T(8,128)(2,1)} copy(bf16[10,12,768,180]{2,3,1,0:T(8,128)(2,1)} %convert_bitcast_fusion) | data formatting | bytes 66355200
  4126.2 70.2 reshape.651
  4196.5 543.2 %reduce-scatter.12.cloned.1.call-done = bf16[192,21600]{1,0:T(8,128)(2,1)} async-done(((bf16[768,21600]{1,0:T(8,128)(2,1)}), bf16[192,21600]{1,0:T(8,128)(2,1)}) %reduce-scatter.12.cloned.1.call-update) | async-done | bytes 8294416
  4739.7 28.4 reshape.652
  4805.1 36.3 all-reduce.15.cloned.1.call-done
  4862.3 50.2 copy.153
  4912.5 134.1 %all_to_all.66 = bf16[960,12,2,192]{3,2,1,0:T(2,128)(2,1)} all-to-all(bf16[960,12,2,192]{3,2,1,0:T(2,128)(2,1)S(1)} %copy.153), channel_id=1, replica_groups=mesh['sp'=8,'tp'=4] {'sp'}, dimensions={0} | all-to-all | bytes 17694720 | tf_op jit(solution)/shard_map/all_to_all | solution.py:95
  5046.6 31.1 copy.192
  5120.3 26.2 convert_bitcast_fusion.2
  5146.4 86.3 %copy.159 = bf16[120,2,768,90]{0,1,3,2:T(2,128)(2,1)} copy(bf16[120,2,768,90]{2,0,1,3:T(8,128)(2,1)} %convert_bitcast_fusion.2) | data formatting | bytes 66355200 | tf_op jit(solution)/shard_map/convert_element_type | solution.py:90
  5233.8 30.5 convert_bitcast_fusion.1
  5264.3 74.9 %copy.194 = bf16[10,12,768,180]{3,1,0,2:T(8,128)(2,1)} copy(bf16[10,12,768,180]{2,3,1,0:T(8,128)(2,1)} %convert_bitcast_fusion.1) | data formatting | bytes 66355200
  5339.1 70.5 reshape.649
  5411.5 64.9 copy.184
  5476.5 91.0 %multiply_multiply_fusion.4 = f32[384,768]{1,0:T(8,128)} fusion(bf16[10,12,768,180]{3,1,0,2:T(8,128)(2,1)} %all-gather.11.cloned.1.call-done, bf16[10,12,384,180]{2,3,1,0:T(8,128)(2,1)} %get-tuple-element.327, f32[768]{0:T(1024)S(1)} %copy-done.38, f32[384]{0:T(512)S(1)} %copy-done.47), kind=kOutput, calls=%fused_computation.123 | convolution fusion | flops 12740788224 | bytes 50950656 | tf_op jit(solution)/shard_map/sjcn,sjhn->hc/dot_general | solution.py:195
  5567.5 825.9 %all-reduce.19.cloned.1.call-done = bf16[120,2,768,90]{0,1,3,2:T(2,128)(2,1)} async-done(((bf16[120,2,768,90]{0,1,3,2:T(2,128)(2,1)}), bf16[120,2,768,90]{0,1,3,2:T(2,128)(2,1)}) %all-reduce.19.cloned.1.call-update) | async-done | bytes 33177616
  6466.0 90.0 %multiply_multiply_fusion.5 = f32[384,768]{1,0:T(8,128)S(1)} fusion(bf16[10,12,768,180]{3,1,0,2:T(8,128)(2,1)} %all-gather.9.cloned.1.call-done, bf16[10,12,384,180]{2,3,1,0:T(8,128)(2,1)} %fusion.36, f32[768]{0:T(1024)S(1)} %copy-done.38, f32[384]{0:T(512)S(1)} %copy-done.47), kind=kOutput, calls=%fused_computation.124 | convolution fusion | flops 12740788224 | bytes 50950656 | tf_op jit(solution)/shard_map/sjcn,sjhn->hc/dot_general | solution.py:197
  6556.1 35.9 fusion.21
  6609.4 26.4 fusion.53
  6654.8 97.3 %scatter_fusion = f32[96,192,768]{2,1,0:T(8,128)} fusion(f32[96,192,768]{2,1,0:T(8,128)} %broadcast_in_dim.114, s32[94]{0:T(128)S(1)} %copy-done.49, f32[94,192,768]{2,1,0:T(8,128)} %fusion.116), kind=kCustom, calls=%fused_computation.3 | custom fusion | bytes 166330752 | tf_op jit(solution)/shard_map/scatter | solution.py:248
  6752.3 192.5 %reduce-scatter.10.cloned.1.call-done = bf16[192,21600]{1,0:T(8,128)(2,1)} async-done(((bf16[768,21600]{1,0:T(8,128)(2,1)}), bf16[192,21600]{1,0:T(8,128)(2,1)}) %reduce-scatter.10.cloned.1.call-update) | async-done | bytes 8294416
  6944.7 28.3 reshape.650
  6973.0 23.8 copy.195
  7011.0 48.1 fusion.50
  7075.5 22.6 convert_element_type.278
  7114.0 22.6 convert_element_type.261
  7136.6 132.6 %reduce-scatter.8.cloned.1.call-done = f32[12,192,768]{2,1,0:T(8,128)} async-done(((f32[96,192,768]{2,1,0:T(8,128)}), f32[12,192,768]{2,1,0:T(8,128)}) %reduce-scatter.8.cloned.1.call-update) | async-done | bytes 7077904 | tf_op jit(solution)/shard_map/reduce_scatter | solution.py:250
  (845 shorter events, 737.0 us)
Async XLA Ops:
  8.0 185.7 %all-reduce.11.cloned.1.call-start = ((), (), s32[]{:S(2)}) async-start(), calls=%async_computation.8 | async-start | bytes 327680 | tf_op jit(solution)/shard_map/psum | solution.py:81
  136.4 59.0 copy-start.18
  156.3 601.1 %all-gather.5.cloned.1.call-start = ((), (), s32[]{:S(2)}) async-start(), calls=%async_computation.7 | async-start | bytes 31850496 | tf_op jit(solution)/shard_map/all_gather | solution.py:145
  162.0 45.5 copy-start.11
  162.0 45.5 copy-start.13
  162.6 44.9 copy-start.39
  239.9 445.9 %all-to-all-start = ((bf16[960,12,2,192]{3,2,1,0:T(2,128)(2,1)}), bf16[960,12,2,192]{3,2,1,0:T(2,128)(2,1)}, u32[]{:S(2)}, u32[]{:S(2)}) async-start(bf16[960,12,2,192]{3,2,1,0:T(2,128)(2,1)} %copy.135), calls=%async_computation | async-start | bytes 23592960 | tf_op jit(solution)/shard_map/all_to_all | solution.py:95
  245.2 1282.1 %all-gather.7.cloned.1.call-start = ((), (), s32[]{:S(2)}) async-start(), calls=%async_computation.9 | async-start | bytes 58982400 | tf_op jit(solution)/shard_map/all_gather | solution.py:85
  685.8 56.8 copy-start.2
  752.5 881.5 %copy-start = (bf16[120,90,96]{2,1,0:T(8,128)(2,1)}, bf16[120,90,96]{2,1,0:T(8,128)(2,1)S(1)}, u32[]{:S(2)}) copy-start(bf16[120,90,96]{2,1,0:T(8,128)(2,1)S(1)} %gather_fusion) | copy-start | bytes 6220804
  757.4 834.5 %copy-start.30 = (bf16[192,768]{1,0:T(8,128)(2,1)}, bf16[192,768]{1,0:T(8,128)(2,1)S(1)}, u32[]{:S(2)}) copy-start(bf16[192,768]{1,0:T(8,128)(2,1)S(1)} %get-tuple-element.314) | copy-start | bytes 884740
  1663.2 125.2 %copy-start.19 = (f32[12,192]{1,0:T(8,128)S(1)}, f32[12,192]{1,0:T(8,128)}, u32[]{:S(2)}) copy-start(f32[12,192]{1,0:T(8,128)} %copy-done.18) | copy-start | bytes 27652
  1663.2 110.5 %all-to-all-start.1 = ((bf16[120,96,2,192]{0,3,2,1:T(8,128)(2,1)}), bf16[120,96,2,192]{0,3,2,1:T(8,128)(2,1)}, u32[]{:S(2)}, u32[]{:S(2)}) async-start(bf16[120,96,2,192]{0,3,2,1:T(8,128)(2,1)} %copy.143), calls=%async_computation.1 | async-start | bytes 18874368 | tf_op jit(solution)/shard_map/all_to_all | solution.py:99
  1668.5 174.3 %all-reduce.13.cloned.1.call-start = ((), (), s32[]{:S(2)}) async-start(), calls=%async_computation.10 | async-start | bytes 327680 | tf_op jit(solution)/shard_map/psum | solution.py:81
  1668.6 142.9 %copy-start.24 = (bf16[2,90,180]{1,2,0:T(8,128)(2,1)}, bf16[2,90,180]{1,2,0:T(8,128)(2,1)S(1)}, u32[]{:S(2)}) copy-start(bf16[2,90,180]{1,2,0:T(8,128)(2,1)S(1)} %fusion.128) | copy-start | bytes 194404
  1788.4 56.6 copy-start.33
  1811.5 1111.0 %all-gather.9.cloned.1.call-start = ((), (), s32[]{:S(2)}) async-start(), calls=%async_computation.11 | async-start | bytes 78643200 | tf_op jit(solution)/shard_map/all_gather | solution.py:85
  1880.3 1042.2 %copy-start.37 = (f32[768]{0:T(1024)S(1)}, f32[768]{0:T(1024)}, u32[]{:S(2)}) copy-start(f32[768]{0:T(1024)} %copy-done.36) | copy-start | bytes 9220
  1880.3 2084.2 %all-gather.11.cloned.1.call-start = ((), (), s32[]{:S(2)}) async-start(), calls=%async_computation.12 | async-start | bytes 78643200 | tf_op jit(solution)/shard_map/all_gather | solution.py:85
  1904.8 2834.9 %reduce-scatter.12.cloned.1.call-start = ((), (), s32[]{:S(2)}) async-start(), calls=%async_computation.17 | async-start | bytes 41533440
  1905.6 2116.4 %copy-start.46 = (f32[384]{0:T(512)}, f32[384]{0:T(512)S(1)}, u32[]{:S(2)}) copy-start(f32[384]{0:T(512)S(1)} %fusion.149) | copy-start | bytes 4612
  1907.1 2057.4 %copy-start.26 = (bf16[192,768]{1,0:T(8,128)(2,1)}, bf16[192,768]{1,0:T(8,128)(2,1)S(1)}, u32[]{:S(2)}) copy-start(bf16[192,768]{1,0:T(8,128)(2,1)S(1)} %get-tuple-element.301) | copy-start | bytes 884740
  1907.1 2057.4 %copy-start.28 = (bf16[192,768]{1,0:T(8,128)(2,1)}, bf16[192,768]{1,0:T(8,128)(2,1)S(1)}, u32[]{:S(2)}) copy-start(bf16[192,768]{1,0:T(8,128)(2,1)S(1)} %get-tuple-element.303) | copy-start | bytes 884740
  4196.4 593.0 %copy-start.6 = (f32[10,12,180]{2,1,0:T(8,128)S(1)}, f32[10,12,180]{2,1,0:T(8,128)}, u32[]{:S(2)}) copy-start(f32[10,12,180]{2,1,0:T(8,128)} %copy-done.5) | copy-start | bytes 259204
  4196.4 593.0 %copy-start.34 = (f32[1,192]{1,0:T(1,128)S(1)}, f32[1,192]{1,0:T(1,128)}, u32[]{:S(2)}) copy-start(f32[1,192]{1,0:T(1,128)} %get-tuple-element.315) | copy-start | bytes 2308
  4196.4 645.0 %all-reduce.15.cloned.1.call-start = ((), (), s32[]{:S(2)}) async-start(), calls=%async_computation.13 | async-start | bytes 327680 | tf_op jit(solution)/shard_map/psum | solution.py:81
  4789.4 52.0 copy-start.16
  4789.4 52.0 copy-start.20
  4789.4 52.0 copy-start.25
  4789.4 52.0 copy-start.51
  4805.1 1588.3 %all-reduce.19.cloned.1.call-start = ((), (), s32[]{:S(2)}) async-start(), calls=%async_computation.18 | async-start | bytes 70778880
  5046.6 47.9 copy-start.1
  5232.8 1712.0 %reduce-scatter.10.cloned.1.call-start = ((), (), s32[]{:S(2)}) async-start(), calls=%async_computation.16 | async-start | bytes 41533440
  5567.4 855.1 %copy-start.3 = (bf16[120,96,90]{2,1,0:T(8,128)(2,1)S(1)}, bf16[120,96,90]{2,1,0:T(8,128)(2,1)}, u32[]{:S(2)}) copy-start(bf16[120,96,90]{2,1,0:T(8,128)(2,1)} %copy-done.2) | copy-start | bytes 6220804
  6460.8 133.8 %all-to-all-start.3 = ((bf16[120,96,2,192]{0,3,2,1:T(8,128)(2,1)}), bf16[120,96,2,192]{0,3,2,1:T(8,128)(2,1)}, u32[]{:S(2)}, u32[]{:S(2)}) async-start(bf16[120,96,2,192]{0,3,2,1:T(8,128)(2,1)} %copy.161), calls=%async_computation.3 | async-start | bytes 18874368 | tf_op jit(solution)/shard_map/all_to_all | solution.py:99
  6465.9 90.1 %copy-start.4 = (f32[192,768]{1,0:T(8,128)S(1)}, f32[192,768]{1,0:T(8,128)}, u32[]{:S(2)}) copy-start(f32[192,768]{1,0:T(8,128)} %get-tuple-element.313) | copy-start | bytes 1769476
  6466.0 545.0 %all-reduce.17.cloned.1.call-start = ((), (), s32[]{:S(2)}) async-start(), calls=%async_computation.14 | async-start | bytes 327680 | tf_op jit(solution)/shard_map/psum | solution.py:81
  6635.9 633.4 %reduce-scatter.8.cloned.1.call-start = ((), (), s32[]{:S(2)}) async-start(), calls=%async_computation.15 | async-start | bytes 63700992 | tf_op jit(solution)/shard_map/reduce_scatter | solution.py:250
  6752.2 244.6 %copy-start.43 = (f32[192]{0:T(256)S(1)}, f32[192]{0:T(256)}, u32[]{:S(2)}) copy-start(f32[192]{0:T(256)} %get-tuple-element.271) | copy-start | bytes 2308
  6752.2 258.2 %copy-start.42 = (f32[2,192]{1,0:T(2,128)S(1)}, f32[2,192]{1,0:T(2,128)}, u32[]{:S(2)}) copy-start(f32[2,192]{1,0:T(2,128)} %param.21) | copy-start | bytes 4612
  6752.2 258.1 %copy-start.44 = (f32[2,192]{1,0:T(2,128)S(1)}, f32[2,192]{1,0:T(2,128)}, u32[]{:S(2)}) copy-start(f32[2,192]{1,0:T(2,128)} %param.22) | copy-start | bytes 4612
  6752.2 258.1 %copy-start.45 = (f32[2,192]{1,0:T(2,128)S(1)}, f32[2,192]{1,0:T(2,128)}, u32[]{:S(2)}) copy-start(f32[2,192]{1,0:T(2,128)} %param.23) | copy-start | bytes 4612
  6752.2 258.7 %copy-start.7 = (f32[10,12,180]{2,1,0:T(8,128)S(1)}, f32[10,12,180]{2,1,0:T(8,128)}, u32[]{:S(2)}) copy-start(f32[10,12,180]{2,1,0:T(8,128)} %copy-done.5) | copy-start | bytes 259204
  6752.2 258.7 %copy-start.15 = (f32[10,12,180]{2,1,0:T(8,128)S(1)}, f32[10,12,180]{2,1,0:T(8,128)}, u32[]{:S(2)}) copy-start(f32[10,12,180]{2,1,0:T(8,128)} %get-tuple-element.307) | copy-start | bytes 259204
  6752.3 258.7 %copy-start.17 = (f32[10,12,180]{2,1,0:T(8,128)S(1)}, f32[10,12,180]{2,1,0:T(8,128)}, u32[]{:S(2)}) copy-start(f32[10,12,180]{2,1,0:T(8,128)} %get-tuple-element.309) | copy-start | bytes 259204
  6752.3 258.7 %copy-start.32 = (f32[10,12,180]{2,1,0:T(8,128)S(1)}, f32[10,12,180]{2,1,0:T(8,128)}, u32[]{:S(2)}) copy-start(f32[10,12,180]{2,1,0:T(8,128)} %all-reduce.15.cloned.1.call-done) | copy-start | bytes 259204
  6752.3 258.7 %copy-start.35 = (f32[1,192]{1,0:T(1,128)S(1)}, f32[1,192]{1,0:T(1,128)}, u32[]{:S(2)}) copy-start(f32[1,192]{1,0:T(1,128)} %get-tuple-element.315) | copy-start | bytes 2308
  6752.3 258.7 %copy-start.52 = (f32[10]{0:T(128)S(1)}, f32[10]{0:T(128)}, u32[]{:S(2)}) copy-start(f32[10]{0:T(128)} %copy-done.50) | copy-start | bytes 124
  (22 other events, 303.9 us)
Sparse Core Ops, SparseCore 0:
  156.4 37.3 all-reduce.10
  1811.6 31.0 all-reduce.12
  1880.4 1042.0 all-gather.8
  2923.9 1040.5 all-gather.10
  4805.2 36.2 all-reduce.14
  5232.9 1160.4 all-reduce.18
  6395.9 548.8 reduce-scatter.9
  6948.9 320.2 reduce-scatter.7
Sparse Core Ops, SparseCore 1:
  161.6 224.1 all-gather.4
  742.7 784.6 all-gather.6
  4196.5 543.2 reduce-scatter.11
  6636.0 143.0 all-reduce.16
where the time goes:
time: 7330 us; the launch traced here: 7300 us
  waiting for transfers between devices  4620 us (63%)
  local copies, waits for them, and re-layouts  1390 us (19%)
  matrix products  600 us (8%)
  other arithmetic  331 us (5%)
  loops' own time  177 us (2%)
  blocking collectives  148 us (2%)
    all_gather x3, waiting for transfers between devices, channel_gather(): return lax.all_gather(value, 'tp', axis=2, tiled=True)  2720 us
    unnamed x15, waiting for transfers between devices  1560 us
    unnamed x123, local copies, waits for them, and re-layouts  408 us
    another operation x1, loops' own time, tables(): _, legendre = lax.scan(degree_step, (start, start), orders)  177 us
  transfers between devices with their start and end apart: 15, of which 11 were waited for; matrix products, arithmetic and copies ran while one was open for 19% of the time, Pallas kernels for 0%

commit v1 on v0

v1 whole, which is shorter than its diff:
```python
import functools
import math

import jax
import jax.numpy as jnp
import ml_dtypes
import numpy as np
from jax import lax
from jax.experimental import pallas as pl
from jax.experimental.pallas import tpu as pltpu
from jax.sharding import PartitionSpec as P

CH = 641
CVALID = 161
NLAT = 90
ROLL = 5
EPS = 1e-05
ADAM_EPS = 1e-08
BIAS_FIX = 1.0 - 0.5**5
GELU_A = math.sqrt(2.0 / math.pi)
GELU_B = 0.044715
BF = jnp.bfloat16
F32 = jnp.float32
NT = (((1,), (1,)), ((), ()))
NN = (((1,), (0,)), ((), ()))
TN = (((0,), (0,)), ((), ()))


def mm(a, b, dims=NN):
    return lax.dot_general(a, b, dims, preferred_element_type=F32)


def tables(nlat, nlatp, nlon, mmax, mpad):
    theta = (np.arange(nlat) + 0.5) * (math.pi / nlat)
    cosine, sine = np.cos(theta), np.sin(theta)
    legendre = np.zeros((mmax, mmax, nlat))
    for m in range(mmax):
        value = math.sqrt(0.5) * np.ones(nlat)
        for k in range(1, m + 1):
            value = value * math.sqrt((2 * k + 1) / (2 * k)) * sine
        legendre[m, m] = value
        if m + 1 < mmax:
            legendre[m, m + 1] = math.sqrt(2 * m + 3) * cosine * value
        for l in range(m + 2, mmax):
            a = math.sqrt((4 * l * l - 1) / (l * l - m * m))
            b = math.sqrt(((l - 1) ** 2 - m * m) / (4 * (l - 1) ** 2 - 1))
            legendre[m, l] = a * (cosine * legendre[m, l - 1] - b * legendre[m, l - 2])
    analysis = np.zeros((mpad, mmax, nlatp))
    synthesis = np.zeros((mpad, mmax, nlatp))
    analysis[:mmax, :, :nlat] = legendre * sine * (math.pi / nlat)
    synthesis[:mmax, :, :nlat] = legendre
    angle = (np.arange(mmax)[:, None] * np.arange(nlon)[None, :] % nlon) * (2.0 * math.pi / nlon)
    fwd = np.zeros((mpad, 2, nlon))
    fwd[:mmax, 0] = np.cos(angle) * math.sqrt(2.0 / nlon)
    fwd[:mmax, 1] = -np.sin(angle) * math.sqrt(2.0 / nlon)
    fwd_low = fwd.astype(np.float32).astype(ml_dtypes.bfloat16)
    inv = fwd.copy()
    inv[0] *= 0.5
    inv_low = inv.astype(np.float32).astype(ml_dtypes.bfloat16)
    low = lambda v: v.astype(np.float32).astype(ml_dtypes.bfloat16)
    return (
        fwd_low.reshape(mpad * 2, nlon),
        inv_low.reshape(mpad * 2, nlon),
        low(analysis),
        low(synthesis),
    )


def params(mib):
    return pltpu.CompilerParams(vmem_limit_bytes=mib * 2**20)


def whole(shape):
    return pl.BlockSpec(shape, lambda *_: (0,) * len(shape), pipeline_mode=pl.Buffered(1))


SMEM = pl.BlockSpec(memory_space=pltpu.SMEM)


LANE = 128


def spread(scr, start, value):
    rows, cols = value.shape
    for t in range(cols // LANE):
        scr[t, start : start + rows, :] = value[:, t * LANE : (t + 1) * LANE].astype(F32)


def pick_rows(scr, start, count, stride):
    parts = [scr[t, pl.ds(start, count, stride=stride), :] for t in range(scr.shape[0])]
    return jnp.concatenate(parts, axis=1).astype(BF)


def pack_rows(state, n_tp, each, lanes, tile):
    slots, latd, _ = state.shape

    def body(x_ref, o_ref):
        d = pl.program_id(0)
        parts = []
        for i in range(each):
            v = x_ref[i].astype(F32)
            parts.append(jnp.where(d * each + i < slots, v, 0.0))
        o_ref[0] = jnp.concatenate(parts, axis=0).astype(BF)

    return pl.pallas_call(
        body,
        grid=(n_tp, lanes // tile),
        in_specs=[pl.BlockSpec((each, latd, tile), lambda d, l: (d, 0, l))],
        out_specs=pl.BlockSpec((1, each * latd, tile), lambda d, l: (d, 0, l)),
        out_shape=jax.ShapeDtypeStruct((n_tp, each * latd, lanes), BF),
        compiler_params=params(32),
        name="pack_rows",
    )(state)


def unpack_rows(packed, slots, latd, flat, valid, tile):
    n_tp, rows, lanes = packed.shape
    each = rows // latd
    last = lanes // tile - 1

    def body(x_ref, o_ref):
        l = pl.program_id(1)
        lane = l * tile + lax.broadcasted_iota(jnp.int32, (rows, tile), 1)
        v = jnp.where(lane < valid, x_ref[0].astype(F32), 0.0)
        for i in range(each):
            o_ref[i] = v[i * latd : (i + 1) * latd].astype(BF)

    return pl.pallas_call(
        body,
        grid=(n_tp, pl.cdiv(flat, tile)),
        in_specs=[pl.BlockSpec((1, rows, tile), lambda d, l: (d, 0, jnp.minimum(l, last)))],
        out_specs=pl.BlockSpec((each, latd, tile), lambda d, l: (d, 0, l)),
        out_shape=jax.ShapeDtypeStruct((slots, latd, flat), BF),
        compiler_params=params(32),
        name="unpack_rows",
    )(packed)


def load_transposed(x_ref, row, eye, scr, csh):
    n_tp, cv = x_ref.shape[0], x_ref.shape[2]
    for t in range(n_tp):
        scr[t * csh : t * csh + cv, :] = x_ref[t, row].astype(F32)
    return mm(eye, scr[...].astype(BF), NT)


def store_transposed(o_ref, row, value, eye, csh):
    n_tp, cv = o_ref.shape[0], o_ref.shape[2]
    vt = mm(value, eye, TN)
    for t in range(n_tp):
        o_ref[t, row] = vt[t * csh : t * csh + cv, :].astype(BF)


def fourier(grid5, fwd, eye, gain, cmask, row_mask, n_sp, each, latd, csh):
    n_tp, rows, cv, nlon = grid5.shape
    cp = n_tp * csh
    mk = fwd.shape[0] // n_sp

    def body(x_ref, fb_ref, eye_ref, g_ref, cm_ref, rm_ref, f_ref, xt_ref, scr):
        s, j = pl.program_id(0), pl.program_id(1)
        r = s * latd + j

        @pl.when(r == 0)
        def _():
            scr[...] = jnp.zeros_like(scr)

        xt = load_transposed(x_ref, 0, eye_ref[...], scr, csh) * (cm_ref[...] * rm_ref[r])
        r1 = lax.rsqrt(jnp.sum(xt * xt, axis=1, keepdims=True) / CH + EPS)
        u = (xt * r1 * g_ref[...]).astype(BF)
        f = mm(fb_ref[...], u)
        for d in range(n_sp):
            f_ref[d, 0, 0] = f[d * mk : (d + 1) * mk].astype(BF)
        xt_ref[0] = xt.astype(BF)

    return pl.pallas_call(
        body,
        grid=(each, latd),
        in_specs=[
            pl.BlockSpec((n_tp, 1, cv, nlon), lambda s, j: (0, s * latd + j, 0, 0)),
            whole(fwd.shape),
            whole(eye.shape),
            whole(gain.shape),
            whole(cmask.shape),
            SMEM,
        ],
        out_specs=[
            pl.BlockSpec((n_sp, 1, 1, mk, cp), lambda s, j: (0, j, s, 0, 0)),
            pl.BlockSpec((1, nlon, cp), lambda s, j: (s * latd + j, 0, 0)),
        ],
        out_shape=[
            jax.ShapeDtypeStruct((n_sp, latd, each, mk, cp), BF),
            jax.ShapeDtypeStruct((rows, nlon, cp), BF),
        ],
        scratch_shapes=[pltpu.VMEM((cp, nlon), F32)],
        compiler_params=params(40),
        name="fourier",
    )(grid5, fwd, eye, gain, cmask, row_mask)


def legendre(data, table, inner, per_order, name):
    n_sp, rows, cp = data.shape
    n_mi, n_out, n_in = table.shape
    out_each = n_out // n_sp
    tile = 256

    def body(x_ref, t_ref, o_ref, fin, fout):
        for d in range(n_sp):
            spread(fin, d * rows, x_ref[d])
        for i in range(inner):
            got = pick_rows(fin, i, n_in, inner)
            res = mm(t_ref[(i // per_order) % n_mi], got)
            for d in range(n_sp):
                fout[d, i * out_each : (i + 1) * out_each] = res[d * out_each : (d + 1) * out_each]
        for d in range(n_sp):
            o_ref[d] = fout[d].astype(BF)

    return pl.pallas_call(
        body,
        grid=(cp // tile,),
        in_specs=[pl.BlockSpec((n_sp, rows, tile), lambda c: (0, 0, c)), whole(table.shape)],
        out_specs=pl.BlockSpec((n_sp, inner * out_each, tile), lambda c: (0, 0, c)),
        out_shape=jax.ShapeDtypeStruct((n_sp, inner * out_each, cp), BF),
        scratch_shapes=[
            pltpu.VMEM((tile // LANE, n_sp * rows, LANE), F32),
            pltpu.VMEM((n_sp, inner * out_each, tile), F32),
        ],
        compiler_params=params(56),
        name=name,
    )(data, table)


def mix_forward(coef, weights):
    n_sp, rows, cp = coef.shape
    n_tp, own, csh, _ = weights.shape
    inner = rows // own
    count = n_sp * inner

    def body(x_ref, w_ref, o_ref, a_ref, fin):
        q = pl.program_id(0)

        @pl.when(q == 0)
        def _():
            for d in range(n_sp):
                spread(fin, d * rows, x_ref[d])

        a = pick_rows(fin, q, count, own)
        a_ref[0] = a
        b = mm(a, w_ref[...].reshape(n_tp * csh, cp), NT)
        for d in range(n_sp):
            o_ref[d, 0] = b[d * inner : (d + 1) * inner].astype(BF)

    return pl.pallas_call(
        body,
        grid=(own,),
        in_specs=[
            whole(coef.shape),
            pl.BlockSpec((n_tp, 1, csh, cp), lambda q: (0, q, 0, 0)),
        ],
        out_specs=[
            pl.BlockSpec((n_sp, 1, inner, cp), lambda q: (0, q, 0, 0)),
            pl.BlockSpec((1, count, cp), lambda q: (q, 0, 0)),
        ],
        out_shape=[
            jax.ShapeDtypeStruct((n_sp, own, inner, cp), BF),
            jax.ShapeDtypeStruct((own, count, cp), BF),
        ],
        scratch_shapes=[pltpu.VMEM((cp // LANE, n_sp * rows, LANE), F32)],
        compiler_params=params(60),
        name="mix_forward",
    )(coef, weights)


def mix_backward(grad, weights, coef):
    n_sp, rows, cp = grad.shape
    n_tp, own, csh, _ = weights.shape
    inner = rows // own
    count = n_sp * inner

    def body(x_ref, w_ref, a_ref, o_ref, g_ref, fin):
        q = pl.program_id(0)

        @pl.when(q == 0)
        def _():
            for d in range(n_sp):
                spread(fin, d * rows, x_ref[d])

        g = pick_rows(fin, q, count, own)
        da = mm(g, w_ref[...].reshape(n_tp * csh, cp))
        for d in range(n_sp):
            o_ref[d, 0] = da[d * inner : (d + 1) * inner].astype(BF)
        dw = mm(g, a_ref[0], TN)
        for t in range(n_tp):
            g_ref[t, 0] = dw[t * csh : (t + 1) * csh].astype(BF)

    return pl.pallas_call(
        body,
        grid=(own,),
        in_specs=[
            whole(grad.shape),
            pl.BlockSpec((n_tp, 1, csh, cp), lambda q: (0, q, 0, 0)),
            pl.BlockSpec((1, count, cp), lambda q: (q, 0, 0)),
        ],
        out_specs=[
            pl.BlockSpec((n_sp, 1, inner, cp), lambda q: (0, q, 0, 0)),
            pl.BlockSpec((n_tp, 1, csh, cp), lambda q: (0, q, 0, 0)),
        ],
        out_shape=[
            jax.ShapeDtypeStruct((n_sp, own, inner, cp), BF),
            jax.ShapeDtypeStruct((n_tp, own, csh, cp), BF),
        ],
        scratch_shapes=[pltpu.VMEM((cp // LANE, n_sp * rows, LANE), F32)],
        compiler_params=params(60),
        name="mix_backward",
    )(grad, weights, coef)


def row_block(latd):
    return 2 if latd % 2 == 0 else 1


def grid_block(coef, xt, cot5, w_in, w_out, inv, inv_t, eye, gain, cmask, row_mask, each, latd, csh):
    n_sp, _, rows_s, cp = coef.shape
    n_tp, rows, cv, nlon = cot5.shape
    hid = w_in.shape[0]
    mk = inv.shape[0] // n_sp
    jb = row_block(latd)
    px = jb * nlon

    def body(
        c_ref, xt_ref, ct_ref, wi_ref, wo_ref, ib_ref, it_ref, eye_ref, g_ref, cm_ref, rm_ref,
        out_ref, dg_ref, dh_ref, dwi_ref, dwo_ref, gg_ref,
        fin, scr, hs, dms,
    ):
        s, jj = pl.program_id(0), pl.program_id(1)

        @pl.when((s == 0) & (jj == 0))
        def _():
            scr[...] = jnp.zeros_like(scr)
            dwi_ref[...] = jnp.zeros_like(dwi_ref)
            dwo_ref[...] = jnp.zeros_like(dwo_ref)
            gg_ref[...] = jnp.zeros_like(gg_ref)

        @pl.when(jj == 0)
        def _():
            for d in range(n_sp):
                spread(fin, d * rows_s, c_ref[d, 0])

        for i in range(jb):
            j = jj * jb + i
            g = pick_rows(fin, j, n_sp * mk, latd)
            hs[i] = xt_ref[i].astype(F32) + mm(it_ref[...], g)
            dm = load_transposed(ct_ref, i, eye_ref[...], scr, csh)
            dms[i] = dm * (cm_ref[...] * rm_ref[s * latd + j])
        h = jnp.concatenate([hs[i] for i in range(jb)], axis=0)
        dm = jnp.concatenate([dms[i] for i in range(jb)], axis=0)
        dmb = dm.astype(BF)
        r2 = lax.rsqrt(jnp.sum(h * h, axis=1, keepdims=True) / CH + EPS)
        g1 = g_ref[...]
        v = (h * r2 * g1).astype(BF)
        z = mm(v, wi_ref[...], NT)
        t = jnp.tanh(GELU_A * (z + GELU_B * z * z * z))
        act = (0.5 * z * (1.0 + t)).astype(BF)
        slope = 0.5 * (1.0 + t) + 0.5 * z * (1.0 - t * t) * (
            GELU_A * (1.0 + 3.0 * GELU_B * z * z)
        )
        out = (h + mm(act, wo_ref[...])).astype(BF)
        dz = (slope * mm(dmb, wo_ref[...], NT)).astype(BF)
        dwo_ref[...] += mm(act, dmb, TN)
        dwi_ref[...] += mm(dz, v, TN)
        dv = mm(dz, wi_ref[...])
        gd = g1 * dv
        proj = jnp.sum(h * gd, axis=1, keepdims=True) / CH
        dh = dm + r2 * gd - h * (r2 * r2 * r2 * proj)
        gg_ref[...] += jnp.sum(dv * h * r2, axis=0, keepdims=True)
        for i in range(jb):
            part = dh[i * nlon : (i + 1) * nlon].astype(BF)
            dh_ref[i] = part
            dg = mm(ib_ref[...], part)
            for d in range(n_sp):
                dg_ref[d, i, 0] = dg[d * mk : (d + 1) * mk].astype(BF)
            store_transposed(out_ref, i, out[i * nlon : (i + 1) * nlon], eye_ref[...], csh)

    blocks = latd // jb
    rowmap = lambda s, j: (s * blocks + j, 0, 0)
    rowmap4 = lambda s, j: (0, s * blocks + j, 0, 0)
    return pl.pallas_call(
        body,
        grid=(each, blocks),
        in_specs=[
            pl.BlockSpec((n_sp, 1, rows_s, cp), lambda s, j: (0, s, 0, 0)),
            pl.BlockSpec((jb, nlon, cp), rowmap),
            pl.BlockSpec((n_tp, jb, cv, nlon), rowmap4),
            whole(w_in.shape),
            whole(w_out.shape),
            whole(inv.shape),
            whole(inv_t.shape),
            whole(eye.shape),
            whole(gain.shape),
            whole(cmask.shape),
            SMEM,
        ],
        out_specs=[
            pl.BlockSpec((n_tp, jb, cv, nlon), rowmap4),
            pl.BlockSpec((n_sp, jb, 1, mk, cp), lambda s, j: (0, j, s, 0, 0)),
            pl.BlockSpec((jb, nlon, cp), rowmap),
            pl.BlockSpec((hid, cp), lambda s, j: (0, 0)),
            pl.BlockSpec((hid, cp), lambda s, j: (0, 0)),
            pl.BlockSpec((1, cp), lambda s, j: (0, 0)),
        ],
        out_shape=[
            jax.ShapeDtypeStruct((n_tp, rows, cv, nlon), BF),
            jax.ShapeDtypeStruct((n_sp, latd, each, mk, cp), BF),
            jax.ShapeDtypeStruct((rows, nlon, cp), BF),
            jax.ShapeDtypeStruct((hid, cp), F32),
            jax.ShapeDtypeStruct((hid, cp), F32),
            jax.ShapeDtypeStruct((1, cp), F32),
        ],
        scratch_shapes=[
            pltpu.VMEM((cp // LANE, n_sp * rows_s, LANE), F32),
            pltpu.VMEM((cp, nlon), F32),
            pltpu.VMEM((jb, nlon, cp), F32),
            pltpu.VMEM((jb, nlon, cp), F32),
        ],
        compiler_params=params(62),
        name="grid_block",
    )(coef, xt, cot5, w_in, w_out, inv, inv_t, eye, gain, cmask, row_mask)


def grid_final(coef, xt, dh, fwd_t, eye, gain, cmask, row_mask, each, latd, csh, n_tp, cv):
    n_sp, _, rows_s, cp = coef.shape
    rows, nlon, _ = xt.shape
    mk2 = fwd_t.shape[1]

    def body(c_ref, xt_ref, dh_ref, ft_ref, eye_ref, g_ref, cm_ref, rm_ref, out_ref, gg_ref, fin):
        s, j = pl.program_id(0), pl.program_id(1)

        @pl.when((s == 0) & (j == 0))
        def _():
            gg_ref[...] = jnp.zeros_like(gg_ref)

        @pl.when(j == 0)
        def _():
            for d in range(n_sp):
                spread(fin, d * rows_s, c_ref[d, 0])

        g = pick_rows(fin, j, mk2, latd)
        du = mm(ft_ref[...], g)
        x = xt_ref[0].astype(F32)
        r1 = lax.rsqrt(jnp.sum(x * x, axis=1, keepdims=True) / CH + EPS)
        gd = g_ref[...] * du
        proj = jnp.sum(x * gd, axis=1, keepdims=True) / CH
        res = dh_ref[0].astype(F32) + r1 * gd - x * (r1 * r1 * r1 * proj)
        res = (res * (cm_ref[...] * rm_ref[s * latd + j])).astype(BF)
        gg_ref[...] += jnp.sum(du * x * r1, axis=0, keepdims=True)
        store_transposed(out_ref, 0, res, eye_ref[...], csh)

    rowmap = lambda s, j: (s * latd + j, 0, 0)
    return pl.pallas_call(
        body,
        grid=(each, latd),
        in_specs=[
            pl.BlockSpec((n_sp, 1, rows_s, cp), lambda s, j: (0, s, 0, 0)),
            pl.BlockSpec((1, nlon, cp), rowmap),
            pl.BlockSpec((1, nlon, cp), rowmap),
            whole(fwd_t.shape),
            whole(eye.shape),
            whole(gain.shape),
            whole(cmask.shape),
            SMEM,
        ],
        out_specs=[
            pl.BlockSpec((n_tp, 1, cv, nlon), lambda s, j: (0, s * latd + j, 0, 0)),
            pl.BlockSpec((1, cp), lambda s, j: (0, 0)),
        ],
        out_shape=[
            jax.ShapeDtypeStruct((n_tp, rows, cv, nlon), BF),
            jax.ShapeDtypeStruct((1, cp), F32),
        ],
        scratch_shapes=[pltpu.VMEM((cp // LANE, n_sp * rows_s, LANE), F32)],
        compiler_params=params(48),
        name="grid_final",
    )(coef, xt, dh, fwd_t, eye, gain, cmask, row_mask)


def adamw(param, grad, first, second, rate, decay):
    new_first = 0.5 * first + 0.5 * grad
    new_second = 0.5 * second + 0.5 * grad * grad
    update = new_first / BIAS_FIX / (jnp.sqrt(new_second / BIAS_FIX) + ADAM_EPS)
    return (param - rate * (update + decay * param), new_first, new_second)


def swap(value, axis):
    return lax.all_to_all(value, axis, split_axis=0, concat_axis=0, tiled=True)


def local(
    n_sp, n_tp,
    state, cotangent, rollout_lengths, channel_sizes, owner_slots,
    master, first_moment, second_moment, gains, gain_first, gain_second,
):
    slots, latd, flat = state.shape
    own, csh, cp = master.shape
    nlon = flat // csh
    sp, tp = lax.axis_index("sp"), lax.axis_index("tp")
    degrees = owner_slots.shape[0] - 4
    n_mi = (degrees + n_sp - 1) // n_sp
    mpad = n_mi * n_sp
    each = (slots + n_tp - 1) // n_tp
    inner = each * n_mi * 2
    nlatp = latd * n_sp
    valid = CVALID * nlon
    tile = 19 * 128
    lanes = pl.cdiv(valid, tile) * tile

    fwd, inv, analysis, synthesis = tables(NLAT, nlatp, nlon, degrees, mpad)
    fwd_t, inv_t = jnp.asarray(fwd.T), jnp.asarray(inv.T)
    fwd, inv = jnp.asarray(fwd), jnp.asarray(inv)
    eye = jnp.asarray(np.eye(nlon).astype(ml_dtypes.bfloat16))
    pick = (owner_slots[:degrees, None] == jnp.arange(n_sp * own)[None, :]).astype(BF)
    mine = lambda t: lax.dynamic_slice_in_dim(jnp.asarray(t), sp * n_mi, n_mi, 0)
    by_slot = lambda t: jnp.einsum("mlj,lq->mqj", mine(t), pick, preferred_element_type=F32).astype(BF)
    ana_q, syn_q = by_slot(analysis), by_slot(synthesis)
    ana_j, syn_j = jnp.swapaxes(ana_q, 1, 2), jnp.swapaxes(syn_q, 1, 2)

    chan = jnp.arange(cp)
    cmask = (chan % csh < channel_sizes[chan // csh]).astype(F32)
    rmask = (jnp.arange(csh) < channel_sizes[tp]).astype(F32)
    lat_mask = (sp * latd + jnp.arange(latd) < NLAT).astype(F32)
    slot_ids = tp * each + jnp.arange(each)
    live = slot_ids % ROLL < rollout_lengths[jnp.minimum(slot_ids // ROLL, rollout_lengths.shape[0] - 1)]
    live = (live & (slot_ids < slots)).astype(F32)
    row_mask = jnp.tile(lat_mask, each)
    cot_mask = (live[:, None] * lat_mask[None, :]).reshape(-1)
    cmask2 = cmask[None, :]

    copies = (master * (rmask[:, None] * cmask[None, :])[None]).astype(BF)
    hrow = (jnp.arange(2 * csh) < 2 * channel_sizes[tp]).astype(F32).reshape(2, csh)
    raw = []
    for i in range(4):
        at = owner_slots[degrees + i] - sp * own
        inside = (at >= 0) & (at < own)
        piece = lax.dynamic_index_in_dim(master, jnp.clip(at, 0, own - 1), 0, keepdims=False)
        keep = hrow[i % 2][:, None] * cmask2 * inside.astype(F32)
        raw.append((piece * keep).astype(BF))
    dense = lax.psum(jnp.stack(raw), "sp")
    gains_all = lax.all_gather(gains, "tp", axis=1, tiled=True)
    gain_a, gain_b = gains_all[:1], gains_all[1:]

    def to_grid(value):
        got = swap(pack_rows(value, n_tp, each, lanes, tile), "tp")
        return got[:, :, :valid].reshape(n_tp, each * latd, CVALID, nlon)

    def to_flat(value):
        got = value.reshape(n_tp, each * latd, valid)
        got = swap(jnp.pad(got, ((0, 0), (0, 0), (0, lanes - valid))), "tp")
        return unpack_rows(got, slots, latd, flat, valid, tile)

    x5 = to_grid(state)
    spec_w = lax.all_gather(copies, "tp", axis=0, tiled=False)
    f, xt = fourier(x5, fwd, eye, gain_a, cmask2, row_mask, n_sp, each, latd, csh)
    rows3 = lambda v: v.reshape(n_sp, -1, cp)
    f = swap(rows3(f), "sp")
    coef = swap(legendre(f, ana_q, inner, 2, "analysis"), "sp")
    cot5 = to_grid(cotangent)
    dense = lax.all_gather(dense, "tp", axis=1, tiled=False)
    w_in = dense[:2].reshape(2 * cp, cp)
    w_out = dense[2:].reshape(2 * cp, cp)
    mixed, coef_q = mix_forward(coef, spec_w)
    mixed = swap(rows3(mixed), "sp")
    synth = swap(legendre(mixed, syn_j, inner, 2, "synthesis"), "sp")
    synth = synth.reshape(n_sp, each, -1, cp)
    out5, dg, dh, dwi, dwo, gg_b = grid_block(
        synth, xt, cot5, w_in, w_out, inv, inv_t, eye, gain_b, cmask2, cot_mask, each, latd, csh
    )
    dg = swap(rows3(dg), "sp")
    result = to_flat(out5)
    db = swap(legendre(dg, syn_q, inner, 2, "synthesis_back"), "sp")
    da, dws = mix_backward(db, spec_w, coef_q)
    da = swap(rows3(da), "sp")
    df = swap(legendre(da, ana_j, inner, 2, "analysis_back"), "sp")
    df = df.reshape(n_sp, each, -1, cp)
    g5, gg_a = grid_final(
        df, xt, dh, fwd_t, eye, gain_a, cmask2, row_mask, each, latd, csh, n_tp, CVALID
    )
    grad_state = to_flat(g5)

    spec_g = lax.psum_scatter(dws, "tp", scatter_dimension=0, tiled=False).astype(F32)
    dense_g = jnp.stack([dwi, dwo]).reshape(4, n_tp, csh, cp).astype(BF)
    dense_g = lax.psum_scatter(dense_g, "tp", scatter_dimension=1, tiled=False)
    dense_g = lax.psum(dense_g.astype(F32), "sp")
    grads = spec_g
    for i in range(4):
        hit = (owner_slots[degrees + i] == sp * own + jnp.arange(own))[:, None, None]
        grads = jnp.where(hit, dense_g[i][None], grads)
    new_master, new_first, new_second = adamw(master, grads, first_moment, second_moment, 0.03, 0.01)
    gain_g = lax.psum(jnp.concatenate([gg_a, gg_b], axis=0), ("sp", "tp"))
    gain_g = lax.dynamic_slice_in_dim(gain_g, tp * csh, csh, 1)
    new_gains, gain_one, gain_two = adamw(gains, gain_g, gain_first, gain_second, 0.5, 0.0)
    return (
        result, grad_state, new_master, new_master.astype(BF), new_first, new_second,
        new_gains, gain_one, gain_two,
    )


def solution(mesh):
    wide, slot, gain = P(None, "sp", "tp"), P("sp", "tp", None), P(None, "tp")
    return jax.shard_map(
        functools.partial(local, mesh.shape["sp"], mesh.shape["tp"]),
        mesh=mesh,
        in_specs=(wide, wide, P(), P(), P(), slot, slot, slot, gain, gain, gain),
        out_specs=(wide, wide, slot, slot, slot, slot, gain, gain, gain),
        check_vma=False,
    )
```

time: 7330 us -> 2740 us (0.37)
  waiting for transfers between devices: 4620 us -> 1170 us
  local copies, waits for them, and re-layouts: 1390 us -> 147 us
  blocking collectives: 148 us -> 845 us
  matrix products: 600 us -> 2.43 us
  Pallas kernels: 0 us -> 447 us
  other arithmetic: 331 us -> 43.3 us
  loops' own time: 177 us -> 0 us
    all_gather x4 -> x2, waiting for transfers between devices: 2720 us -> 101 us  [the longest x1 101 us: local(): dense = lax.all_gather(dense, 'tp', axis=1, tiled=False)]
    unnamed x15 -> x6, waiting for transfers between devices: 1560 us -> 0.61 us
    all_to_all x3 -> x10, waiting for transfers between devices: 105 us -> 960 us  [swap(): return lax.all_to_all(value, axis, split_axis=0, concat_axis=0, tiled=True)]
    dot_general x17 -> x2, matrix products: 600 us -> 2.43 us  [local(): jnp.einsum('mlj,lq->mqj', mine(t), pick, preferred_element_type=F32)]
    pallas_call x0 -> x13, Pallas kernels: none -> 447 us  [the longest x1 161 us: grid_block(): pl.pallas_call(body, grid=(each, blocks), in_specs=[pl.BlockSpec((n_sp, 1...]
    all_gather x0 -> x1, blocking collectives: none -> 409 us  [local(): gains_all = lax.all_gather(gains, 'tp', axis=1, tiled=True)]
    unnamed x123 -> x49, local copies, waits for them, and re-layouts: 408 us -> 19.6 us
    convert_element_type x16 -> x3, local copies, waits for them, and re-layouts: 386 us -> 4.35 us  [the longest x1 2.6 us: local(): dense_g = jnp.stack([dwi, dwo]).reshape(4, n_tp, csh, cp).astype(BF)]
  transfers between devices with their start and end apart: 15 -> 16, of which waited for: 11 -> 9; matrix products, arithmetic and copies ran while one was open for 19% -> 6% of each run, Pallas kernels for 0% -> 6%
where the time goes in v1:
time: 2740 us; the launch traced here: 2730 us
  waiting for transfers between devices  1170 us (43%)
  blocking collectives  845 us (31%)
  Pallas kernels  447 us (16%)
  local copies, waits for them, and re-layouts  147 us (5%)
  starting transfers between devices  56.1 us (2%)
  other arithmetic  43.3 us (2%)
    all_to_all x10, waiting for transfers between devices, swap(): return lax.all_to_all(value, axis, split_axis=0, concat_axis=0, tiled=True)  960 us
    all_gather x1, blocking collectives, local(): gains_all = lax.all_gather(gains, 'tp', axis=1, tiled=True)  409 us
    all_to_all x2, blocking collectives, swap(): return lax.all_to_all(value, axis, split_axis=0, concat_axis=0, tiled=True)  248 us
    psum x1, blocking collectives, local(): gain_g = lax.psum(jnp.concatenate([gg_a, gg_b], axis=0), ('sp', 'tp'))  187 us
    pallas_call x1, Pallas kernels, grid_block(): pl.pallas_call(body, grid=(each, blocks), in_specs=[pl.BlockSpec((n_sp, 1...  161 us
    psum x1, waiting for transfers between devices, local(): dense = lax.psum(jnp.stack(raw), 'sp')  110 us
    all_gather x1, waiting for transfers between devices, local(): dense = lax.all_gather(dense, 'tp', axis=1, tiled=False)  101 us
    pallas_call x2, Pallas kernels, unpack_rows(): pl.pallas_call(body, grid=(n_tp, pl.cdiv(flat, tile)), in_specs=[pl.Block...  65.3 us
  transfers between devices with their start and end apart: 16, of which 9 were waited for; matrix products, arithmetic and copies ran while one was open for 6% of the time, Pallas kernels for 6%

profile of v1, /device:TPU:0, one launch (start us, length us, event | category | flops | bytes accessed | tf_op | source)
XLA Modules:
  0.0 2731.2 jit_solution(8144286448548298437)
XLA Ops:
  8.0 4.1 copy-done.5
  12.2 20.5 pack_rows.2
  36.4 6.4 all-to-all-start
  46.9 5.6 multiply_convert_fusion
  52.6 409.4 %all-gather.1 = f32[4,192,2]{1,2,0:T(2,128)S(1)} all-gather(f32[1,192,2]{1,2,0:T(2,128)S(1)} %bitcast.77), channel_id=1, replica_groups=mesh['sp'=8,'tp'=4] {'tp'}, dimensions={0}, use_global_device_ids=true | all-gather | bytes 7680 | tf_op jit(solution)/shard_map/all_gather | solution.py:545
  465.3 7.9 slice.83
  473.2 23.3 reshape.475.x_ref
  496.6 33.7 %fourier.1 = (bf16[8,12,3,24,768]{4,3,2,1,0:T(8,128)(2,1)}, bf16[36,180,768]{2,1,0:T(8,128)(2,1)S(1)}) custom-call(bf16[4,36,161,180]{3,2,1,0:T(8,128)(2,1)} %reshape.475.x_ref, bf16[192,180]{1,0:T(8,128)(2,1)S(1)} %copy-done.9, bf16[180,180]{1,0:T(8,128)(2,1)S(1)} %copy-done.7, f32[1,768]{1,0:T(1,128)S(1)} %get-tuple-element.57.g_ref, ...), custom_call_target="tpu_custom_call" | custom-call | tf_op jit(solution)/shard_map/fourier/pallas_call | solution.py:174
  534.1 5.3 all-to-all-start.1
  541.5 115.8 %all-to-all-done.1.x_ref = bf16[8,864,768]{2,1,0:T(8,128)(2,1)} async-done(((bf16[8,864,768]{2,1,0:T(8,128)(2,1)}), bf16[8,864,768]{2,1,0:T(8,128)(2,1)}, u32[]{:S(2)}, u32[]{:S(2)}) %all-to-all-start.1) | async-done | bytes 10616864 | tf_op jit(solution)/shard_map/all_to_all | solution.py:492
  657.3 11.9 analysis.1
  669.3 5.6 all-to-all-start.2
  675.0 117.9 %all-to-all-done.2.x_ref = bf16[8,864,768]{2,1,0:T(8,128)(2,1)} async-done(((bf16[8,864,768]{2,1,0:T(8,128)(2,1)}), bf16[8,864,768]{2,1,0:T(8,128)(2,1)}, u32[]{:S(2)}, u32[]{:S(2)}) %all-to-all-start.2) | async-done | bytes 10616864 | tf_op jit(solution)/shard_map/all_to_all | solution.py:492
  792.9 24.1 mix_forward.1
  817.0 5.2 all-to-all-start.3
  826.3 20.5 pack_rows.3
  850.5 89.7 %all-to-all-done.3.x_ref = bf16[8,864,768]{2,1,0:T(8,128)(2,1)} async-done(((bf16[8,864,768]{2,1,0:T(8,128)(2,1)}), bf16[8,864,768]{2,1,0:T(8,128)(2,1)}, u32[]{:S(2)}, u32[]{:S(2)}) %all-to-all-start.3) | async-done | bytes 10616864 | tf_op jit(solution)/shard_map/all_to_all | solution.py:492
  940.1 6.0 all-to-all-start.5
  948.2 11.8 synthesis.1
  960.0 186.9 %all-to-all-done.5 = bf16[4,36,29184]{2,1,0:T(8,128)(2,1)} async-done(((bf16[4,36,29184]{2,1,0:T(8,128)(2,1)}), bf16[4,36,29184]{2,1,0:T(8,128)(2,1)}, u32[]{:S(2)}, u32[]{:S(2)}) %all-to-all-start.5) | async-done | bytes 8405024 | tf_op jit(solution)/shard_map/all_to_all | solution.py:492
  1146.9 5.2 all-to-all-start.4
  1159.5 109.9 %all-reduce.5.cloned.1.call-done = bf16[4,1,192,768]{3,2,0,1:T(8,128)(2,1)} async-done(((bf16[4,1,192,768]{3,2,0,1:T(8,128)(2,1)}), bf16[4,1,192,768]{3,2,0,1:T(8,128)(2,1)}) %all-reduce.5.cloned.1.call-update) | async-done | bytes 1179664 | tf_op jit(solution)/shard_map/psum | solution.py:544
  1270.8 100.7 %all-gather.5.cloned.1.call-done = bf16[4,4,192,768]{3,2,0,1:T(8,128)(2,1)} async-done(((bf16[4,1,192,768]{3,2,0,1:T(8,128)(2,1)}), bf16[4,4,192,768]{3,2,0,1:T(8,128)(2,1)}) %all-gather.5.cloned.1.call-update) | async-done | bytes 4718608 | tf_op jit(solution)/shard_map/all_gather | solution.py:564
  1377.3 7.7 slice.85
  1385.1 23.3 reshape.476.ct_ref
  1408.4 160.7 %grid_block.1 = (bf16[4,36,161,180]{3,2,1,0:T(8,128)(2,1)}, bf16[8,12,3,24,768]{4,3,2,1,0:T(8,128)(2,1)}, bf16[36,180,768]{2,1,0:T(8,128)(2,1)}, f32[1536,768]{1...) custom-call(bf16[8,3,288,768]{3,2,1,0:T(8,128)(2,1)} %bitcast.15.c_ref, bf16[36,180,768]{2,1,0:T(8,128)(2,1)} %copy-done.2, ...), custom_call_target="tpu_custom_call" | custom-call | tf_op jit(solution)/shard_map/grid_block/pallas_call | solution.py:385
  1569.1 124.0 %all_to_all.60.x_ref = bf16[8,864,768]{2,1,0:T(8,128)(2,1)} all-to-all(bf16[8,864,768]{2,1,0:T(8,128)(2,1)} %bitcast.66), channel_id=1, replica_groups=mesh['sp'=8,'tp'=4] {'sp'}, dimensions={0} | all-to-all | bytes 21233664 | tf_op jit(solution)/shard_map/all_to_all | solution.py:492
  1693.1 11.9 synthesis_back.1
  1705.0 124.3 %all_to_all.61.x_ref = bf16[8,864,768]{2,1,0:T(8,128)(2,1)} all-to-all(bf16[8,864,768]{2,1,0:T(8,128)(2,1)} %synthesis_back.1), channel_id=1, replica_groups=mesh['sp'=8,'tp'=4] {'sp'}, dimensions={0} | all-to-all | bytes 21233664 | tf_op jit(solution)/shard_map/all_to_all | solution.py:492
  1829.2 32.2 %mix_backward.1 = (bf16[8,12,72,768]{3,2,1,0:T(8,128)(2,1)}, bf16[4,12,192,768]{3,2,1,0:T(8,128)(2,1)}) custom-call(bf16[8,864,768]{2,1,0:T(8,128)(2,1)} %all_to_all.61.x_ref, bf16[4,12,192,768]{3,2,1,0:T(8,128)(2,1)} %bitcast.62, bf16[12,576,768]{2,1,0:T(8,128)(2,1)} %get-tuple-element.28.a_ref), custom_call_target="tpu_custom_call" | custom-call | tf_op jit(solution)/shard_map/mix_backward/pallas_call | solution.py:294
  1861.5 5.2 all-to-all-start.9
  1866.7 4.2 convert_bitcast_fusion
  1874.0 110.6 %all-to-all-done.9.x_ref = bf16[8,864,768]{2,1,0:T(8,128)(2,1)} async-done(((bf16[8,864,768]{2,1,0:T(8,128)(2,1)}), bf16[8,864,768]{2,1,0:T(8,128)(2,1)}, u32[]{:S(2)}, u32[]{:S(2)}) %all-to-all-start.9) | async-done | bytes 10616864 | tf_op jit(solution)/shard_map/all_to_all | solution.py:492
  1984.6 11.9 analysis_back.1
  1996.5 5.2 all-to-all-start.10
  2005.3 16.9 reshape.477
  2022.2 8.1 pad.7
  2030.3 114.6 %all-to-all-done.10 = bf16[8,864,768]{2,1,0:T(8,128)(2,1)} async-done(((bf16[8,864,768]{2,1,0:T(8,128)(2,1)}), bf16[8,864,768]{2,1,0:T(8,128)(2,1)}, u32[]{:S(2)}, u32[]{:S(2)}) %all-to-all-start.10) | async-done | bytes 10616864 | tf_op jit(solution)/shard_map/all_to_all | solution.py:492
  2144.9 6.0 all-to-all-start.6
  2151.0 42.5 %grid_final.1 = (bf16[4,36,161,180]{3,2,1,0:T(8,128)(2,1)}, f32[1,768]{1,0:T(1,128)S(1)}) custom-call(bf16[8,3,288,768]{3,2,1,0:T(8,128)(2,1)} %bitcast.28.c_ref, bf16[36,180,768]{2,1,0:T(8,128)(2,1)} %copy-done.2, bf16[36,180,768]{2,1,0:T(8,128)(2,1)} %get-tuple-element.30.dh_ref, bf16[180,192]{1,0:T(8,128)(2,1)S(1)} %copy-done.10, ...), custom_call_target="tpu_custom_call" | custom-call | tf_op jit(solution)/shard_map/grid_final/pallas_call | solution.py:457
  2193.6 16.9 reshape.478
  2210.5 8.1 pad.8
  2218.5 224.7 %all-to-all-done.6.x_ref = bf16[4,36,29184]{2,1,0:T(8,128)(2,1)} async-done(((bf16[4,36,29184]{2,1,0:T(8,128)(2,1)}), bf16[4,36,29184]{2,1,0:T(8,128)(2,1)}, u32[]{:S(2)}, u32[]{:S(2)}) %all-to-all-start.6) | async-done | bytes 8405024 | tf_op jit(solution)/shard_map/all_to_all | solution.py:492
  2443.2 5.8 all-to-all-start.11
  2453.4 32.6 %unpack_rows.2 = bf16[10,12,34560]{2,1,0:T(8,128)(2,1)} custom-call(bf16[4,36,29184]{2,1,0:T(8,128)(2,1)} %all-to-all-done.6.x_ref), custom_call_target="tpu_custom_call" | custom-call | tf_op jit(solution)/shard_map/unpack_rows/pallas_call | solution.py:128
  2486.1 187.1 %psum.23 = f32[2,768]{1,0:T(2,128)S(1)} all-reduce(f32[2,768]{1,0:T(2,128)S(1)} %pad_maximum_fusion.1), channel_id=1, replica_groups=mesh['sp'=8,'tp'=4] {'sp','tp'}, use_global_device_ids=true, to_apply=%region_4.5 | all-reduce | flops 1536 | bytes 12288 | tf_op jit(solution)/shard_map/psum | solution.py:595
  2673.9 17.1 fusion.35
  2691.0 32.6 %unpack_rows.3 = bf16[10,12,34560]{2,1,0:T(8,128)(2,1)} custom-call(bf16[4,36,29184]{2,1,0:T(8,128)(2,1)} %all-to-all-done.11.x_ref), custom_call_target="tpu_custom_call" | custom-call | tf_op jit(solution)/shard_map/unpack_rows/pallas_call | solution.py:128
  (105 shorter events, 49.9 us)
Async XLA Ops:
  8.0 1261.4 %copy-start = (s32[2]{0:T(128)S(1)}, s32[2]{0:T(128)}, u32[]{:S(2)}) copy-start(s32[2]{0:T(128)} %param.20) | copy-start | bytes 28
  8.0 4.1 copy-start.5
  32.7 3.7 copy-start.3
  36.4 6.5 copy-start.18
  36.4 428.9 %all-to-all-start = ((bf16[4,36,29184]{2,1,0:T(8,128)(2,1)}), bf16[4,36,29184]{2,1,0:T(8,128)(2,1)}, u32[]{:S(2)}, u32[]{:S(2)}) async-start(bf16[4,36,29184]{2,1,0:T(8,128)(2,1)} %copy-done.3), calls=%async_computation | async-start | bytes 18677760 | tf_op jit(solution)/shard_map/all_to_all | solution.py:492
  42.9 632.1 %all-gather.7.cloned.1.call-start = ((), (), s32[]{:S(2)}) async-start(), calls=%async_computation.19 | async-start | bytes 17694720 | tf_op jit(solution)/shard_map/all_gather | solution.py:558
  46.9 5.7 copy-start.19
  464.7 31.9 %copy-start.11 = (f32[1,768]{1,0:T(1,128)}, f32[1,768]{1,0:T(1,128)S(1)}, u32[]{:S(2)}) copy-start(f32[1,768]{1,0:T(1,128)S(1)} %compare_convert_fusion.cm_ref) | copy-start | bytes 9220
  465.3 31.3 %copy-start.13 = (f32[1,768]{1,0:T(1,128)}, f32[1,768]{1,0:T(1,128)S(1)}, u32[]{:S(2)}) copy-start(f32[1,768]{1,0:T(1,128)S(1)} %get-tuple-element.57.g_ref) | copy-start | bytes 9220
  473.2 23.3 copy-start.7
  473.2 23.3 copy-start.9
  530.3 3.8 copy-start.2
  534.1 5.3 copy-start.17
  534.1 123.3 %all-to-all-start.1 = ((bf16[8,864,768]{2,1,0:T(8,128)(2,1)}), bf16[8,864,768]{2,1,0:T(8,128)(2,1)}, u32[]{:S(2)}, u32[]{:S(2)}) async-start(bf16[8,864,768]{2,1,0:T(8,128)(2,1)} %bitcast.65), calls=%async_computation.1 | async-start | bytes 21233664 | tf_op jit(solution)/shard_map/all_to_all | solution.py:492
  540.7 128.6 %copy-start.15 = (bf16[96,12,96]{0,2,1:T(8,128)(2,1)}, bf16[96,12,96]{0,2,1:T(8,128)(2,1)S(1)}, u32[]{:S(2)}) copy-start(bf16[96,12,96]{0,2,1:T(8,128)(2,1)S(1)} %convolution_convert_fusion.1) | copy-start | bytes 663556
  669.3 123.6 %all-to-all-start.2 = ((bf16[8,864,768]{2,1,0:T(8,128)(2,1)}), bf16[8,864,768]{2,1,0:T(8,128)(2,1)}, u32[]{:S(2)}, u32[]{:S(2)}) async-start(bf16[8,864,768]{2,1,0:T(8,128)(2,1)} %analysis.1), calls=%async_computation.2 | async-start | bytes 21233664 | tf_op jit(solution)/shard_map/all_to_all | solution.py:492
  817.0 123.1 %all-to-all-start.3 = ((bf16[8,864,768]{2,1,0:T(8,128)(2,1)}), bf16[8,864,768]{2,1,0:T(8,128)(2,1)}, u32[]{:S(2)}, u32[]{:S(2)}) async-start(bf16[8,864,768]{2,1,0:T(8,128)(2,1)} %bitcast.67), calls=%async_computation.3 | async-start | bytes 21233664 | tf_op jit(solution)/shard_map/all_to_all | solution.py:492
  822.2 4.1 copy-start.6
  846.9 3.6 copy-start.4
  940.1 206.8 %all-to-all-start.5 = ((bf16[4,36,29184]{2,1,0:T(8,128)(2,1)}), bf16[4,36,29184]{2,1,0:T(8,128)(2,1)}, u32[]{:S(2)}, u32[]{:S(2)}) async-start(bf16[4,36,29184]{2,1,0:T(8,128)(2,1)} %copy-done.4), calls=%async_computation.5 | async-start | bytes 18677760 | tf_op jit(solution)/shard_map/all_to_all | solution.py:492
  947.3 12.7 copy-start.16
  1146.9 261.4 %all-to-all-start.4 = ((bf16[8,864,768]{2,1,0:T(8,128)(2,1)}), bf16[8,864,768]{2,1,0:T(8,128)(2,1)}, u32[]{:S(2)}, u32[]{:S(2)}) async-start(bf16[8,864,768]{2,1,0:T(8,128)(2,1)} %synthesis.1), calls=%async_computation.4 | async-start | bytes 21233664 | tf_op jit(solution)/shard_map/all_to_all | solution.py:492
  1152.1 117.3 %all-reduce.5.cloned.1.call-start = ((), (), s32[]{:S(2)}) async-start(), calls=%async_computation.14 | async-start | bytes 2359296 | tf_op jit(solution)/shard_map/psum | solution.py:544
  1159.4 212.0 %all-gather.5.cloned.1.call-start = ((), (), s32[]{:S(2)}) async-start(), calls=%async_computation.15 | async-start | bytes 5898240 | tf_op jit(solution)/shard_map/all_gather | solution.py:564
  1861.5 123.1 %all-to-all-start.9 = ((bf16[8,864,768]{2,1,0:T(8,128)(2,1)}), bf16[8,864,768]{2,1,0:T(8,128)(2,1)}, u32[]{:S(2)}, u32[]{:S(2)}) async-start(bf16[8,864,768]{2,1,0:T(8,128)(2,1)} %bitcast.64), calls=%async_computation.9 | async-start | bytes 21233664 | tf_op jit(solution)/shard_map/all_to_all | solution.py:492
  1866.7 135.1 %reduce-scatter.3.cloned.1.call-start = ((), (), s32[]{:S(2)}) async-start(), calls=%async_computation.16 | async-start | bytes 5898240 | tf_op jit(solution)/shard_map/reduce_scatter | solution.py:588
  1996.5 148.4 %all-to-all-start.10 = ((bf16[8,864,768]{2,1,0:T(8,128)(2,1)}), bf16[8,864,768]{2,1,0:T(8,128)(2,1)}, u32[]{:S(2)}, u32[]{:S(2)}) async-start(bf16[8,864,768]{2,1,0:T(8,128)(2,1)} %analysis_back.1), calls=%async_computation.10 | async-start | bytes 21233664 | tf_op jit(solution)/shard_map/all_to_all | solution.py:492
  2001.7 449.9 %all-reduce.7.cloned.1.call-start = ((), (), s32[]{:S(2)}) async-start(), calls=%async_computation.17 | async-start | bytes 4718592 | tf_op jit(solution)/shard_map/psum | solution.py:589
  2004.7 669.2 %reduce-scatter.5.cloned.1.call-start = ((), (), s32[]{:S(2)}) async-start(), calls=%async_computation.18 | async-start | bytes 17694720 | tf_op jit(solution)/shard_map/reduce_scatter | solution.py:586
  2030.3 120.7 %copy-start.8 = (bf16[180,180]{1,0:T(8,128)(2,1)S(1)}, bf16[180,180]{1,0:T(8,128)(2,1)}, u32[]{:S(2)}) copy-start(bf16[180,180]{1,0:T(8,128)(2,1)} %constant.123.clone.eye_ref) | copy-start | bytes 194404
  2030.3 120.7 %copy-start.10 = (bf16[180,192]{1,0:T(8,128)(2,1)S(1)}, bf16[180,192]{1,0:T(8,128)(2,1)}, u32[]{:S(2)}) copy-start(bf16[180,192]{1,0:T(8,128)(2,1)} %constant.119.clone.ft_ref) | copy-start | bytes 207364
  2030.3 120.7 %copy-start.12 = (f32[1,768]{1,0:T(1,128)S(1)}, f32[1,768]{1,0:T(1,128)}, u32[]{:S(2)}) copy-start(f32[1,768]{1,0:T(1,128)} %copy-done.11) | copy-start | bytes 9220
  2030.3 120.7 %copy-start.14 = (f32[1,768]{1,0:T(1,128)S(1)}, f32[1,768]{1,0:T(1,128)}, u32[]{:S(2)}) copy-start(f32[1,768]{1,0:T(1,128)} %copy-done.13) | copy-start | bytes 9220
  2144.9 298.3 %all-to-all-start.6 = ((bf16[4,36,29184]{2,1,0:T(8,128)(2,1)}), bf16[4,36,29184]{2,1,0:T(8,128)(2,1)}, u32[]{:S(2)}, u32[]{:S(2)}) async-start(bf16[4,36,29184]{2,1,0:T(8,128)(2,1)} %pad.7), calls=%async_computation.6 | async-start | bytes 18677760 | tf_op jit(solution)/shard_map/all_to_all | solution.py:492
  2443.2 247.8 %all-to-all-start.11 = ((bf16[4,36,29184]{2,1,0:T(8,128)(2,1)}), bf16[4,36,29184]{2,1,0:T(8,128)(2,1)}, u32[]{:S(2)}, u32[]{:S(2)}) async-start(bf16[4,36,29184]{2,1,0:T(8,128)(2,1)} %pad.8), calls=%async_computation.11 | async-start | bytes 18677760 | tf_op jit(solution)/shard_map/all_to_all | solution.py:492
  2453.4 32.7 %copy-start.21 = (f32[1,768]{1,0:T(1,128)S(1)}, f32[1,768]{1,0:T(1,128)}, u32[]{:S(2)}) copy-start(f32[1,768]{1,0:T(1,128)} %get-tuple-element.36) | copy-start | bytes 9220
  2453.4 219.8 %copy-start.20 = (f32[2,192]{1,0:T(2,128)S(1)}, f32[2,192]{1,0:T(2,128)}, u32[]{:S(2)}) copy-start(f32[2,192]{1,0:T(2,128)} %param.26) | copy-start | bytes 4612
  2453.4 219.8 %copy-start.22 = (f32[2,192]{1,0:T(2,128)S(1)}, f32[2,192]{1,0:T(2,128)}, u32[]{:S(2)}) copy-start(f32[2,192]{1,0:T(2,128)} %param.27) | copy-start | bytes 4612
  2453.4 219.8 %copy-start.23 = (f32[2,192]{1,0:T(2,128)S(1)}, f32[2,192]{1,0:T(2,128)}, u32[]{:S(2)}) copy-start(f32[2,192]{1,0:T(2,128)} %param.28) | copy-start | bytes 4612
  2673.9 49.8 %copy-start.1 = (s32[2]{0:T(128)S(1)}, s32[2]{0:T(128)}, u32[]{:S(2)}) copy-start(s32[2]{0:T(128)} %param.20) | copy-start | bytes 28
Sparse Core Ops, SparseCore 0:
  52.6 422.7 all-gather.6
  1269.5 101.8 all-gather.4
  1874.1 84.1 reduce-scatter.2
  2007.7 331.1 reduce-scatter.4
Sparse Core Ops, SparseCore 1:
  1159.5 109.8 all-reduce.4
  2006.4 129.9 all-reduce.6

commit v2 on v1

v2 whole, which is shorter than its diff:
```python
import functools
import math

import jax
import jax.numpy as jnp
import ml_dtypes
import numpy as np
from jax import lax
from jax.experimental import pallas as pl
from jax.experimental.pallas import tpu as pltpu
from jax.sharding import PartitionSpec as P

CH = 641
CVALID = 161
CROWS = 168
NLAT = 90
ROLL = 5
EPS = 1e-05
ADAM_EPS = 1e-08
BIAS_FIX = 1.0 - 0.5**5
GELU_A = math.sqrt(2.0 / math.pi)
GELU_B = 0.044715
BF = jnp.bfloat16
F32 = jnp.float32
NT = (((1,), (1,)), ((), ()))
NN = (((1,), (0,)), ((), ()))
TN = (((0,), (0,)), ((), ()))


def mm(a, b, dims=NN):
    return lax.dot_general(a, b, dims, preferred_element_type=F32)


def tables(nlat, nlatp, nlon, mmax, mpad):
    theta = (np.arange(nlat) + 0.5) * (math.pi / nlat)
    cosine, sine = np.cos(theta), np.sin(theta)
    legendre = np.zeros((mmax, mmax, nlat))
    for m in range(mmax):
        value = math.sqrt(0.5) * np.ones(nlat)
        for k in range(1, m + 1):
            value = value * math.sqrt((2 * k + 1) / (2 * k)) * sine
        legendre[m, m] = value
        if m + 1 < mmax:
            legendre[m, m + 1] = math.sqrt(2 * m + 3) * cosine * value
        for l in range(m + 2, mmax):
            a = math.sqrt((4 * l * l - 1) / (l * l - m * m))
            b = math.sqrt(((l - 1) ** 2 - m * m) / (4 * (l - 1) ** 2 - 1))
            legendre[m, l] = a * (cosine * legendre[m, l - 1] - b * legendre[m, l - 2])
    analysis = np.zeros((mpad, mmax, nlatp))
    synthesis = np.zeros((mpad, mmax, nlatp))
    analysis[:mmax, :, :nlat] = legendre * sine * (math.pi / nlat)
    synthesis[:mmax, :, :nlat] = legendre
    angle = (np.arange(mmax)[:, None] * np.arange(nlon)[None, :] % nlon) * (2.0 * math.pi / nlon)
    fwd = np.zeros((mpad, 2, nlon))
    fwd[:mmax, 0] = np.cos(angle) * math.sqrt(2.0 / nlon)
    fwd[:mmax, 1] = -np.sin(angle) * math.sqrt(2.0 / nlon)
    fwd_low = fwd.astype(np.float32).astype(ml_dtypes.bfloat16)
    inv = fwd.copy()
    inv[0] *= 0.5
    inv_low = inv.astype(np.float32).astype(ml_dtypes.bfloat16)
    low = lambda v: v.astype(np.float32).astype(ml_dtypes.bfloat16)
    return (
        fwd_low.reshape(mpad * 2, nlon),
        inv_low.reshape(mpad * 2, nlon),
        low(analysis),
        low(synthesis),
    )


def params(mib):
    return pltpu.CompilerParams(vmem_limit_bytes=mib * 2**20)


def whole(shape):
    return pl.BlockSpec(shape, lambda *_: (0,) * len(shape), pipeline_mode=pl.Buffered(1))


SMEM = pl.BlockSpec(memory_space=pltpu.SMEM)


LANE = 128


def spread(scr, start, value):
    rows, cols = value.shape
    for t in range(cols // LANE):
        scr[t, start : start + rows, :] = value[:, t * LANE : (t + 1) * LANE].astype(F32)


def pick_rows(scr, start, count, stride):
    parts = [scr[t, pl.ds(start, count, stride=stride), :] for t in range(scr.shape[0])]
    return jnp.concatenate(parts, axis=1).astype(BF)


class Plan:
    def __init__(self, slots, latd, n_sp, n_tp, n_mi):
        left = slots % n_tp
        self.split = left > 0 and latd % n_tp == 0 and n_mi % n_tp == 0
        self.slots, self.latd, self.n_tp = slots, latd, n_tp
        self.main = slots // n_tp if self.split else -(-slots // n_tp)
        self.left = left if self.split else 0
        self.part = latd // n_tp if self.split else 0
        self.chunks = [Chunk(self.main, latd, n_sp, n_mi, "sp", False)]
        if self.split:
            self.chunks.append(
                Chunk(left, self.part, n_sp * n_tp, n_mi // n_tp, ("sp", "tp"), True)
            )


class Chunk:
    def __init__(self, each, jn, nd, nm, axes, left):
        self.each, self.jn, self.nd, self.nm, self.axes, self.left = each, jn, nd, nm, axes, left
        self.rows = each * jn
        self.mk = 2 * nm
        self.inner = each * self.mk
        self.jb = 2 if jn % 2 == 0 else 1
        self.step = self.rows if left else self.jb
        self.blocks = 1 if left else jn // self.jb
        self.grid = (1, 1) if left else (each, self.blocks)
        self.stride = self.rows if left else jn

    def raw(self, i):
        return (i % self.each) * self.jn + i // self.each if self.left else i

    def row_map(self, *rest):
        return lambda s, k: (s * self.blocks + k,) + rest

    def order_spec(self, cp):
        if self.left:
            return pl.BlockSpec((self.nd, self.rows * self.mk, cp), lambda s, k: (0, 0, 0))
        return pl.BlockSpec((self.nd, self.jb, 1, self.mk, cp), lambda s, k: (0, k, s, 0, 0))

    def order_shape(self, cp):
        if self.left:
            return jax.ShapeDtypeStruct((self.nd, self.rows * self.mk, cp), BF)
        return jax.ShapeDtypeStruct((self.nd, self.jn, self.each, self.mk, cp), BF)

    def order_scratch(self, cp):
        return pltpu.VMEM((self.nd, self.step * self.mk, cp), F32)

    def keep_orders(self, fs, i, value):
        for d in range(self.nd):
            fs[d, i * self.mk : (i + 1) * self.mk] = value[d * self.mk : (d + 1) * self.mk]

    def write_orders(self, ref, fs):
        for d in range(self.nd):
            if self.left:
                ref[d] = fs[d].astype(BF)
            else:
                for i in range(self.step):
                    ref[d, i, 0] = fs[d, i * self.mk : (i + 1) * self.mk].astype(BF)

    def grid_coef(self, value):
        return value.reshape(self.nd, self.grid[0], -1, value.shape[-1])

    def coef_spec(self, rows_s, cp):
        return pl.BlockSpec((self.nd, 1, rows_s, cp), lambda s, k: (0, s, 0, 0))


def pack_rows(state, me, plan, lanes, tile):
    slots, latd, _ = state.shape
    n_tp, main, left, part = plan.n_tp, plan.main, plan.left, plan.part

    def body(me_ref, x_ref, *outs):
        for d in range(n_tp):
            t = me_ref[0] ^ d
            parts = []
            for i in range(main):
                at = t * main + i
                v = x_ref[jnp.minimum(at, slots - 1)].astype(F32)
                parts.append(jnp.where(at < slots, v, 0.0) if n_tp * main > slots else v)
            outs[d][...] = jnp.concatenate(parts, axis=0).astype(BF)
        if left:
            whole_rows = [x_ref[n_tp * main + i].astype(F32) for i in range(left)]
            options = [
                jnp.concatenate([v[t * part : (t + 1) * part] for v in whole_rows], axis=0)
                for t in range(n_tp)
            ]
            for d in range(n_tp):
                t = me_ref[0] ^ d
                acc = options[0]
                for o in range(1, n_tp):
                    acc = jnp.where(t == o, options[o], acc)
                outs[n_tp + d][...] = acc.astype(BF)

    counts = [main * latd] * n_tp + [left * part] * (n_tp if left else 0)
    got = pl.pallas_call(
        body,
        grid=(lanes // tile,),
        in_specs=[SMEM, pl.BlockSpec((slots, latd, tile), lambda l: (0, 0, l))],
        out_specs=[pl.BlockSpec((c, tile), lambda l: (0, l)) for c in counts],
        out_shape=[jax.ShapeDtypeStruct((c, lanes), BF) for c in counts],
        compiler_params=params(32),
        name="pack_rows",
    )(me, state)
    return got[:n_tp], got[n_tp:]


def unpack_rows(pieces, me, plan, flat, valid, lanes, tile):
    slots, latd, n_tp, main, left, part = (
        plan.slots, plan.latd, plan.n_tp, plan.main, plan.left, plan.part,
    )
    last = lanes // tile - 1
    arrays = [a for _, group in pieces for a in group]

    def body(me_ref, *refs):
        o_ref = refs[-1]
        lane = pl.program_id(0) * tile + lax.broadcasted_iota(jnp.int32, (1, tile), 1)
        keep = lane < valid
        for p, (first, _) in enumerate(pieces):
            group = refs[p * n_tp : (p + 1) * n_tp]
            values = [jnp.where(keep, g[...].astype(F32), 0.0) for g in group]
            if first >= 0:
                for d in range(n_tp):
                    for i in range(values[d].shape[0] // latd):
                        at = (me_ref[0] ^ d) * main + first + i

                        @pl.when(at < slots)
                        def _(at=at, d=d, i=i):
                            o_ref[at] = values[d][i * latd : (i + 1) * latd].astype(BF)
            else:
                ordered = []
                for t in range(n_tp):
                    acc = values[0]
                    for d in range(1, n_tp):
                        acc = jnp.where((me_ref[0] ^ d) == t, values[d], acc)
                    ordered.append(acc)
                for i in range(left):
                    o_ref[n_tp * main + i] = jnp.concatenate(
                        [v[i * part : (i + 1) * part] for v in ordered], axis=0
                    ).astype(BF)

    return pl.pallas_call(
        body,
        grid=(pl.cdiv(flat, tile),),
        in_specs=[SMEM]
        + [pl.BlockSpec((a.shape[0], tile), lambda l: (0, jnp.minimum(l, last))) for a in arrays],
        out_specs=pl.BlockSpec((slots, latd, tile), lambda l: (0, 0, l)),
        out_shape=jax.ShapeDtypeStruct((slots, latd, flat), BF),
        compiler_params=params(48),
        name="unpack_rows",
    )(me, *arrays)


def load_transposed(refs, row, me, eye, scr, csh):
    for d, ref in enumerate(refs):
        start = pl.multiple_of((me ^ d) * csh, 64)
        scr[pl.ds(start, ref.shape[1]), :] = ref[row].astype(F32)
    return mm(eye, scr[...].astype(BF), NT)


def store_transposed(refs, row, value, me, eye, scr, csh):
    scr[...] = mm(value, eye, TN)
    for d, ref in enumerate(refs):
        start = pl.multiple_of((me ^ d) * csh, 64)
        ref[row] = scr[pl.ds(start, ref.shape[1]), :].astype(BF)


def fourier(ck, grids, me, fwd, eye, gain, cmask, row_mask, csh):
    _, cv, nlon = grids[0].shape
    n = len(grids)
    cp = cmask.shape[1]
    step = ck.step

    def body(me_ref, fb_ref, eye_ref, g_ref, cm_ref, rm_ref, *refs):
        x_refs, (f_ref, xt_ref, scr, fs) = refs[:n], refs[n:]
        at = pl.program_id(0) * ck.blocks + pl.program_id(1)

        @pl.when(at == 0)
        def _():
            scr[...] = jnp.zeros_like(scr)

        for i in range(step):
            xt = load_transposed(x_refs, ck.raw(i), me_ref[0], eye_ref[...], scr, csh)
            xt = xt * (cm_ref[...] * rm_ref[at * step + i])
            r1 = lax.rsqrt(jnp.sum(xt * xt, axis=1, keepdims=True) / CH + EPS)
            u = (xt * r1 * g_ref[...]).astype(BF)
            ck.keep_orders(fs, i, mm(fb_ref[...], u))
            xt_ref[i] = xt.astype(BF)
        ck.write_orders(f_ref, fs)

    return pl.pallas_call(
        body,
        grid=ck.grid,
        in_specs=[SMEM]
        + [whole(fwd.shape), whole(eye.shape), whole(gain.shape), whole(cmask.shape), SMEM]
        + [pl.BlockSpec((step, cv, nlon), ck.row_map(0, 0))] * n,
        out_specs=[
            ck.order_spec(cp),
            pl.BlockSpec((step, nlon, cp), ck.row_map(0, 0)),
        ],
        out_shape=[
            ck.order_shape(cp),
            jax.ShapeDtypeStruct((ck.rows, nlon, cp), BF),
        ],
        scratch_shapes=[pltpu.VMEM((cp, nlon), F32), ck.order_scratch(cp)],
        compiler_params=params(48),
        name="fourier",
    )(me, fwd, eye, gain, cmask, row_mask, *grids)


def legendre(ck, data, table, n_dest, by_order, name):
    n_src, rows, cp = data.shape
    n_mi, n_out, n_in = table.shape
    inner = ck.inner
    out_each = n_out // n_dest
    tile = 256

    def body(x_ref, t_ref, o_ref, fin, fout):
        for d in range(n_src):
            spread(fin, d * rows, x_ref[d])
        for i in range(inner):
            got = pick_rows(fin, i, n_in, inner)
            res = mm(t_ref[(i // 2) % n_mi], got)
            at = i % ck.mk * ck.each + i // ck.mk if by_order and ck.left else i
            for d in range(n_dest):
                fout[d, at * out_each : (at + 1) * out_each] = res[d * out_each : (d + 1) * out_each]
        for d in range(n_dest):
            o_ref[d] = fout[d].astype(BF)

    return pl.pallas_call(
        body,
        grid=(cp // tile,),
        in_specs=[pl.BlockSpec((n_src, rows, tile), lambda c: (0, 0, c)), whole(table.shape)],
        out_specs=pl.BlockSpec((n_dest, inner * out_each, tile), lambda c: (0, 0, c)),
        out_shape=jax.ShapeDtypeStruct((n_dest, inner * out_each, cp), BF),
        scratch_shapes=[
            pltpu.VMEM((tile // LANE, n_src * rows, LANE), F32),
            pltpu.VMEM((n_dest, inner * out_each, tile), F32),
        ],
        compiler_params=params(56),
        name=name,
    )(data, table)


def mix(ck, coef, weights, csh, dims, name):
    n_sp, rows, cp = coef.shape
    n_tp, own, wrows, _ = weights.shape
    inner = ck.inner
    count = n_sp * inner
    qb = next((b for b in range(1, own + 1) if own % b == 0 and b * inner % 16 == 0), own)

    def body(x_ref, w_ref, o_ref, a_ref, fin, fout, wfull):
        k = pl.program_id(0)

        @pl.when(k == 0)
        def _():
            wfull[...] = jnp.zeros_like(wfull)
            for d in range(n_sp):
                spread(fin, d * rows, x_ref[d])

        for i in range(qb):
            a = pick_rows(fin, k * qb + i, count, own)
            a_ref[i] = a
            for t in range(n_tp):
                wfull[t * csh : t * csh + wrows] = w_ref[t, i]
            b = mm(a, wfull[...], dims)
            for d in range(n_sp):
                fout[d, i * inner : (i + 1) * inner] = b[d * inner : (d + 1) * inner]
        for d in range(n_sp):
            o_ref[d] = fout[d].astype(BF)

    return pl.pallas_call(
        body,
        grid=(own // qb,),
        in_specs=[
            whole(coef.shape),
            pl.BlockSpec((n_tp, qb, wrows, cp), lambda k: (0, k, 0, 0)),
        ],
        out_specs=[
            pl.BlockSpec((n_sp, qb * inner, cp), lambda k: (0, k, 0)),
            pl.BlockSpec((qb, count, cp), lambda k: (k, 0, 0)),
        ],
        out_shape=[
            jax.ShapeDtypeStruct((n_sp, own * inner, cp), BF),
            jax.ShapeDtypeStruct((own, count, cp), BF),
        ],
        scratch_shapes=[
            pltpu.VMEM((cp // LANE, n_sp * rows, LANE), F32),
            pltpu.VMEM((n_sp, qb * inner, cp), F32),
            pltpu.VMEM((n_tp * csh, cp), BF),
        ],
        compiler_params=params(56),
        name=name,
    )(coef, weights)


def weight_grads(grads, coefs, n_tp, wrows):
    n = len(grads)
    own, _, cp = grads[0].shape
    csh = cp // n_tp

    def body(*refs):
        o_ref = refs[-1]
        g = jnp.concatenate([r[0] for r in refs[:n]], axis=0)
        a = jnp.concatenate([r[0] for r in refs[n : 2 * n]], axis=0)
        dw = mm(g, a, TN)
        for t in range(n_tp):
            o_ref[t, 0] = dw[t * csh : t * csh + wrows].astype(BF)

    return pl.pallas_call(
        body,
        grid=(own,),
        in_specs=[pl.BlockSpec((1,) + v.shape[1:], lambda q: (q, 0, 0)) for v in grads + coefs],
        out_specs=pl.BlockSpec((n_tp, 1, wrows, cp), lambda q: (0, q, 0, 0)),
        out_shape=jax.ShapeDtypeStruct((n_tp, own, wrows, cp), BF),
        compiler_params=params(48),
        name="weight_grads",
    )(*grads, *coefs)


def grid_block(ck, coef, xt, cots, me, w_in, w_out, inv, inv_t, eye, gain, cmask, row_mask, csh):
    nd, _, rows_s, cp = coef.shape
    _, cv, nlon = cots[0].shape
    n = len(cots)
    hid = w_in.shape[0]
    rows, step, mk = ck.rows, ck.step, ck.mk
    jb = 2 if step % 2 == 0 else 1

    def body(me_ref, c_ref, xt_ref, wi_ref, wo_ref, ib_ref, it_ref, eye_ref, g_ref, cm_ref, rm_ref, *refs):
        ct_refs, out_refs = refs[:n], refs[n : 2 * n]
        dg_ref, dh_ref, dwi_ref, dwo_ref, gg_ref, fin, scr, oscr, hs, dms, fs = refs[2 * n :]
        k = pl.program_id(1)
        at = pl.program_id(0) * ck.blocks + k

        @pl.when(at == 0)
        def _():
            scr[...] = jnp.zeros_like(scr)
            dwi_ref[...] = jnp.zeros_like(dwi_ref)
            dwo_ref[...] = jnp.zeros_like(dwo_ref)
            gg_ref[...] = jnp.zeros_like(gg_ref)

        @pl.when(k == 0)
        def _():
            for d in range(nd):
                spread(fin, d * rows_s, c_ref[d, 0])

        for base in range(0, step, jb):
            for i in range(jb):
                r = base + i
                g = pick_rows(fin, k * ck.jb + ck.raw(r), nd * mk, ck.stride)
                hs[i] = xt_ref[r].astype(F32) + mm(it_ref[...], g)
                dm = load_transposed(ct_refs, ck.raw(r), me_ref[0], eye_ref[...], scr, csh)
                dms[i] = dm * (cm_ref[...] * rm_ref[at * step + r])
            h = jnp.concatenate([hs[i] for i in range(jb)], axis=0)
            dm = jnp.concatenate([dms[i] for i in range(jb)], axis=0)
            dmb = dm.astype(BF)
            r2 = lax.rsqrt(jnp.sum(h * h, axis=1, keepdims=True) / CH + EPS)
            g1 = g_ref[...]
            v = (h * r2 * g1).astype(BF)
            z = mm(v, wi_ref[...], NT)
            t = jnp.tanh(GELU_A * (z + GELU_B * z * z * z))
            act = (0.5 * z * (1.0 + t)).astype(BF)
            slope = 0.5 * (1.0 + t) + 0.5 * z * (1.0 - t * t) * (
                GELU_A * (1.0 + 3.0 * GELU_B * z * z)
            )
            out = (h + mm(act, wo_ref[...])).astype(BF)
            dz = (slope * mm(dmb, wo_ref[...], NT)).astype(BF)
            dwo_ref[...] += mm(act, dmb, TN)
            dwi_ref[...] += mm(dz, v, TN)
            dv = mm(dz, wi_ref[...])
            gd = g1 * dv
            proj = jnp.sum(h * gd, axis=1, keepdims=True) / CH
            dh = dm + r2 * gd - h * (r2 * r2 * r2 * proj)
            gg_ref[...] += jnp.sum(dv * h * r2, axis=0, keepdims=True)
            for i in range(jb):
                r = base + i
                part = dh[i * nlon : (i + 1) * nlon].astype(BF)
                dh_ref[r] = part
                ck.keep_orders(fs, r, mm(ib_ref[...], part))
                store_transposed(
                    out_refs, ck.raw(r), out[i * nlon : (i + 1) * nlon], me_ref[0], eye_ref[...], oscr, csh
                )
        ck.write_orders(dg_ref, fs)

    rowmap = ck.row_map(0, 0)
    fixed = lambda s, k: (0, 0)
    grid_spec = pl.BlockSpec((step, cv, nlon), rowmap)
    got = pl.pallas_call(
        body,
        grid=ck.grid,
        in_specs=[
            SMEM,
            ck.coef_spec(rows_s, cp),
            pl.BlockSpec((step, nlon, cp), rowmap),
            whole(w_in.shape),
            whole(w_out.shape),
            whole(inv.shape),
            whole(inv_t.shape),
            whole(eye.shape),
            whole(gain.shape),
            whole(cmask.shape),
            SMEM,
        ]
        + [grid_spec] * n,
        out_specs=[grid_spec] * n
        + [
            ck.order_spec(cp),
            pl.BlockSpec((step, nlon, cp), rowmap),
            pl.BlockSpec((hid, cp), fixed),
            pl.BlockSpec((hid, cp), fixed),
            pl.BlockSpec((1, cp), fixed),
        ],
        out_shape=[jax.ShapeDtypeStruct((rows, cv, nlon), BF)] * n
        + [
            ck.order_shape(cp),
            jax.ShapeDtypeStruct((rows, nlon, cp), BF),
            jax.ShapeDtypeStruct((hid, cp), F32),
            jax.ShapeDtypeStruct((hid, cp), F32),
            jax.ShapeDtypeStruct((1, cp), F32),
        ],
        scratch_shapes=[
            pltpu.VMEM((cp // LANE, nd * rows_s, LANE), F32),
            pltpu.VMEM((cp, nlon), F32),
            pltpu.VMEM((cp, nlon), F32),
            pltpu.VMEM((jb, nlon, cp), F32),
            pltpu.VMEM((jb, nlon, cp), F32),
            ck.order_scratch(cp),
        ],
        compiler_params=params(62),
        name="grid_block",
    )(me, coef, xt, w_in, w_out, inv, inv_t, eye, gain, cmask, row_mask, *cots)
    return got[:n], got[n:]


def grid_final(ck, coef, xt, dh, me, fwd_t, eye, gain, cmask, row_mask, csh, n, cv):
    nd, _, rows_s, cp = coef.shape
    rows, nlon, _ = xt.shape
    step, mk = ck.step, ck.mk

    def body(me_ref, c_ref, xt_ref, dh_ref, ft_ref, eye_ref, g_ref, cm_ref, rm_ref, *refs):
        out_refs, (gg_ref, fin, oscr) = refs[:n], refs[n:]
        k = pl.program_id(1)
        at = pl.program_id(0) * ck.blocks + k

        @pl.when(at == 0)
        def _():
            gg_ref[...] = jnp.zeros_like(gg_ref)

        @pl.when(k == 0)
        def _():
            for d in range(nd):
                spread(fin, d * rows_s, c_ref[d, 0])

        for i in range(step):
            du = mm(ft_ref[...], pick_rows(fin, k * ck.jb + ck.raw(i), nd * mk, ck.stride))
            x = xt_ref[i].astype(F32)
            r1 = lax.rsqrt(jnp.sum(x * x, axis=1, keepdims=True) / CH + EPS)
            gd = g_ref[...] * du
            proj = jnp.sum(x * gd, axis=1, keepdims=True) / CH
            res = dh_ref[i].astype(F32) + r1 * gd - x * (r1 * r1 * r1 * proj)
            res = (res * (cm_ref[...] * rm_ref[at * step + i])).astype(BF)
            gg_ref[...] += jnp.sum(du * x * r1, axis=0, keepdims=True)
            store_transposed(out_refs, ck.raw(i), res, me_ref[0], eye_ref[...], oscr, csh)

    rowmap = ck.row_map(0, 0)
    got = pl.pallas_call(
        body,
        grid=ck.grid,
        in_specs=[
            SMEM,
            ck.coef_spec(rows_s, cp),
            pl.BlockSpec((step, nlon, cp), rowmap),
            pl.BlockSpec((step, nlon, cp), rowmap),
            whole(fwd_t.shape),
            whole(eye.shape),
            whole(gain.shape),
            whole(cmask.shape),
            SMEM,
        ],
        out_specs=[pl.BlockSpec((step, cv, nlon), rowmap)] * n
        + [pl.BlockSpec((1, cp), lambda s, k: (0, 0))],
        out_shape=[jax.ShapeDtypeStruct((rows, cv, nlon), BF)] * n
        + [jax.ShapeDtypeStruct((1, cp), F32)],
        scratch_shapes=[
            pltpu.VMEM((cp // LANE, nd * rows_s, LANE), F32),
            pltpu.VMEM((cp, nlon), F32),
        ],
        compiler_params=params(48),
        name="grid_final",
    )(me, coef, xt, dh, fwd_t, eye, gain, cmask, row_mask)
    return got[:n], got[n]


def adamw(param, grad, first, second, rate, decay):
    new_first = 0.5 * first + 0.5 * grad
    new_second = 0.5 * second + 0.5 * grad * grad
    update = new_first / BIAS_FIX / (jnp.sqrt(new_second / BIAS_FIX) + ADAM_EPS)
    return (param - rate * (update + decay * param), new_first, new_second)


def swap(value, axis):
    return lax.all_to_all(value, axis, split_axis=0, concat_axis=0, tiled=True)


def after(value, *others):
    return lax.optimization_barrier((value, others))[0]


def local(
    n_sp, n_tp,
    state, cotangent, rollout_lengths, channel_sizes, owner_slots,
    master, first_moment, second_moment, gains, gain_first, gain_second,
):
    slots, latd, flat = state.shape
    own, csh, cp = master.shape
    nlon = flat // csh
    sp, tp = lax.axis_index("sp"), lax.axis_index("tp")
    me = tp.astype(jnp.int32).reshape(1)
    degrees = owner_slots.shape[0] - 4
    n_mi = (degrees + n_sp - 1) // n_sp
    mpad = n_mi * n_sp
    plan = Plan(slots, latd, n_sp, n_tp, n_mi)
    chunks = plan.chunks
    nlatp = latd * n_sp
    valid = CVALID * nlon
    tile = 19 * 128
    lanes = pl.cdiv(valid, tile) * tile

    fwd, inv, analysis, synthesis = tables(NLAT, nlatp, nlon, degrees, mpad)
    fwd_t, inv_t = jnp.asarray(fwd.T), jnp.asarray(inv.T)
    fwd, inv = jnp.asarray(fwd), jnp.asarray(inv)
    eye = jnp.asarray(np.eye(nlon).astype(ml_dtypes.bfloat16))
    pick = (owner_slots[:degrees, None] == jnp.arange(n_sp * own)[None, :]).astype(BF)
    mine = lambda t: lax.dynamic_slice_in_dim(jnp.asarray(t), sp * n_mi, n_mi, 0)
    by_slot = lambda t: jnp.einsum("mlj,lq->mqj", mine(t), pick, preferred_element_type=F32).astype(BF)
    ana_q, syn_q = by_slot(analysis), by_slot(synthesis)
    ana_j, syn_j = jnp.swapaxes(ana_q, 1, 2), jnp.swapaxes(syn_q, 1, 2)

    def table(ck, t):
        return t if ck.nm == n_mi else lax.dynamic_slice_in_dim(t, tp * ck.nm, ck.nm, 0)

    chan = jnp.arange(cp)
    cmask = (chan % csh < channel_sizes[chan // csh]).astype(F32)
    rmask = (jnp.arange(csh) < channel_sizes[tp]).astype(F32)
    cmask2 = cmask[None, :]
    samples = rollout_lengths.shape[0]
    row_masks, cot_masks = [], []
    for ck in chunks:
        first, lat0 = (n_tp * plan.main, tp * ck.jn) if ck.left else (tp * plan.main, 0)
        ids = first + jnp.arange(ck.each)
        live = ids % ROLL < rollout_lengths[jnp.minimum(ids // ROLL, samples - 1)]
        live = (live & (ids < slots)).astype(F32)
        lat = (sp * latd + lat0 + jnp.arange(ck.jn) < NLAT).astype(F32)
        masks = jnp.ones((ck.each, 1), F32) * lat[None, :], live[:, None] * lat[None, :]
        masks = [(m.T if ck.left else m).reshape(-1) for m in masks]
        row_masks.append(masks[0])
        cot_masks.append(masks[1])

    copies = (master * (rmask[:, None] * cmask2)[None]).astype(BF)
    hrow = (jnp.arange(2 * csh) < 2 * channel_sizes[tp]).astype(F32).reshape(2, csh)
    raw = []
    for i in range(4):
        at = owner_slots[degrees + i] - sp * own
        inside = (at >= 0) & (at < own)
        piece = lax.dynamic_index_in_dim(master, jnp.clip(at, 0, own - 1), 0, keepdims=False)
        keep = hrow[i % 2][:, None] * cmask2 * inside.astype(F32)
        raw.append((piece * keep).astype(BF))
    gains_all = swap(jnp.broadcast_to(gains[None], (n_tp,) + gains.shape), "tp")
    gains_all = jnp.swapaxes(gains_all, 0, 1).reshape(2, cp)

    cut = lambda a: a[:, :valid].reshape(-1, CVALID, nlon)
    flat_of = lambda a: jnp.pad(a.reshape(a.shape[0], valid), ((0, 0), (0, lanes - valid)))
    send = lambda a, d: lax.ppermute(a, "tp", [(i, i ^ d) for i in range(n_tp)]) if d else a
    send_all = lambda arrays: [send(a, d) for d, a in enumerate(arrays)]
    rows3 = lambda v: v.reshape(v.shape[0], -1, cp)

    main, left = pack_rows(state, me, plan, lanes, tile)
    dense = lax.psum_scatter(jnp.stack(raw), "sp", scatter_dimension=1, tiled=True)
    main, left = send_all(main), send_all(left)
    dense = lax.all_gather(after(dense, main[1]), ("tp", "sp"), axis=1, tiled=True)
    w_in = dense[:2].reshape(2 * cp, cp)
    w_out = dense[2:].reshape(2 * cp, cp)
    main, left = [cut(a) for a in main], [cut(a) for a in left]
    x5 = [main, left]
    spec_w = lax.all_gather(after(copies[:, :CROWS], main, left), "tp", axis=0, tiled=False)
    gain_a, gain_b = gains_all[:1], gains_all[1:]
    n = len(chunks)
    odd = lambda arrays: [send(a, d) if d % 2 else a for d, a in enumerate(arrays)]
    even = lambda arrays: [a if d % 2 else send(a, d) for d, a in enumerate(arrays)]

    coefs, xts = [], []
    for i, ck in enumerate(chunks):
        f, xt = fourier(ck, x5[i], me, fwd, eye, gain_a, cmask2, row_masks[i], csh)
        xts.append(xt)
        f = swap(rows3(f), ck.axes)
        c = legendre(ck, f, table(ck, ana_q), n_sp, False, "analysis")
        coefs.append(swap(c, "sp"))
    m, a = mix(chunks[0], after(coefs[0], dense), spec_w, csh, NT, "mix_forward")
    mixed, coef_q = [swap(m, "sp")], [a]
    main, left = pack_rows(after(cotangent, m), me, plan, lanes, tile)
    ahead = odd(main)
    if n > 1:
        m, a = mix(chunks[1], after(coefs[1], main), spec_w, csh, NT, "mix_forward")
        mixed.append(swap(after(m, ahead), "sp"))
        coef_q.append(a)
    main, left = after((ahead, left), mixed[0])
    main, left = even(main), send_all(left)
    synth = [
        legendre(ck, m, table(ck, syn_j), ck.nd, True, "synthesis") for ck, m in zip(chunks, mixed)
    ]
    if n > 1:
        synth[1] = after(synth[1], main, left)
    synth = [ck.grid_coef(swap(g, ck.axes)) for ck, g in zip(chunks, synth)]
    cot5 = [[cut(a) for a in main], [cut(a) for a in left]]
    outs, rest, dgs = [], [], []
    for i, ck in enumerate(chunks):
        o, r = grid_block(
            ck, synth[i], xts[i], cot5[i], me, w_in, w_out, inv, inv_t, eye, gain_b, cmask2,
            cot_masks[i], csh,
        )
        outs.append([flat_of(a) for a in o])
        rest.append(r)
        dgs.append(rows3(r[0]))
    main, left = odd(outs[0]), outs[1] if n > 1 else []
    if n > 1:
        dgs[1] = after(dgs[1], main)
    dgs = [swap(g, ck.axes) for ck, g in zip(chunks, dgs)]
    main, left = after((main, left), dgs[0])
    main, left = even(main), send_all(left)
    dbs = [
        legendre(ck, g, table(ck, syn_q), n_sp, False, "synthesis_back")
        for ck, g in zip(chunks, dgs)
    ]
    if n > 1:
        dbs[1] = after(dbs[1], main, left)
    dbs = [swap(b, "sp") for b in dbs]
    das = [mix(ck, b, spec_w, csh, NN, "mix_backward") for ck, b in zip(chunks, dbs)]
    grad_q = [a[1] for a in das]
    das = [swap(a[0], "sp") for a in das]
    pieces_out = [(0, main)] + ([(-1, left)] if left else [])
    result = unpack_rows(pieces_out, me, plan, flat, valid, lanes, tile)
    dws = weight_grads(grad_q, coef_q, n_tp, CROWS)
    dfs = [
        legendre(ck, a, table(ck, ana_j), ck.nd, True, "analysis_back") for ck, a in zip(chunks, das)
    ]
    dfs[0] = swap(dfs[0], chunks[0].axes)
    if n > 1:
        dfs[1] = swap(after(dfs[1], dfs[0]), chunks[1].axes)
    pieces, gg_a = [], 0.0
    for i, ck in enumerate(chunks):
        o, gg = grid_final(
            ck, ck.grid_coef(dfs[i]), xts[i], rest[i][1], me, fwd_t, eye, gain_a, cmask2,
            row_masks[i], csh, n_tp, CVALID,
        )
        gg_a = gg_a + gg
        pieces.append((-1 if ck.left else 0, send_all([flat_of(a) for a in o])))

    dwi = sum(r[2] for r in rest)
    dwo = sum(r[3] for r in rest)
    gg_b = sum(r[4] for r in rest)
    dense_g = jnp.stack([dwi, dwo]).reshape(4, n_tp, csh, cp).astype(BF)
    dense_g = lax.psum_scatter(after(dense_g, pieces_out), "tp", scatter_dimension=1, tiled=False)
    spec_g = lax.psum_scatter(after(dws, pieces_out), "tp", scatter_dimension=0, tiled=False)
    dense_g = lax.psum(dense_g.astype(F32), "sp")
    spec_g = jnp.pad(spec_g.astype(F32), ((0, 0), (0, csh - CROWS), (0, 0)))
    grads = spec_g
    for i in range(4):
        hit = (owner_slots[degrees + i] == sp * own + jnp.arange(own))[:, None, None]
        grads = jnp.where(hit, dense_g[i][None], grads)
    new_master, new_first, new_second = adamw(master, grads, first_moment, second_moment, 0.03, 0.01)
    gain_g = lax.psum(after(jnp.concatenate([gg_a, gg_b], axis=0), new_master), ("sp", "tp"))
    gain_g = lax.dynamic_slice_in_dim(gain_g, tp * csh, csh, 1)
    new_gains, gain_one, gain_two = adamw(gains, gain_g, gain_first, gain_second, 0.5, 0.0)
    grad_state = unpack_rows(
        pieces, after(me, new_gains, new_master), plan, flat, valid, lanes, tile
    )
    return (
        result, grad_state, new_master, new_master.astype(BF), new_first, new_second,
        new_gains, gain_one, gain_two,
    )


def solution(mesh):
    wide, slot, gain = P(None, "sp", "tp"), P("sp", "tp", None), P(None, "tp")
    return jax.shard_map(
        functools.partial(local, mesh.shape["sp"], mesh.shape["tp"]),
        mesh=mesh,
        in_specs=(wide, wide, P(), P(), P(), slot, slot, slot, gain, gain, gain),
        out_specs=(wide, wide, slot, slot, slot, slot, gain, gain, gain),
        check_vma=False,
    )
```

time: 2740 us -> 1830 us (0.67)
  blocking collectives: 845 us -> 136 us
  waiting for transfers between devices: 1170 us -> 882 us
  starting transfers between devices: 56.1 us -> 169 us
  Pallas kernels: 447 us -> 361 us
  local copies, waits for them, and re-layouts: 147 us -> 193 us
    all_to_all x10 -> x16, waiting for transfers between devices: 960 us -> 403 us  [swap(): return lax.all_to_all(value, axis, split_axis=0, concat_axis=0, tiled=True)]
    all_gather x1 -> x0, blocking collectives: 409 us -> none  [local(): gains_all = lax.all_gather(gains, 'tp', axis=1, tiled=True)]
    ppermute x0 -> x24, waiting for transfers between devices: none -> 399 us  [local(): lax.ppermute(a, 'tp', [(i, i ^ d) for i in range(n_tp)])]
    all_to_all x2 -> x1, blocking collectives: 248 us -> 85.6 us  [swap(): return lax.all_to_all(value, axis, split_axis=0, concat_axis=0, tiled=True)]
    psum x1, blocking collectives: 187 us -> 50.3 us  [local(): lax.psum(after(jnp.concatenate([gg_a, gg_b], axis=0), new_master), ('sp',...]
    psum x1 -> x0, waiting for transfers between devices: 110 us -> none  [local(): dense = lax.psum(jnp.stack(raw), 'sp')]
    all_gather x2, waiting for transfers between devices: 101 us -> 0.04 us  [the longest x1 0.02 us: local(): lax.all_gather(after(dense, main[1]), ('tp', 'sp'), axis=1, tiled=True)]
    pallas_call x13 -> x23, Pallas kernels: 447 us -> 361 us  [the longest x2 144 us: grid_block(): pl.pallas_call(body, grid=ck.grid, in_specs=[SMEM, ck.coef_spec(rows_s, c...]
  transfers between devices with their start and end apart: 16 -> 46, of which waited for: 9 -> 23; matrix products, arithmetic and copies ran while one was open for 6% -> 11% of each run, Pallas kernels for 6% -> 19%
where the time goes in v2:
time: 1830 us; the launch traced here: 1810 us
  waiting for transfers between devices  882 us (48%)
  Pallas kernels  361 us (20%)
  local copies, waits for them, and re-layouts  193 us (11%)
  starting transfers between devices  169 us (9%)
  blocking collectives  136 us (7%)
  other arithmetic  52.8 us (3%)
  between operations  18.5 us (1%)
    all_to_all x16, waiting for transfers between devices, swap(): return lax.all_to_all(value, axis, split_axis=0, concat_axis=0, tiled=True)  403 us
    ppermute x24, waiting for transfers between devices, local(): lax.ppermute(a, 'tp', [(i, i ^ d) for i in range(n_tp)])  399 us
    pallas_call x2, Pallas kernels, grid_block(): pl.pallas_call(body, grid=ck.grid, in_specs=[SMEM, ck.coef_spec(rows_s, c...  144 us
    all_to_all x16, starting transfers between devices, swap(): return lax.all_to_all(value, axis, split_axis=0, concat_axis=0, tiled=True)  94.7 us
    all_to_all x1, blocking collectives, swap(): return lax.all_to_all(value, axis, split_axis=0, concat_axis=0, tiled=True)  85.6 us
    ppermute x24, starting transfers between devices, local(): lax.ppermute(a, 'tp', [(i, i ^ d) for i in range(n_tp)])  73.8 us
    pallas_call x8, Pallas kernels, legendre(): pl.pallas_call(body, grid=(cp // tile,), in_specs=[pl.BlockSpec((n_src, r...  59.4 us
    pallas_call x4, Pallas kernels, mix(): pl.pallas_call(body, grid=(own // qb,), in_specs=[whole(coef.shape), pl.B...  57.9 us
  transfers between devices with their start and end apart: 46, of which 23 were waited for; matrix products, arithmetic and copies ran while one was open for 11% of the time, Pallas kernels for 19%

profile of v2, /device:TPU:0, one launch (start us, length us, event | category | flops | bytes accessed | tf_op | source)
XLA Modules:
  0.0 1814.9 jit_solution(1628410652059904910)
XLA Ops:
  24.4 5.8 pack_rows.2
  36.7 23.5 %reduce-scatter.10.cloned.1.call-done = bf16[24,3072]{1,0:T(8,128)(2,1)} async-done(((bf16[192,3072]{1,0:T(8,128)(2,1)}), bf16[24,3072]{1,0:T(8,128)(2,1)}) %reduce-scatter.10.cloned.1.call-update) | async-done | bytes 147472
  61.8 5.8 collective-permute-done
  81.8 5.3 reshape.585.refs_0_
  92.0 53.1 %collective-permute-done.3 = bf16[6,29184]{1,0:T(8,128)(2,1)} collective-permute-done((bf16[6,29184]{1,0:T(8,128)(2,1)}, bf16[6,29184]{1,0:T(8,128)(2,1)}, u32[]{:S(2)}, u32[]{:S(2)}) %collective-permute-start.3) | collective-permute-done | bytes 350240 | tf_op jit(solution)/shard_map/ppermute | solution.py:664
  147.1 96.9 %collective-permute-done.4 = bf16[6,29184]{1,0:T(8,128)(2,1)} collective-permute-done((bf16[6,29184]{1,0:T(8,128)(2,1)}, bf16[6,29184]{1,0:T(8,128)(2,1)}, u32[]{:S(2)}, u32[]{:S(2)}) %collective-permute-start.4) | collective-permute-done | bytes 350240 | tf_op jit(solution)/shard_map/ppermute | solution.py:664
  252.2 5.3 reshape.586.refs_1_
  260.0 5.3 reshape.587.refs_2_
  272.2 10.9 all-to-all-start
  292.4 17.8 fourier.2
  321.6 73.5 %all-to-all-done.1.x_ref = bf16[8,576,768]{2,1,0:T(8,128)(2,1)} async-done(((bf16[8,576,768]{2,1,0:T(8,128)(2,1)}), bf16[8,576,768]{2,1,0:T(8,128)(2,1)}, u32[]{:S(2)}, u32[]{:S(2)}) %all-to-all-start.1) | async-done | bytes 7077920 | tf_op jit(solution)/shard_map/all_to_all | solution.py:593
  399.9 10.5 analysis.2
  410.4 77.1 %all-to-all-done.5.x_ref = bf16[32,36,768]{2,1,0:T(8,128)(2,1)S(1)} async-done(((bf16[32,36,768]{2,1,0:T(8,128)(2,1)}), bf16[32,36,768]{2,1,0:T(8,128)(2,1)S(1)}, u32[]{:S(2)}, u32[]{:S(2)}) %all-to-all-start.5) | async-done | bytes 1769504 | tf_op jit(solution)/shard_map/all_to_all | solution.py:593
  499.1 74.5 %all-to-all-done.2.x_ref = bf16[8,576,768]{2,1,0:T(8,128)(2,1)} async-done(((bf16[8,576,768]{2,1,0:T(8,128)(2,1)}), bf16[8,576,768]{2,1,0:T(8,128)(2,1)}, u32[]{:S(2)}, u32[]{:S(2)}) %all-to-all-start.2) | async-done | bytes 7077920 | tf_op jit(solution)/shard_map/all_to_all | solution.py:593
  577.2 19.1 %mix_forward.2 = (bf16[8,576,768]{2,1,0:T(8,128)(2,1)}, bf16[12,384,768]{2,1,0:T(8,128)(2,1)}) custom-call(bf16[8,576,768]{2,1,0:T(8,128)(2,1)} %all-to-all-done.2.x_ref, bf16[4,12,168,768]{3,2,1,0:T(8,128)(2,1)} %bitcast.64), custom_call_target="tpu_custom_call" | custom-call | tf_op jit(solution)/shard_map/mix_forward/pallas_call | solution.py:363
  621.5 10.0 mix_forward.3
  631.5 51.3 %collective-permute-done.6 = bf16[24,29184]{1,0:T(8,128)(2,1)S(1)} collective-permute-done((bf16[24,29184]{1,0:T(8,128)(2,1)S(1)}, bf16[24,29184]{1,0:T(8,128)(2,1)S(1)}, u32[]{:S(2)}, u32[]{:S(2)}) %collective-permute-start.6) | collective-permute-done | bytes 1400864 | tf_op jit(solution)/shard_map/ppermute | solution.py:664
  694.7 10.5 synthesis.2
  705.2 9.0 all-to-all-done.7.x_ref
  733.6 30.0 %collective-permute-done.11 = bf16[6,29184]{1,0:T(8,128)(2,1)} collective-permute-done((bf16[6,29184]{1,0:T(8,128)(2,1)}, bf16[6,29184]{1,0:T(8,128)(2,1)}, u32[]{:S(2)}, u32[]{:S(2)}) %collective-permute-start.11) | collective-permute-done | bytes 350240 | tf_op jit(solution)/shard_map/ppermute | solution.py:664
  763.6 50.5 %collective-permute-done.12 = bf16[6,29184]{1,0:T(8,128)(2,1)} collective-permute-done((bf16[6,29184]{1,0:T(8,128)(2,1)}, bf16[6,29184]{1,0:T(8,128)(2,1)}, u32[]{:S(2)}, u32[]{:S(2)}) %collective-permute-start.12) | collective-permute-done | bytes 350240 | tf_op jit(solution)/shard_map/ppermute | solution.py:664
  814.1 14.8 all-to-all-start.8
  856.7 110.8 %grid_block.2 = (bf16[24,161,180]{2,1,0:T(8,128)(2,1)}, bf16[24,161,180]{2,1,0:T(8,128)(2,1)}, bf16[24,161,180]{2,1,0:T(8,128)(2,1)}, bf16[24,161,180]{2,1,0:T(8...) custom-call(s32[1]{0:T(128)} %bitcast.me_ref, ...), custom_call_target="tpu_custom_call" | custom-call | tf_op jit(solution)/shard_map/grid_block/pallas_call | solution.py:479
  995.4 33.2 %grid_block.3 = (bf16[6,161,180]{2,1,0:T(8,128)(2,1)}, bf16[6,161,180]{2,1,0:T(8,128)(2,1)}, bf16[6,161,180]{2,1,0:T(8,128)(2,1)}, bf16[6,161,180]{2,1,0:T(8,128...) custom-call(s32[1]{0:T(128)} %bitcast.me_ref, ...), custom_call_target="tpu_custom_call" | custom-call | tf_op jit(solution)/shard_map/grid_block/pallas_call | solution.py:479
  1055.2 9.6 fusion.2
  1075.6 52.7 %collective-permute-done.15.refs_5_ = bf16[6,29184]{1,0:T(8,128)(2,1)S(1)} collective-permute-done((bf16[6,29184]{1,0:T(8,128)(2,1)}, bf16[6,29184]{1,0:T(8,128)(2,1)S(1)}, u32[]{:S(2)}, u32[]{:S(2)}) %collective-permute-start.15) | collective-permute-done | bytes 350240 | tf_op jit(solution)/shard_map/ppermute | solution.py:664
  1129.2 58.4 %collective-permute-done.16.refs_6_ = bf16[6,29184]{1,0:T(8,128)(2,1)S(1)} collective-permute-done((bf16[6,29184]{1,0:T(8,128)(2,1)}, bf16[6,29184]{1,0:T(8,128)(2,1)S(1)}, u32[]{:S(2)}, u32[]{:S(2)}) %collective-permute-start.16) | collective-permute-done | bytes 350240 | tf_op jit(solution)/shard_map/ppermute | solution.py:664
  1200.2 10.9 synthesis_back.2
  1211.0 12.3 all-to-all-done.14.x_ref
  1223.3 5.0 all-to-all-start.10
  1228.4 57.3 %reduce-scatter.6.cloned.1.call-done = bf16[4,1,192,768]{3,2,0,1:T(8,128)(2,1)} async-done(((bf16[4,4,192,768]{3,2,0,1:T(8,128)(2,1)}), bf16[4,1,192,768]{3,2,0,1:T(8,128)(2,1)}) %reduce-scatter.6.cloned.1.call-update) | async-done | bytes 1179664 | tf_op jit(solution)/shard_map/reduce_scatter | solution.py:753
  1288.6 9.3 mix_backward.3
  1297.9 20.0 %all-to-all-done.10.x_ref = bf16[8,576,768]{2,1,0:T(8,128)(2,1)} async-done(((bf16[8,576,768]{2,1,0:T(8,128)(2,1)}), bf16[8,576,768]{2,1,0:T(8,128)(2,1)}, u32[]{:S(2)}, u32[]{:S(2)}) %all-to-all-start.10) | async-done | bytes 7077920 | tf_op jit(solution)/shard_map/all_to_all | solution.py:593
  1317.9 19.5 %mix_backward.2 = (bf16[8,576,768]{2,1,0:T(8,128)(2,1)}, bf16[12,384,768]{2,1,0:T(8,128)(2,1)}) custom-call(bf16[8,576,768]{2,1,0:T(8,128)(2,1)} %all-to-all-done.10.x_ref, bf16[4,12,168,768]{3,2,1,0:T(8,128)(2,1)} %bitcast.67), custom_call_target="tpu_custom_call" | custom-call | tf_op jit(solution)/shard_map/mix_backward/pallas_call | solution.py:363
  1337.4 16.8 weight_grads.1
  1354.3 85.6 %all_to_all.85.x_ref = bf16[8,576,768]{2,1,0:T(8,128)(2,1)} all-to-all(bf16[8,576,768]{2,1,0:T(8,128)(2,1)} %get-tuple-element.149), channel_id=1, replica_groups=mesh['sp'=8,'tp'=4] {'sp'}, dimensions={0} | all-to-all | bytes 14155776 | tf_op jit(solution)/shard_map/all_to_all | solution.py:593
  1444.1 10.5 analysis_back.2
  1454.6 12.7 all-to-all-done.15.x_ref
  1476.6 75.5 %all-to-all-done.12 = bf16[8,576,768]{2,1,0:T(8,128)(2,1)} async-done(((bf16[8,576,768]{2,1,0:T(8,128)(2,1)}), bf16[8,576,768]{2,1,0:T(8,128)(2,1)}, u32[]{:S(2)}, u32[]{:S(2)}) %all-to-all-start.12) | async-done | bytes 7077920 | tf_op jit(solution)/shard_map/all_to_all | solution.py:593
  1552.1 11.8 all-to-all-start.16
  1563.9 20.6 %grid_final.2 = (bf16[24,161,180]{2,1,0:T(8,128)(2,1)S(1)}, bf16[24,161,180]{2,1,0:T(8,128)(2,1)S(1)}, bf16[24,161,180]{2,1,0:T(8,128)(2,1)}, bf16[24,161,180]{2,1,0:T(8,128)(2,1)}, f32[1,768]{1,0:T(1,128)S(1)}) custom-call(s32[1]{0:T(128)} %bitcast.me_ref, bf16[8,2,288,768]{3,2,1,0:T(8,128)(2,1)} %bitcast.28.c_ref, ...), custom_call_target="tpu_custom_call" | custom-call | tf_op jit(solution)/shard_map/grid_final/pallas_call | solution.py:557
  1603.3 12.4 unpack_rows.2
  1635.0 36.5 %all-to-all-done.16 = bf16[32,36,768]{2,1,0:T(8,128)(2,1)} async-done(((bf16[32,36,768]{2,1,0:T(8,128)(2,1)}), bf16[32,36,768]{2,1,0:T(8,128)(2,1)}, u32[]{:S(2)}, u32[]{:S(2)}) %all-to-all-start.16) | async-done | bytes 1769504 | tf_op jit(solution)/shard_map/all_to_all | solution.py:593
  1672.9 5.2 grid_final.3
  1694.2 29.1 %collective-permute-start.21 = (bf16[6,29184]{1,0:T(8,128)(2,1)}, bf16[6,29184]{1,0:T(8,128)(2,1)S(1)}, u32[]{:S(2)}, u32[]{:S(2)}) collective-permute-start(bf16[6,29184]{1,0:T(8,128)(2,1)} %pad.72), channel_id=1, source_target_pairs={{0,1},{1,0},{2,3},{3,2},{4,5},{5,4},{6,7},{7,6},{8,9},{9,8},{10,11... | collective-permute-start | bytes 1050632 | tf_op jit(solution)/shard_map/ppermute | solution.py:664
  1723.4 20.3 %fusion.35 = (bf16[12,192,768]{2,1,0:T(8,128)(2,1)}, f32[12,192,768]{2,1,0:T(8,128)}, f32[12,192,768]{2,1,0:T(8,128)}, f32[12,192,768]{2,1,0:T(8,128)}) fusion(f32[12,192,768]{2,1,0:T(8,128)} %param.23, bf16[12,168,768]{2,1,0:T(8,128)(2,1)} %bitcast.81, f32[192,768]{1,0:T(8,128)} %get-tuple-element.199, pred[12]{0:T(512)(128)(4,1)S(1)} %get-tuple-element.217, ...), kind=kLoop, calls=%fused_computation.95 | loop fusion | flops 35389440 | bytes 51462192 | tf_op jit(solution)/shard_map/convert_element_type | solution.py:769
  1743.6 50.3 %psum.15 = f32[2,768]{1,0:T(2,128)S(1)} all-reduce(f32[2,768]{1,0:T(2,128)S(1)} %pad_maximum_fusion.2), channel_id=1, replica_groups=mesh['sp'=8,'tp'=4] {'sp','tp'}, use_global_device_ids=true, to_apply=%region_4.5 | all-reduce | flops 1536 | bytes 12288 | tf_op jit(solution)/shard_map/psum | solution.py:762
  1794.7 12.9 unpack_rows.3
  (312 shorter events, 337.0 us)
Async XLA Ops:
  7.2 821.8 %copy-start = (s32[2]{0:T(128)S(1)}, s32[2]{0:T(128)}, u32[]{:S(2)}) copy-start(s32[2]{0:T(128)} %param.20) | copy-start | bytes 28
  7.2 53.0 %reduce-scatter.10.cloned.1.call-start = ((), (), s32[]{:S(2)}) async-start(), calls=%async_computation.25 | async-start | bytes 1327104
  20.2 557.0 %all-gather.4.cloned.1.call-start = ((), (), s32[]{:S(2)}) async-start(), calls=%async_computation.20 | async-start | bytes 4866048 | tf_op jit(solution)/shard_map/all_gather | solution.py:671
  33.6 34.0 %collective-permute-start = (bf16[24,29184]{1,0:T(8,128)(2,1)}, bf16[24,29184]{1,0:T(8,128)(2,1)}, u32[]{:S(2)}, u32[]{:S(2)}) collective-permute-start(bf16[24,29184]{1,0:T(8,128)(2,1)} %get-tuple-element.96), channel_id=1, source_target_pairs={{0,1},{1,0},{2,3},{3,2},{4,5},{5,4},{6,7},{7,6},{8,9},{9,8},{10,11... | collective-permute-start | bytes 4202504 | tf_op jit(solution)/shard_map/ppermute | solution.py:664
  67.6 509.6 %all-gather.6.cloned.1.call-start = ((), (), s32[]{:S(2)}) async-start(), calls=%async_computation.24 | async-start | bytes 15482880 | tf_op jit(solution)/shard_map/all_gather | solution.py:676
  67.7 189.8 %collective-permute-start.1 = (bf16[24,29184]{1,0:T(8,128)(2,1)}, bf16[24,29184]{1,0:T(8,128)(2,1)}, u32[]{:S(2)}, u32[]{:S(2)}) collective-permute-start(bf16[24,29184]{1,0:T(8,128)(2,1)} %copy-done.34), channel_id=1, source_target_pairs={{0,2},{1,3},{2,0},{3,1},{4,6},{5,7},{6,4},{7,5},{8,10},{9,11},{10,... | collective-permute-start | bytes 4202504 | tf_op jit(solution)/shard_map/ppermute | solution.py:664
  70.5 194.8 %collective-permute-start.2 = (bf16[24,29184]{1,0:T(8,128)(2,1)S(1)}, bf16[24,29184]{1,0:T(8,128)(2,1)}, u32[]{:S(2)}, u32[]{:S(2)}) collective-permute-start(bf16[24,29184]{1,0:T(8,128)(2,1)S(1)} %get-tuple-element.98), channel_id=1, source_target_pairs={{0,3},{1,2},{2,1},{3,0},{4,7},{5,6},{6,5},{7,4},{8,11},{9,10},{10,... | collective-permute-start | bytes 4202504 | tf_op jit(solution)/shard_map/ppermute | solution.py:664
  71.8 73.3 %collective-permute-start.3 = (bf16[6,29184]{1,0:T(8,128)(2,1)}, bf16[6,29184]{1,0:T(8,128)(2,1)}, u32[]{:S(2)}, u32[]{:S(2)}) collective-permute-start(bf16[6,29184]{1,0:T(8,128)(2,1)} %copy-done.39), channel_id=1, source_target_pairs={{0,1},{1,0},{2,3},{3,2},{4,5},{5,4},{6,7},{7,6},{8,9},{9,8},{10,11... | collective-permute-start | bytes 1050632 | tf_op jit(solution)/shard_map/ppermute | solution.py:664
  72.1 171.9 %collective-permute-start.4 = (bf16[6,29184]{1,0:T(8,128)(2,1)}, bf16[6,29184]{1,0:T(8,128)(2,1)}, u32[]{:S(2)}, u32[]{:S(2)}) collective-permute-start(bf16[6,29184]{1,0:T(8,128)(2,1)} %copy-done.38), channel_id=1, source_target_pairs={{0,2},{1,3},{2,0},{3,1},{4,6},{5,7},{6,4},{7,5},{8,10},{9,11},{10,... | collective-permute-start | bytes 1050632 | tf_op jit(solution)/shard_map/ppermute | solution.py:664
  74.9 171.0 %collective-permute-start.5 = (bf16[6,29184]{1,0:T(8,128)(2,1)}, bf16[6,29184]{1,0:T(8,128)(2,1)}, u32[]{:S(2)}, u32[]{:S(2)}) collective-permute-start(bf16[6,29184]{1,0:T(8,128)(2,1)} %copy-done.35), channel_id=1, source_target_pairs={{0,3},{1,2},{2,1},{3,0},{4,7},{5,6},{6,5},{7,4},{8,11},{9,10},{10,... | collective-permute-start | bytes 1050632 | tf_op jit(solution)/shard_map/ppermute | solution.py:664
  272.2 16.5 all-to-all-start
  310.2 84.9 %all-to-all-start.1 = ((bf16[8,576,768]{2,1,0:T(8,128)(2,1)}), bf16[8,576,768]{2,1,0:T(8,128)(2,1)}, u32[]{:S(2)}, u32[]{:S(2)}) async-start(bf16[8,576,768]{2,1,0:T(8,128)(2,1)} %bitcast.74), calls=%async_computation.1 | async-start | bytes 14155776 | tf_op jit(solution)/shard_map/all_to_all | solution.py:593
  395.0 92.4 %all-to-all-start.5 = ((bf16[32,36,768]{2,1,0:T(8,128)(2,1)}), bf16[32,36,768]{2,1,0:T(8,128)(2,1)S(1)}, u32[]{:S(2)}, u32[]{:S(2)}) async-start(bf16[32,36,768]{2,1,0:T(8,128)(2,1)} %copy-done.12), calls=%async_computation.5 | async-start | bytes 3932160 | tf_op jit(solution)/shard_map/all_to_all | solution.py:593
  399.0 94.5 %copy-start.44 = (bf16[96,12,96]{0,2,1:T(8,128)(2,1)}, bf16[96,12,96]{0,2,1:T(8,128)(2,1)S(1)}, u32[]{:S(2)}) copy-start(bf16[96,12,96]{0,2,1:T(8,128)(2,1)S(1)} %convolution_convert_fusion.1) | copy-start | bytes 663556
  488.7 84.9 %all-to-all-start.2 = ((bf16[8,576,768]{2,1,0:T(8,128)(2,1)}), bf16[8,576,768]{2,1,0:T(8,128)(2,1)}, u32[]{:S(2)}, u32[]{:S(2)}) async-start(bf16[8,576,768]{2,1,0:T(8,128)(2,1)} %analysis.2), calls=%async_computation.2 | async-start | bytes 14155776 | tf_op jit(solution)/shard_map/all_to_all | solution.py:593
  573.6 26.7 %all-to-all-start.6 = ((bf16[8,144,768]{2,1,0:T(8,128)(2,1)}), bf16[8,144,768]{2,1,0:T(8,128)(2,1)S(1)}, u32[]{:S(2)}, u32[]{:S(2)}) async-start(bf16[8,144,768]{2,1,0:T(8,128)(2,1)} %analysis.3), calls=%async_computation.6 | async-start | bytes 3538944 | tf_op jit(solution)/shard_map/all_to_all | solution.py:593
  601.5 84.8 %all-to-all-start.3 = ((bf16[8,576,768]{2,1,0:T(8,128)(2,1)}), bf16[8,576,768]{2,1,0:T(8,128)(2,1)}, u32[]{:S(2)}, u32[]{:S(2)}) async-start(bf16[8,576,768]{2,1,0:T(8,128)(2,1)} %get-tuple-element.107), calls=%async_computation.3 | async-start | bytes 14155776 | tf_op jit(solution)/shard_map/all_to_all | solution.py:593
  616.6 66.2 %collective-permute-start.6 = (bf16[24,29184]{1,0:T(8,128)(2,1)S(1)}, bf16[24,29184]{1,0:T(8,128)(2,1)S(1)}, u32[]{:S(2)}, u32[]{:S(2)}) collective-permute-start(bf16[24,29184]{1,0:T(8,128)(2,1)S(1)} %get-tuple-element.111), channel_id=1, source_target_pairs={{0,1},{1,0},{2,3},{3,2},{4,5},{5,4},{6,7},{7,6},{8,9},{9,8},{10,11... | collective-permute-start | bytes 4202504 | tf_op jit(solution)/shard_map/ppermute | solution.py:664
  621.5 61.3 %collective-permute-start.7 = (bf16[24,29184]{1,0:T(8,128)(2,1)S(1)}, bf16[24,29184]{1,0:T(8,128)(2,1)}, u32[]{:S(2)}, u32[]{:S(2)}) collective-permute-start(bf16[24,29184]{1,0:T(8,128)(2,1)S(1)} %get-tuple-element.113), channel_id=1, source_target_pairs={{0,3},{1,2},{2,1},{3,0},{4,7},{5,6},{6,5},{7,4},{8,11},{9,10},{10,... | collective-permute-start | bytes 4202504 | tf_op jit(solution)/shard_map/ppermute | solution.py:664
  686.3 27.9 %all-to-all-start.7 = ((bf16[8,144,768]{2,1,0:T(8,128)(2,1)}), bf16[8,144,768]{2,1,0:T(8,128)(2,1)}, u32[]{:S(2)}, u32[]{:S(2)}) async-start(bf16[8,144,768]{2,1,0:T(8,128)(2,1)} %get-tuple-element.129), calls=%async_computation.7 | async-start | bytes 3538944 | tf_op jit(solution)/shard_map/all_to_all | solution.py:593
  714.2 99.9 %all-to-all-start.4 = ((bf16[8,576,768]{2,1,0:T(8,128)(2,1)}), bf16[8,576,768]{2,1,0:T(8,128)(2,1)}, u32[]{:S(2)}, u32[]{:S(2)}) async-start(bf16[8,576,768]{2,1,0:T(8,128)(2,1)} %synthesis.2), calls=%async_computation.4 | async-start | bytes 14155776 | tf_op jit(solution)/shard_map/all_to_all | solution.py:593
  719.0 95.1 %collective-permute-start.8 = (bf16[24,29184]{1,0:T(8,128)(2,1)S(1)}, bf16[24,29184]{1,0:T(8,128)(2,1)}, u32[]{:S(2)}, u32[]{:S(2)}) collective-permute-start(bf16[24,29184]{1,0:T(8,128)(2,1)S(1)} %get-tuple-element.120), channel_id=1, source_target_pairs={{0,2},{1,3},{2,0},{3,1},{4,6},{5,7},{6,4},{7,5},{8,10},{9,11},{10,... | collective-permute-start | bytes 4202504 | tf_op jit(solution)/shard_map/ppermute | solution.py:664
  722.4 41.2 %collective-permute-start.11 = (bf16[6,29184]{1,0:T(8,128)(2,1)}, bf16[6,29184]{1,0:T(8,128)(2,1)}, u32[]{:S(2)}, u32[]{:S(2)}) collective-permute-start(bf16[6,29184]{1,0:T(8,128)(2,1)} %copy-done.37), channel_id=1, source_target_pairs={{0,1},{1,0},{2,3},{3,2},{4,5},{5,4},{6,7},{7,6},{8,9},{9,8},{10,11... | collective-permute-start | bytes 1050632 | tf_op jit(solution)/shard_map/ppermute | solution.py:664
  724.1 90.0 %collective-permute-start.12 = (bf16[6,29184]{1,0:T(8,128)(2,1)}, bf16[6,29184]{1,0:T(8,128)(2,1)}, u32[]{:S(2)}, u32[]{:S(2)}) collective-permute-start(bf16[6,29184]{1,0:T(8,128)(2,1)} %copy-done.36), channel_id=1, source_target_pairs={{0,2},{1,3},{2,0},{3,1},{4,6},{5,7},{6,4},{7,5},{8,10},{9,11},{10,... | collective-permute-start | bytes 1050632 | tf_op jit(solution)/shard_map/ppermute | solution.py:664
  727.0 87.1 %collective-permute-start.13 = (bf16[6,29184]{1,0:T(8,128)(2,1)S(1)}, bf16[6,29184]{1,0:T(8,128)(2,1)}, u32[]{:S(2)}, u32[]{:S(2)}) collective-permute-start(bf16[6,29184]{1,0:T(8,128)(2,1)S(1)} %get-tuple-element.133), channel_id=1, source_target_pairs={{0,3},{1,2},{2,1},{3,0},{4,7},{5,6},{6,5},{7,4},{8,11},{9,10},{10,... | collective-permute-start | bytes 1050632 | tf_op jit(solution)/shard_map/ppermute | solution.py:664
  814.1 153.5 %all-to-all-start.8 = ((bf16[32,36,768]{2,1,0:T(8,128)(2,1)}), bf16[32,36,768]{2,1,0:T(8,128)(2,1)}, u32[]{:S(2)}, u32[]{:S(2)}) async-start(bf16[32,36,768]{2,1,0:T(8,128)(2,1)} %synthesis.3), calls=%async_computation.8 | async-start | bytes 3932160 | tf_op jit(solution)/shard_map/all_to_all | solution.py:593
  967.6 85.0 %all-to-all-start.9 = ((bf16[8,576,768]{2,1,0:T(8,128)(2,1)}), bf16[8,576,768]{2,1,0:T(8,128)(2,1)}, u32[]{:S(2)}, u32[]{:S(2)}) async-start(bf16[8,576,768]{2,1,0:T(8,128)(2,1)} %bitcast.73), calls=%async_computation.9 | async-start | bytes 14155776 | tf_op jit(solution)/shard_map/all_to_all | solution.py:593
  980.5 69.5 %collective-permute-start.10 = (bf16[24,29184]{1,0:T(8,128)(2,1)}, bf16[24,29184]{1,0:T(8,128)(2,1)}, u32[]{:S(2)}, u32[]{:S(2)}) collective-permute-start(bf16[24,29184]{1,0:T(8,128)(2,1)} %pad.60), channel_id=1, source_target_pairs={{0,3},{1,2},{2,1},{3,0},{4,7},{5,6},{6,5},{7,4},{8,11},{9,10},{10,... | collective-permute-start | bytes 4202504 | tf_op jit(solution)/shard_map/ppermute | solution.py:664
  984.1 66.0 %collective-permute-start.9 = (bf16[24,29184]{1,0:T(8,128)(2,1)}, bf16[24,29184]{1,0:T(8,128)(2,1)S(1)}, u32[]{:S(2)}, u32[]{:S(2)}) collective-permute-start(bf16[24,29184]{1,0:T(8,128)(2,1)} %pad.58), channel_id=1, source_target_pairs={{0,1},{1,0},{2,3},{3,2},{4,5},{5,4},{6,7},{7,6},{8,9},{9,8},{10,11... | collective-permute-start | bytes 4202504 | tf_op jit(solution)/shard_map/ppermute | solution.py:664
  1052.6 136.5 %collective-permute-start.14 = (bf16[24,29184]{1,0:T(8,128)(2,1)}, bf16[24,29184]{1,0:T(8,128)(2,1)}, u32[]{:S(2)}, u32[]{:S(2)}) collective-permute-start(bf16[24,29184]{1,0:T(8,128)(2,1)} %pad.59), channel_id=1, source_target_pairs={{0,2},{1,3},{2,0},{3,1},{4,6},{5,7},{6,4},{7,5},{8,10},{9,11},{10,... | collective-permute-start | bytes 4202504 | tf_op jit(solution)/shard_map/ppermute | solution.py:664
  1064.8 126.9 %all-to-all-start.13 = ((bf16[32,36,768]{2,1,0:T(8,128)(2,1)}), bf16[32,36,768]{2,1,0:T(8,128)(2,1)}, u32[]{:S(2)}, u32[]{:S(2)}) async-start(bf16[32,36,768]{2,1,0:T(8,128)(2,1)} %get-tuple-element.153), calls=%async_computation.13 | async-start | bytes 3932160 | tf_op jit(solution)/shard_map/all_to_all | solution.py:593
  1068.3 217.4 %reduce-scatter.6.cloned.1.call-start = ((), (), s32[]{:S(2)}) async-start(), calls=%async_computation.21 | async-start | bytes 5898240 | tf_op jit(solution)/shard_map/reduce_scatter | solution.py:753
  1068.3 60.0 %collective-permute-start.15 = (bf16[6,29184]{1,0:T(8,128)(2,1)}, bf16[6,29184]{1,0:T(8,128)(2,1)S(1)}, u32[]{:S(2)}, u32[]{:S(2)}) collective-permute-start(bf16[6,29184]{1,0:T(8,128)(2,1)} %pad.62), channel_id=1, source_target_pairs={{0,1},{1,0},{2,3},{3,2},{4,5},{5,4},{6,7},{7,6},{8,9},{9,8},{10,11... | collective-permute-start | bytes 1050632 | tf_op jit(solution)/shard_map/ppermute | solution.py:664
  1070.0 117.5 %collective-permute-start.16 = (bf16[6,29184]{1,0:T(8,128)(2,1)}, bf16[6,29184]{1,0:T(8,128)(2,1)S(1)}, u32[]{:S(2)}, u32[]{:S(2)}) collective-permute-start(bf16[6,29184]{1,0:T(8,128)(2,1)} %pad.63), channel_id=1, source_target_pairs={{0,2},{1,3},{2,0},{3,1},{4,6},{5,7},{6,4},{7,5},{8,10},{9,11},{10,... | collective-permute-start | bytes 1050632 | tf_op jit(solution)/shard_map/ppermute | solution.py:664
  1072.5 115.8 %collective-permute-start.17 = (bf16[6,29184]{1,0:T(8,128)(2,1)}, bf16[6,29184]{1,0:T(8,128)(2,1)S(1)}, u32[]{:S(2)}, u32[]{:S(2)}) collective-permute-start(bf16[6,29184]{1,0:T(8,128)(2,1)} %pad.64), channel_id=1, source_target_pairs={{0,3},{1,2},{2,1},{3,0},{4,7},{5,6},{6,5},{7,4},{8,11},{9,10},{10,... | collective-permute-start | bytes 1050632 | tf_op jit(solution)/shard_map/ppermute | solution.py:664
  1195.8 27.5 %all-to-all-start.14 = ((bf16[8,144,768]{2,1,0:T(8,128)(2,1)}), bf16[8,144,768]{2,1,0:T(8,128)(2,1)}, u32[]{:S(2)}, u32[]{:S(2)}) async-start(bf16[8,144,768]{2,1,0:T(8,128)(2,1)} %synthesis_back.3), calls=%async_computation.14 | async-start | bytes 3538944 | tf_op jit(solution)/shard_map/all_to_all | solution.py:593
  1223.3 94.5 %all-to-all-start.10 = ((bf16[8,576,768]{2,1,0:T(8,128)(2,1)}), bf16[8,576,768]{2,1,0:T(8,128)(2,1)}, u32[]{:S(2)}, u32[]{:S(2)}) async-start(bf16[8,576,768]{2,1,0:T(8,128)(2,1)} %synthesis_back.2), calls=%async_computation.10 | async-start | bytes 14155776 | tf_op jit(solution)/shard_map/all_to_all | solution.py:593
  1228.4 387.3 %all-reduce.19.cloned.1.call-start = ((), (), s32[]{:S(2)}) async-start(), calls=%async_computation.22 | async-start | bytes 4718592 | tf_op jit(solution)/shard_map/psum | solution.py:755
  1288.6 434.8 %reduce-scatter.8.cloned.1.call-start = ((), (), s32[]{:S(2)}) async-start(), calls=%async_computation.23 | async-start | bytes 15482880 | tf_op jit(solution)/shard_map/reduce_scatter | solution.py:754
  1439.8 27.5 %all-to-all-start.15 = ((bf16[8,144,768]{2,1,0:T(8,128)(2,1)}), bf16[8,144,768]{2,1,0:T(8,128)(2,1)}, u32[]{:S(2)}, u32[]{:S(2)}) async-start(bf16[8,144,768]{2,1,0:T(8,128)(2,1)} %get-tuple-element.155), calls=%async_computation.15 | async-start | bytes 3538944 | tf_op jit(solution)/shard_map/all_to_all | solution.py:593
  1467.3 84.9 %all-to-all-start.12 = ((bf16[8,576,768]{2,1,0:T(8,128)(2,1)}), bf16[8,576,768]{2,1,0:T(8,128)(2,1)}, u32[]{:S(2)}, u32[]{:S(2)}) async-start(bf16[8,576,768]{2,1,0:T(8,128)(2,1)} %analysis_back.2), calls=%async_computation.12 | async-start | bytes 14155776 | tf_op jit(solution)/shard_map/all_to_all | solution.py:593
  1552.1 119.3 %all-to-all-start.16 = ((bf16[32,36,768]{2,1,0:T(8,128)(2,1)}), bf16[32,36,768]{2,1,0:T(8,128)(2,1)}, u32[]{:S(2)}, u32[]{:S(2)}) async-start(bf16[32,36,768]{2,1,0:T(8,128)(2,1)} %analysis_back.3), calls=%async_computation.16 | async-start | bytes 3932160 | tf_op jit(solution)/shard_map/all_to_all | solution.py:593
  1594.1 100.1 %collective-permute-start.20 = (bf16[24,29184]{1,0:T(8,128)(2,1)}, bf16[24,29184]{1,0:T(8,128)(2,1)}, u32[]{:S(2)}, u32[]{:S(2)}) collective-permute-start(bf16[24,29184]{1,0:T(8,128)(2,1)} %pad.70), channel_id=1, source_target_pairs={{0,3},{1,2},{2,1},{3,0},{4,7},{5,6},{6,5},{7,4},{8,11},{9,10},{10,... | collective-permute-start | bytes 4202504 | tf_op jit(solution)/shard_map/ppermute | solution.py:664
  1634.2 160.5 %collective-permute-start.19 = (bf16[24,29184]{1,0:T(8,128)(2,1)}, bf16[24,29184]{1,0:T(8,128)(2,1)}, u32[]{:S(2)}, u32[]{:S(2)}) collective-permute-start(bf16[24,29184]{1,0:T(8,128)(2,1)} %pad.69), channel_id=1, source_target_pairs={{0,2},{1,3},{2,0},{3,1},{4,6},{5,7},{6,4},{7,5},{8,10},{9,11},{10,... | collective-permute-start | bytes 4202504 | tf_op jit(solution)/shard_map/ppermute | solution.py:664
  1634.2 160.5 %collective-permute-start.18 = (bf16[24,29184]{1,0:T(8,128)(2,1)}, bf16[24,29184]{1,0:T(8,128)(2,1)}, u32[]{:S(2)}, u32[]{:S(2)}) collective-permute-start(bf16[24,29184]{1,0:T(8,128)(2,1)} %pad.68), channel_id=1, source_target_pairs={{0,1},{1,0},{2,3},{3,2},{4,5},{5,4},{6,7},{7,6},{8,9},{9,8},{10,11... | collective-permute-start | bytes 4202504 | tf_op jit(solution)/shard_map/ppermute | solution.py:664
  1689.0 105.6 %collective-permute-start.23 = (bf16[6,29184]{1,0:T(8,128)(2,1)}, bf16[6,29184]{1,0:T(8,128)(2,1)S(1)}, u32[]{:S(2)}, u32[]{:S(2)}) collective-permute-start(bf16[6,29184]{1,0:T(8,128)(2,1)} %pad.74), channel_id=1, source_target_pairs={{0,3},{1,2},{2,1},{3,0},{4,7},{5,6},{6,5},{7,4},{8,11},{9,10},{10,... | collective-permute-start | bytes 1050632 | tf_op jit(solution)/shard_map/ppermute | solution.py:664
  1692.5 102.2 %collective-permute-start.22 = (bf16[6,29184]{1,0:T(8,128)(2,1)}, bf16[6,29184]{1,0:T(8,128)(2,1)S(1)}, u32[]{:S(2)}, u32[]{:S(2)}) collective-permute-start(bf16[6,29184]{1,0:T(8,128)(2,1)} %pad.73), channel_id=1, source_target_pairs={{0,2},{1,3},{2,0},{3,1},{4,6},{5,7},{6,4},{7,5},{8,10},{9,11},{10,... | collective-permute-start | bytes 1050632 | tf_op jit(solution)/shard_map/ppermute | solution.py:664
  1694.2 100.5 %collective-permute-start.21 = (bf16[6,29184]{1,0:T(8,128)(2,1)}, bf16[6,29184]{1,0:T(8,128)(2,1)S(1)}, u32[]{:S(2)}, u32[]{:S(2)}) collective-permute-start(bf16[6,29184]{1,0:T(8,128)(2,1)} %pad.72), channel_id=1, source_target_pairs={{0,1},{1,0},{2,3},{3,2},{4,5},{5,4},{6,7},{7,6},{8,9},{9,8},{10,11... | collective-permute-start | bytes 1050632 | tf_op jit(solution)/shard_map/ppermute | solution.py:664
  (54 other events, 815.6 us)
Sparse Core Ops, SparseCore 0:
  20.4 39.7 reduce-scatter.9
  67.7 153.8 all-gather.3
  271.1 264.4 all-gather.5
  1191.8 93.7 reduce-scatter.5
  1289.7 71.0 all-reduce.18
  1363.0 210.5 reduce-scatter.7

commit v3 on v2

--- a/solution.py
+++ b/solution.py
@@ -665,43 +665,55 @@
     send_all = lambda arrays: [send(a, d) for d, a in enumerate(arrays)]
     rows3 = lambda v: v.reshape(v.shape[0], -1, cp)
 
+    turn = []
+
+    def swap_next(value, axes, *ties):
+        out = swap(after(value, *turn, *ties), axes)
+        turn[:] = [out]
+        return out
+
     main, left = pack_rows(state, me, plan, lanes, tile)
-    dense = lax.psum_scatter(jnp.stack(raw), "sp", scatter_dimension=1, tiled=True)
-    main, left = send_all(main), send_all(left)
-    dense = lax.all_gather(after(dense, main[1]), ("tp", "sp"), axis=1, tiled=True)
-    w_in = dense[:2].reshape(2 * cp, cp)
-    w_out = dense[2:].reshape(2 * cp, cp)
+    main = send_all(after(main, gains_all))
+    left = send_all(after(left, main[1])) if left else []
     main, left = [cut(a) for a in main], [cut(a) for a in left]
     x5 = [main, left]
-    spec_w = lax.all_gather(after(copies[:, :CROWS], main, left), "tp", axis=0, tiled=False)
+    spec_w = lax.all_gather(after(copies[:, :CROWS], main, gains_all), "tp", axis=0, tiled=False)
     gain_a, gain_b = gains_all[:1], gains_all[1:]
     n = len(chunks)
     odd = lambda arrays: [send(a, d) if d % 2 else a for d, a in enumerate(arrays)]
     even = lambda arrays: [a if d % 2 else send(a, d) for d, a in enumerate(arrays)]
 
-    coefs, xts = [], []
+    fs, xts = [], []
     for i, ck in enumerate(chunks):
         f, xt = fourier(ck, x5[i], me, fwd, eye, gain_a, cmask2, row_masks[i], csh)
         xts.append(xt)
-        f = swap(rows3(f), ck.axes)
+        if i == 1:
+            fs[0] = after(fs[0], f)
+        fs.append(swap_next(rows3(f), ck.axes))
+    dense = lax.psum_scatter(after(jnp.stack(raw), fs[0]), "sp", scatter_dimension=1, tiled=True)
+    coefs = []
+    for f, ck in zip(fs, chunks):
         c = legendre(ck, f, table(ck, ana_q), n_sp, False, "analysis")
-        coefs.append(swap(c, "sp"))
-    m, a = mix(chunks[0], after(coefs[0], dense), spec_w, csh, NT, "mix_forward")
-    mixed, coef_q = [swap(m, "sp")], [a]
-    main, left = pack_rows(after(cotangent, m), me, plan, lanes, tile)
+        coefs.append(swap_next(c, "sp", *((spec_w,) if ck.left else ())))
+    coefs[0] = after(coefs[0], dense)
+    dense = lax.all_gather(after(dense, coefs[0]), "tp", axis=1, tiled=False)
+    m, a = mix(chunks[0], coefs[0], spec_w, csh, NT, "mix_forward")
+    mixed, coef_q = [swap_next(m, "sp")], [a]
+    main, left = pack_rows(after(cotangent, m, dense), me, plan, lanes, tile)
     ahead = odd(main)
     if n > 1:
         m, a = mix(chunks[1], after(coefs[1], main), spec_w, csh, NT, "mix_forward")
-        mixed.append(swap(after(m, ahead), "sp"))
+        mixed.append(swap_next(m, "sp", ahead))
         coef_q.append(a)
+    dense = lax.all_gather(after(dense, mixed[0]), "sp", axis=2, tiled=True)
+    w_in = dense[:2].reshape(2 * cp, cp)
+    w_out = dense[2:].reshape(2 * cp, cp)
     main, left = after((ahead, left), mixed[0])
     main, left = even(main), send_all(left)
-    synth = [
-        legendre(ck, m, table(ck, syn_j), ck.nd, True, "synthesis") for ck, m in zip(chunks, mixed)
-    ]
-    if n > 1:
-        synth[1] = after(synth[1], main, left)
-    synth = [ck.grid_coef(swap(g, ck.axes)) for ck, g in zip(chunks, synth)]
+    synth = []
+    for i, ck in enumerate(chunks):
+        g = legendre(ck, mixed[i], table(ck, syn_j), ck.nd, True, "synthesis")
+        synth.append(ck.grid_coef(swap_next(g, ck.axes, *((main, left) if i else ()))))
     cot5 = [[cut(a) for a in main], [cut(a) for a in left]]
     outs, rest, dgs = [], [], []
     for i, ck in enumerate(chunks):
@@ -711,32 +723,41 @@
         )
         outs.append([flat_of(a) for a in o])
         rest.append(r)
-        dgs.append(rows3(r[0]))
-    main, left = odd(outs[0]), outs[1] if n > 1 else []
-    if n > 1:
-        dgs[1] = after(dgs[1], main)
-    dgs = [swap(g, ck.axes) for ck, g in zip(chunks, dgs)]
-    main, left = after((main, left), dgs[0])
-    main, left = even(main), send_all(left)
-    dbs = [
-        legendre(ck, g, table(ck, syn_q), n_sp, False, "synthesis_back")
-        for ck, g in zip(chunks, dgs)
-    ]
-    if n > 1:
-        dbs[1] = after(dbs[1], main, left)
-    dbs = [swap(b, "sp") for b in dbs]
-    das = [mix(ck, b, spec_w, csh, NN, "mix_backward") for ck, b in zip(chunks, dbs)]
-    grad_q = [a[1] for a in das]
-    das = [swap(a[0], "sp") for a in das]
+        if i == 0:
+            dgs.append(swap_next(rows3(r[0]), ck.axes))
+            main = odd(outs[0])
+        else:
+            dgs.append(swap_next(rows3(r[0]), ck.axes, main))
+    left = outs[1] if n > 1 else []
+    dbs = []
+    for i, ck in enumerate(chunks):
+        g = legendre(ck, dgs[i], table(ck, syn_q), n_sp, False, "synthesis_back")
+        if i == 0:
+            main, left = after((main, left), g)
+            main, left = even(main), send_all(left)
+            dbs.append(swap_next(g, "sp"))
+        else:
+            dbs.append(swap_next(g, "sp", main))
+    das, grad_q = [], []
+    for ck, b in zip(chunks, dbs):
+        a, g = mix(ck, b, spec_w, csh, NN, "mix_backward")
+        das.append(swap_next(a, "sp", *((left,) if ck.left else ())))
+        grad_q.append(g)
     pieces_out = [(0, main)] + ([(-1, left)] if left else [])
     result = unpack_rows(pieces_out, me, plan, flat, valid, lanes, tile)
     dws = weight_grads(grad_q, coef_q, n_tp, CROWS)
-    dfs = [
-        legendre(ck, a, table(ck, ana_j), ck.nd, True, "analysis_back") for ck, a in zip(chunks, das)
-    ]
-    dfs[0] = swap(dfs[0], chunks[0].axes)
-    if n > 1:
-        dfs[1] = swap(after(dfs[1], dfs[0]), chunks[1].axes)
+    das[0] = after(das[0], dws)
+    dfs = []
+    for ck, a in zip(chunks, das):
+        g = legendre(ck, a, table(ck, ana_j), ck.nd, True, "analysis_back")
+        dfs.append(swap_next(g, ck.axes))
+    half = own // 2
+    scatter = lambda v: lax.psum_scatter(v, "tp", scatter_dimension=0, tiled=False)
+    spec_a = scatter(after(dws[:, :half], pieces_out))
+    dfs[0] = after(dfs[0], spec_a)
+    spec_b = scatter(after(dws[:, half:], spec_a))
+    dfs[-1] = after(dfs[-1], spec_b)
+    spec_g = jnp.concatenate([spec_a, spec_b], axis=0)
     pieces, gg_a = [], 0.0
     for i, ck in enumerate(chunks):
         o, gg = grid_final(
@@ -750,9 +771,9 @@
     dwo = sum(r[3] for r in rest)
     gg_b = sum(r[4] for r in rest)
     dense_g = jnp.stack([dwi, dwo]).reshape(4, n_tp, csh, cp).astype(BF)
-    dense_g = lax.psum_scatter(after(dense_g, pieces_out), "tp", scatter_dimension=1, tiled=False)
-    spec_g = lax.psum_scatter(after(dws, pieces_out), "tp", scatter_dimension=0, tiled=False)
-    dense_g = lax.psum(dense_g.astype(F32), "sp")
+    dense_g = lax.psum_scatter(after(dense_g, dgs[0]), "sp", scatter_dimension=2, tiled=True)
+    dense_g = lax.psum_scatter(after(dense_g, das[0]), "tp", scatter_dimension=1, tiled=False)
+    dense_g = lax.all_gather(after(dense_g, dfs[0]), "sp", axis=1, tiled=True).astype(F32)
     spec_g = jnp.pad(spec_g.astype(F32), ((0, 0), (0, csh - CROWS), (0, 0)))
     grads = spec_g
     for i in range(4):

time: 1830 us -> 1720 us (0.940)
  waiting for transfers between devices: 882 us -> 796 us
  blocking collectives: 136 us -> 67.9 us
  starting transfers between devices: 169 us -> 210 us
    all_to_all x1 -> x0, blocking collectives: 85.6 us -> none  [swap(): return lax.all_to_all(value, axis, split_axis=0, concat_axis=0, tiled=True)]
    ppermute x24, waiting for transfers between devices: 399 us -> 324 us  [local(): lax.ppermute(a, 'tp', [(i, i ^ d) for i in range(n_tp)])]
    reduce_scatter x2 -> x3, waiting for transfers between devices: 57.3 us -> 119 us  [the longest x2 119 us: local(): lax.psum_scatter(v, 'tp', scatter_dimension=0, tiled=False)]
    all_to_all x16 -> x17, waiting for transfers between devices: 403 us -> 352 us  [swap(): return lax.all_to_all(value, axis, split_axis=0, concat_axis=0, tiled=True)]
    all_gather x0 -> x1, blocking collectives: none -> 27.2 us  [local(): dense = lax.all_gather(after(dense, coefs[0]), 'tp', axis=1, tiled=False)]
    unnamed x7 -> x10, waiting for transfers between devices: 23.6 us -> 1.38 us
    ppermute x24, starting transfers between devices: 73.8 us -> 94.6 us  [local(): lax.ppermute(a, 'tp', [(i, i ^ d) for i in range(n_tp)])]
    all_to_all x16 -> x17, starting transfers between devices: 94.7 us -> 115 us  [swap(): return lax.all_to_all(value, axis, split_axis=0, concat_axis=0, tiled=True)]
  transfers between devices with their start and end apart: 46 -> 49, of which waited for: 23 -> 24; matrix products, arithmetic and copies ran while one was open for 11% -> 12% of each run, Pallas kernels for 19% -> 20%
where the time goes in v3:
time: 1720 us; the launch traced here: 1710 us
  waiting for transfers between devices  796 us (46%)
  Pallas kernels  358 us (21%)
  starting transfers between devices  210 us (12%)
  local copies, waits for them, and re-layouts  201 us (12%)
  blocking collectives  67.9 us (4%)
  other arithmetic  50.7 us (3%)
  between operations  20 us (1%)
    all_to_all x17, waiting for transfers between devices, swap(): return lax.all_to_all(value, axis, split_axis=0, concat_axis=0, tiled=True)  352 us
    ppermute x24, waiting for transfers between devices, local(): lax.ppermute(a, 'tp', [(i, i ^ d) for i in range(n_tp)])  324 us
    pallas_call x2, Pallas kernels, grid_block(): pl.pallas_call(body, grid=ck.grid, in_specs=[SMEM, ck.coef_spec(rows_s, c...  144 us
    reduce_scatter x2, waiting for transfers between devices, local(): lax.psum_scatter(v, 'tp', scatter_dimension=0, tiled=False)  119 us
    all_to_all x17, starting transfers between devices, swap(): return lax.all_to_all(value, axis, split_axis=0, concat_axis=0, tiled=True)  115 us
    ppermute x24, starting transfers between devices, local(): lax.ppermute(a, 'tp', [(i, i ^ d) for i in range(n_tp)])  94.6 us
    pallas_call x8, Pallas kernels, legendre(): pl.pallas_call(body, grid=(cp // tile,), in_specs=[pl.BlockSpec((n_src, r...  59.2 us
    pallas_call x4, Pallas kernels, mix(): pl.pallas_call(body, grid=(own // qb,), in_specs=[whole(coef.shape), pl.B...  57.6 us
  transfers between devices with their start and end apart: 49, of which 24 were waited for; matrix products, arithmetic and copies ran while one was open for 12% of the time, Pallas kernels for 20%

profile of v3, /device:TPU:0, one launch (start us, length us, event | category | flops | bytes accessed | tf_op | source)
XLA Modules:
  0.0 1706.5 jit_solution(8191532882625464095)
XLA Ops:
  9.3 6.3 all-to-all-start
  48.0 41.6 %collective-permute-done = bf16[24,29184]{1,0:T(8,128)(2,1)} collective-permute-done((bf16[24,29184]{1,0:T(8,128)(2,1)}, bf16[24,29184]{1,0:T(8,128)(2,1)}, u32[]{:S(2)}, u32[]{:S(2)}) %collective-permute-start) | collective-permute-done | bytes 1400864 | tf_op jit(solution)/shard_map/ppermute | solution.py:664
  95.1 29.9 %collective-permute-done.1 = bf16[24,29184]{1,0:T(8,128)(2,1)} collective-permute-done((bf16[24,29184]{1,0:T(8,128)(2,1)}, bf16[24,29184]{1,0:T(8,128)(2,1)}, u32[]{:S(2)}, u32[]{:S(2)}) %collective-permute-start.1) | collective-permute-done | bytes 1400864 | tf_op jit(solution)/shard_map/ppermute | solution.py:664
  142.3 17.8 %fourier.2 = (bf16[8,12,2,24,768]{4,3,2,1,0:T(8,128)(2,1)}, bf16[24,180,768]{2,1,0:T(8,128)(2,1)}) custom-call(s32[1]{0:T(128)} %bitcast.me_ref, bf16[192,180]{1,0:T(8,128)(2,1)S(1)} %copy-done.26, bf16[180,180]{1,0:T(8,128)(2,1)S(1)} %copy-done.8, f32[1,768]{1,0:T(1,128)S(1)} %slice.117.g_ref, f32[1,768]{1,0:T(1,128)S(1)} %compare_convert_fusion.cm_ref, ...), custom_call_target="tpu_custom_call" | custom-call | tf_op jit(solution)/shard_map/fourier/pallas_call | solution.py:282
  165.2 23.3 %collective-permute-start.3 = (bf16[6,29184]{1,0:T(8,128)(2,1)S(1)}, bf16[6,29184]{1,0:T(8,128)(2,1)}, u32[]{:S(2)}, u32[]{:S(2)}) collective-permute-start(bf16[6,29184]{1,0:T(8,128)(2,1)S(1)} %copy-done.39), channel_id=1, source_target_pairs={{0,1},{1,0},{2,3},{3,2},{4,5},{5,4},{6,7},{7,6},{8,9},{9,8},{10,11... | collective-permute-start | bytes 1050632 | tf_op jit(solution)/shard_map/ppermute | solution.py:664
  193.8 34.5 %collective-permute-done.3 = bf16[6,29184]{1,0:T(8,128)(2,1)} collective-permute-done((bf16[6,29184]{1,0:T(8,128)(2,1)S(1)}, bf16[6,29184]{1,0:T(8,128)(2,1)}, u32[]{:S(2)}, u32[]{:S(2)}) %collective-permute-start.3) | collective-permute-done | bytes 350240 | tf_op jit(solution)/shard_map/ppermute | solution.py:664
  230.3 11.5 collective-permute-done.4
  243.7 8.6 collective-permute-done.5
  260.7 33.9 %all-to-all-start.2 = ((bf16[32,36,768]{2,1,0:T(8,128)(2,1)}), bf16[32,36,768]{2,1,0:T(8,128)(2,1)S(1)}, u32[]{:S(2)}, u32[]{:S(2)}) async-start(bf16[32,36,768]{2,1,0:T(8,128)(2,1)} %copy-done.12), calls=%async_computation.2 | async-start | bytes 3932160 | tf_op jit(solution)/shard_map/all_to_all | solution.py:593
  296.8 10.5 analysis.2
  307.3 76.4 %all-to-all-done.2.x_ref = bf16[32,36,768]{2,1,0:T(8,128)(2,1)S(1)} async-done(((bf16[32,36,768]{2,1,0:T(8,128)(2,1)}), bf16[32,36,768]{2,1,0:T(8,128)(2,1)S(1)}, u32[]{:S(2)}, u32[]{:S(2)}) %all-to-all-start.2) | async-done | bytes 1769504 | tf_op jit(solution)/shard_map/all_to_all | solution.py:593
  403.8 70.7 %all-to-all-done.3.x_ref = bf16[8,576,768]{2,1,0:T(8,128)(2,1)} async-done(((bf16[8,576,768]{2,1,0:T(8,128)(2,1)}), bf16[8,576,768]{2,1,0:T(8,128)(2,1)}, u32[]{:S(2)}, u32[]{:S(2)}) %all-to-all-start.3) | async-done | bytes 7077920 | tf_op jit(solution)/shard_map/all_to_all | solution.py:593
  479.4 19.1 %mix_forward.2 = (bf16[8,576,768]{2,1,0:T(8,128)(2,1)}, bf16[12,384,768]{2,1,0:T(8,128)(2,1)}) custom-call(bf16[8,576,768]{2,1,0:T(8,128)(2,1)} %all-to-all-done.3.x_ref, bf16[4,12,168,768]{3,2,1,0:T(8,128)(2,1)} %bitcast.69), custom_call_target="tpu_custom_call" | custom-call | tf_op jit(solution)/shard_map/mix_forward/pallas_call | solution.py:363
  507.5 27.2 %all-gather.1 = bf16[4,96,768]{2,1,0:T(8,128)(2,1)} all-gather(bf16[4,24,768]{2,1,0:T(8,128)(2,1)S(1)} %copy.54), channel_id=3, replica_groups=mesh['sp'=8,'tp'=4] {'tp'}, dimensions={1}, use_global_device_ids=true | all-gather | bytes 737280 | tf_op jit(solution)/shard_map/all_gather | solution.py:699
  547.8 10.0 mix_forward.3
  557.8 19.7 %collective-permute-done.6 = bf16[24,29184]{1,0:T(8,128)(2,1)S(1)} collective-permute-done((bf16[24,29184]{1,0:T(8,128)(2,1)S(1)}, bf16[24,29184]{1,0:T(8,128)(2,1)S(1)}, u32[]{:S(2)}, u32[]{:S(2)}) %collective-permute-start.6) | collective-permute-done | bytes 1400864 | tf_op jit(solution)/shard_map/ppermute | solution.py:664
  578.6 28.4 %collective-permute-done.7 = bf16[24,29184]{1,0:T(8,128)(2,1)} collective-permute-done((bf16[24,29184]{1,0:T(8,128)(2,1)S(1)}, bf16[24,29184]{1,0:T(8,128)(2,1)}, u32[]{:S(2)}, u32[]{:S(2)}) %collective-permute-start.7) | collective-permute-done | bytes 1400864 | tf_op jit(solution)/shard_map/ppermute | solution.py:664
  615.1 10.5 synthesis.2
  625.5 8.9 all-to-all-done.6.x_ref
  653.1 30.1 %collective-permute-done.11 = bf16[6,29184]{1,0:T(8,128)(2,1)} collective-permute-done((bf16[6,29184]{1,0:T(8,128)(2,1)}, bf16[6,29184]{1,0:T(8,128)(2,1)}, u32[]{:S(2)}, u32[]{:S(2)}) %collective-permute-start.11) | collective-permute-done | bytes 350240 | tf_op jit(solution)/shard_map/ppermute | solution.py:664
  683.1 51.2 %collective-permute-done.12 = bf16[6,29184]{1,0:T(8,128)(2,1)} collective-permute-done((bf16[6,29184]{1,0:T(8,128)(2,1)}, bf16[6,29184]{1,0:T(8,128)(2,1)}, u32[]{:S(2)}, u32[]{:S(2)}) %collective-permute-start.12) | collective-permute-done | bytes 350240 | tf_op jit(solution)/shard_map/ppermute | solution.py:664
  738.3 9.9 all-to-all-start.8
  776.1 111.1 %grid_block.2 = (bf16[24,161,180]{2,1,0:T(8,128)(2,1)}, bf16[24,161,180]{2,1,0:T(8,128)(2,1)}, bf16[24,161,180]{2,1,0:T(8,128)(2,1)}, bf16[24,161,180]{2,1,0:T(8...) custom-call(s32[1]{0:T(128)} %bitcast.me_ref, ...), custom_call_target="tpu_custom_call" | custom-call | tf_op jit(solution)/shard_map/grid_block/pallas_call | solution.py:479
  923.4 32.8 %grid_block.3 = (bf16[6,161,180]{2,1,0:T(8,128)(2,1)}, bf16[6,161,180]{2,1,0:T(8,128)(2,1)}, bf16[6,161,180]{2,1,0:T(8,128)(2,1)}, bf16[6,161,180]{2,1,0:T(8,128...) custom-call(s32[1]{0:T(128)} %bitcast.me_ref, ...), custom_call_target="tpu_custom_call" | custom-call | tf_op jit(solution)/shard_map/grid_block/pallas_call | solution.py:479
  956.2 10.8 collective-permute-done.9.refs_1_
  976.5 10.5 synthesis_back.2
  987.0 34.0 %all-to-all-done.10.x_ref = bf16[32,36,768]{2,1,0:T(8,128)(2,1)} async-done(((bf16[32,36,768]{2,1,0:T(8,128)(2,1)}), bf16[32,36,768]{2,1,0:T(8,128)(2,1)}, u32[]{:S(2)}, u32[]{:S(2)}) %all-to-all-start.10) | async-done | bytes 1769504 | tf_op jit(solution)/shard_map/all_to_all | solution.py:593
  1025.9 8.8 fusion.5
  1036.8 5.8 copy.60
  1042.7 8.3 reshape.673
  1065.4 57.7 %collective-permute-done.14.refs_2_ = bf16[24,29184]{1,0:T(8,128)(2,1)S(1)} collective-permute-done((bf16[24,29184]{1,0:T(8,128)(2,1)}, bf16[24,29184]{1,0:T(8,128)(2,1)S(1)}, u32[]{:S(2)}, u32[]{:S(2)}) %collective-permute-start.14) | collective-permute-done | bytes 1400864 | tf_op jit(solution)/shard_map/ppermute | solution.py:664
  1133.2 19.3 %mix_backward.2 = (bf16[8,576,768]{2,1,0:T(8,128)(2,1)}, bf16[12,384,768]{2,1,0:T(8,128)(2,1)}) custom-call(bf16[8,576,768]{2,1,0:T(8,128)(2,1)} %all-to-all-done.11.x_ref, bf16[4,12,168,768]{3,2,1,0:T(8,128)(2,1)} %bitcast.71), custom_call_target="tpu_custom_call" | custom-call | tf_op jit(solution)/shard_map/mix_backward/pallas_call | solution.py:363
  1157.4 9.2 mix_backward.3
  1168.0 16.7 weight_grads.1
  1184.7 10.1 fusion.41
  1195.6 41.8 %all-to-all-done.13.x_ref = bf16[8,576,768]{2,1,0:T(8,128)(2,1)} async-done(((bf16[8,576,768]{2,1,0:T(8,128)(2,1)}), bf16[8,576,768]{2,1,0:T(8,128)(2,1)}, u32[]{:S(2)}, u32[]{:S(2)}) %all-to-all-start.13) | async-done | bytes 7077920 | tf_op jit(solution)/shard_map/all_to_all | solution.py:593
  1241.6 10.5 analysis_back.2
  1252.1 12.7 all-to-all-done.14.x_ref
  1274.2 30.6 %reduce-scatter.10.cloned.1.call-done = bf16[1,6,168,768]{3,2,1,0:T(8,128)(2,1)} async-done(((bf16[4,6,168,768]{3,2,1,0:T(8,128)(2,1)}), bf16[1,6,168,768]{3,2,1,0:T(8,128)(2,1)}) %reduce-scatter.10.cloned.1.call-update) | async-done | bytes 1548304 | tf_op jit(solution)/shard_map/reduce_scatter | solution.py:755
  1304.7 44.9 %all-to-all-done.15 = bf16[8,576,768]{2,1,0:T(8,128)(2,1)} async-done(((bf16[8,576,768]{2,1,0:T(8,128)(2,1)}), bf16[8,576,768]{2,1,0:T(8,128)(2,1)}, u32[]{:S(2)}, u32[]{:S(2)}) %all-to-all-start.15) | async-done | bytes 7077920 | tf_op jit(solution)/shard_map/all_to_all | solution.py:593
  1358.8 20.9 %grid_final.2 = (bf16[24,161,180]{2,1,0:T(8,128)(2,1)S(1)}, bf16[24,161,180]{2,1,0:T(8,128)(2,1)S(1)}, bf16[24,161,180]{2,1,0:T(8,128)(2,1)}, bf16[24,161,180]{2,1,0:T(8,128)(2,1)}, f32[1,768]{1,0:T(1,128)S(1)}) custom-call(s32[1]{0:T(128)} %bitcast.me_ref, bf16[8,2,288,768]{3,2,1,0:T(8,128)(2,1)} %bitcast.31.c_ref, ...), custom_call_target="tpu_custom_call" | custom-call | tf_op jit(solution)/shard_map/grid_final/pallas_call | solution.py:557
  1397.0 12.4 unpack_rows.2
  1426.0 50.3 %all-to-all-done.16 = bf16[32,36,768]{2,1,0:T(8,128)(2,1)} async-done(((bf16[32,36,768]{2,1,0:T(8,128)(2,1)}), bf16[32,36,768]{2,1,0:T(8,128)(2,1)}, u32[]{:S(2)}, u32[]{:S(2)}) %all-to-all-start.16) | async-done | bytes 1769504 | tf_op jit(solution)/shard_map/all_to_all | solution.py:593
  1476.2 88.4 %reduce-scatter.12.cloned.1.call-done = bf16[1,6,168,768]{3,2,1,0:T(8,128)(2,1)} async-done(((bf16[4,6,168,768]{3,2,1,0:T(8,128)(2,1)}), bf16[1,6,168,768]{3,2,1,0:T(8,128)(2,1)}) %reduce-scatter.12.cloned.1.call-update) | async-done | bytes 1548304 | tf_op jit(solution)/shard_map/reduce_scatter | solution.py:755
  1582.0 39.0 %collective-permute-start.22 = (bf16[6,29184]{1,0:T(8,128)(2,1)}, bf16[6,29184]{1,0:T(8,128)(2,1)S(1)}, u32[]{:S(2)}, u32[]{:S(2)}) collective-permute-start(bf16[6,29184]{1,0:T(8,128)(2,1)} %pad.73), channel_id=1, source_target_pairs={{0,2},{1,3},{2,0},{3,1},{4,6},{5,7},{6,4},{7,5},{8,10},{9,11},{10,... | collective-permute-start | bytes 1050632 | tf_op jit(solution)/shard_map/ppermute | solution.py:664
  1621.1 20.8 %fusion.38 = (bf16[12,192,768]{2,1,0:T(8,128)(2,1)}, f32[12,192,768]{2,1,0:T(8,128)}, f32[12,192,768]{2,1,0:T(8,128)}, f32[12,192,768]{2,1,0:T(8,128)}) fusion(f32[12,192,768]{2,1,0:T(8,128)} %param.23, bf16[6,168,768]{2,1,0:T(8,128)(2,1)} %bitcast.90, bf16[6,168,768]{2,1,0:T(8,128)(2,1)} %bitcast.89, f32[192,768]{1,0:T(8,128)} %get-tuple-element.255, ...), kind=kLoop, calls=%fused_computation.99 | loop fusion | flops 46006272 | bytes 51462192 | tf_op jit(solution)/shard_map/convert_element_type | solution.py:790
  1644.6 40.7 %psum.7 = f32[2,768]{1,0:T(2,128)S(1)} all-reduce(f32[2,768]{1,0:T(2,128)S(1)} %pad_maximum_fusion.2), channel_id=1, replica_groups=mesh['sp'=8,'tp'=4] {'sp','tp'}, use_global_device_ids=true, to_apply=%region_5.6 | all-reduce | flops 1536 | bytes 12288 | tf_op jit(solution)/shard_map/psum | solution.py:783
  1686.0 12.9 unpack_rows.3
  (332 shorter events, 345.7 us)
Async XLA Ops:
  15.6 458.9 %all-gather.10.cloned.1.call-start = ((), (), s32[]{:S(2)}) async-start(), calls=%async_computation.27 | async-start | bytes 15482880 | tf_op jit(solution)/shard_map/all_gather | solution.py:680
  28.1 61.4 %collective-permute-start = (bf16[24,29184]{1,0:T(8,128)(2,1)}, bf16[24,29184]{1,0:T(8,128)(2,1)}, u32[]{:S(2)}, u32[]{:S(2)}) collective-permute-start(bf16[24,29184]{1,0:T(8,128)(2,1)} %copy-done.33), channel_id=1, source_target_pairs={{0,1},{1,0},{2,3},{3,2},{4,5},{5,4},{6,7},{7,6},{8,9},{9,8},{10,11... | collective-permute-start | bytes 4202504 | tf_op jit(solution)/shard_map/ppermute | solution.py:664
  30.2 94.9 %collective-permute-start.1 = (bf16[24,29184]{1,0:T(8,128)(2,1)}, bf16[24,29184]{1,0:T(8,128)(2,1)}, u32[]{:S(2)}, u32[]{:S(2)}) collective-permute-start(bf16[24,29184]{1,0:T(8,128)(2,1)} %copy-done.32), channel_id=1, source_target_pairs={{0,2},{1,3},{2,0},{3,1},{4,6},{5,7},{6,4},{7,5},{8,10},{9,11},{10,... | collective-permute-start | bytes 4202504 | tf_op jit(solution)/shard_map/ppermute | solution.py:664
  32.5 98.2 %collective-permute-start.2 = (bf16[24,29184]{1,0:T(8,128)(2,1)S(1)}, bf16[24,29184]{1,0:T(8,128)(2,1)}, u32[]{:S(2)}, u32[]{:S(2)}) collective-permute-start(bf16[24,29184]{1,0:T(8,128)(2,1)S(1)} %get-tuple-element.129), channel_id=1, source_target_pairs={{0,3},{1,2},{2,1},{3,0},{4,7},{5,6},{6,5},{7,4},{8,11},{9,10},{10,... | collective-permute-start | bytes 4202504 | tf_op jit(solution)/shard_map/ppermute | solution.py:664
  160.1 100.6 %all-to-all-start.1 = ((bf16[8,576,768]{2,1,0:T(8,128)(2,1)}), bf16[8,576,768]{2,1,0:T(8,128)(2,1)}, u32[]{:S(2)}, u32[]{:S(2)}) async-start(bf16[8,576,768]{2,1,0:T(8,128)(2,1)} %bitcast.80), calls=%async_computation.1 | async-start | bytes 14155776 | tf_op jit(solution)/shard_map/all_to_all | solution.py:593
  165.2 63.1 %collective-permute-start.3 = (bf16[6,29184]{1,0:T(8,128)(2,1)S(1)}, bf16[6,29184]{1,0:T(8,128)(2,1)}, u32[]{:S(2)}, u32[]{:S(2)}) collective-permute-start(bf16[6,29184]{1,0:T(8,128)(2,1)S(1)} %copy-done.39), channel_id=1, source_target_pairs={{0,1},{1,0},{2,3},{3,2},{4,5},{5,4},{6,7},{7,6},{8,9},{9,8},{10,11... | collective-permute-start | bytes 1050632 | tf_op jit(solution)/shard_map/ppermute | solution.py:664
  188.5 53.3 %collective-permute-start.4 = (bf16[6,29184]{1,0:T(8,128)(2,1)S(1)}, bf16[6,29184]{1,0:T(8,128)(2,1)}, u32[]{:S(2)}, u32[]{:S(2)}) collective-permute-start(bf16[6,29184]{1,0:T(8,128)(2,1)S(1)} %copy-done.37), channel_id=1, source_target_pairs={{0,2},{1,3},{2,0},{3,1},{4,6},{5,7},{6,4},{7,5},{8,10},{9,11},{10,... | collective-permute-start | bytes 1050632 | tf_op jit(solution)/shard_map/ppermute | solution.py:664
  189.5 62.8 %collective-permute-start.5 = (bf16[6,29184]{1,0:T(8,128)(2,1)S(1)}, bf16[6,29184]{1,0:T(8,128)(2,1)}, u32[]{:S(2)}, u32[]{:S(2)}) collective-permute-start(bf16[6,29184]{1,0:T(8,128)(2,1)S(1)} %copy-done.35), channel_id=1, source_target_pairs={{0,3},{1,2},{2,1},{3,0},{4,7},{5,6},{6,5},{7,4},{8,11},{9,10},{10,... | collective-permute-start | bytes 1050632 | tf_op jit(solution)/shard_map/ppermute | solution.py:664
  260.7 123.0 %all-to-all-start.2 = ((bf16[32,36,768]{2,1,0:T(8,128)(2,1)}), bf16[32,36,768]{2,1,0:T(8,128)(2,1)S(1)}, u32[]{:S(2)}, u32[]{:S(2)}) async-start(bf16[32,36,768]{2,1,0:T(8,128)(2,1)} %copy-done.12), calls=%async_computation.2 | async-start | bytes 3932160 | tf_op jit(solution)/shard_map/all_to_all | solution.py:593
  384.9 89.6 %all-to-all-start.3 = ((bf16[8,576,768]{2,1,0:T(8,128)(2,1)}), bf16[8,576,768]{2,1,0:T(8,128)(2,1)}, u32[]{:S(2)}, u32[]{:S(2)}) async-start(bf16[8,576,768]{2,1,0:T(8,128)(2,1)} %analysis.2), calls=%async_computation.3 | async-start | bytes 14155776 | tf_op jit(solution)/shard_map/all_to_all | solution.py:593
  389.8 88.6 %reduce-scatter.16.cloned.1.call-start = ((), (), s32[]{:S(2)}) async-start(), calls=%async_computation.28 | async-start | bytes 1327104
  474.5 26.9 %all-to-all-start.4 = ((bf16[8,144,768]{2,1,0:T(8,128)(2,1)}), bf16[8,144,768]{2,1,0:T(8,128)(2,1)S(1)}, u32[]{:S(2)}, u32[]{:S(2)}) async-start(bf16[8,144,768]{2,1,0:T(8,128)(2,1)} %analysis.3), calls=%async_computation.4 | async-start | bytes 3538944 | tf_op jit(solution)/shard_map/all_to_all | solution.py:593
  502.6 104.4 %all-to-all-start.5 = ((bf16[8,576,768]{2,1,0:T(8,128)(2,1)}), bf16[8,576,768]{2,1,0:T(8,128)(2,1)}, u32[]{:S(2)}, u32[]{:S(2)}) async-start(bf16[8,576,768]{2,1,0:T(8,128)(2,1)} %get-tuple-element.148), calls=%async_computation.5 | async-start | bytes 14155776 | tf_op jit(solution)/shard_map/all_to_all | solution.py:593
  544.2 33.3 %collective-permute-start.6 = (bf16[24,29184]{1,0:T(8,128)(2,1)S(1)}, bf16[24,29184]{1,0:T(8,128)(2,1)S(1)}, u32[]{:S(2)}, u32[]{:S(2)}) collective-permute-start(bf16[24,29184]{1,0:T(8,128)(2,1)S(1)} %get-tuple-element.152), channel_id=1, source_target_pairs={{0,1},{1,0},{2,3},{3,2},{4,5},{5,4},{6,7},{7,6},{8,9},{9,8},{10,11... | collective-permute-start | bytes 4202504 | tf_op jit(solution)/shard_map/ppermute | solution.py:664
  545.8 61.2 %collective-permute-start.7 = (bf16[24,29184]{1,0:T(8,128)(2,1)S(1)}, bf16[24,29184]{1,0:T(8,128)(2,1)}, u32[]{:S(2)}, u32[]{:S(2)}) collective-permute-start(bf16[24,29184]{1,0:T(8,128)(2,1)S(1)} %get-tuple-element.154), channel_id=1, source_target_pairs={{0,3},{1,2},{2,1},{3,0},{4,7},{5,6},{6,5},{7,4},{8,11},{9,10},{10,... | collective-permute-start | bytes 4202504 | tf_op jit(solution)/shard_map/ppermute | solution.py:664
  607.0 27.5 %all-to-all-start.6 = ((bf16[8,144,768]{2,1,0:T(8,128)(2,1)}), bf16[8,144,768]{2,1,0:T(8,128)(2,1)}, u32[]{:S(2)}, u32[]{:S(2)}) async-start(bf16[8,144,768]{2,1,0:T(8,128)(2,1)} %get-tuple-element.157), calls=%async_computation.6 | async-start | bytes 3538944 | tf_op jit(solution)/shard_map/all_to_all | solution.py:593
  634.5 103.8 %all-to-all-start.7 = ((bf16[8,576,768]{2,1,0:T(8,128)(2,1)}), bf16[8,576,768]{2,1,0:T(8,128)(2,1)}, u32[]{:S(2)}, u32[]{:S(2)}) async-start(bf16[8,576,768]{2,1,0:T(8,128)(2,1)} %synthesis.2), calls=%async_computation.7 | async-start | bytes 14155776 | tf_op jit(solution)/shard_map/all_to_all | solution.py:593
  639.3 131.8 %all-gather.6.cloned.1.call-start = ((), (), s32[]{:S(2)}) async-start(), calls=%async_computation.22 | async-start | bytes 5308416 | tf_op jit(solution)/shard_map/all_gather | solution.py:708
  639.9 94.4 %collective-permute-start.8 = (bf16[24,29184]{1,0:T(8,128)(2,1)S(1)}, bf16[24,29184]{1,0:T(8,128)(2,1)}, u32[]{:S(2)}, u32[]{:S(2)}) collective-permute-start(bf16[24,29184]{1,0:T(8,128)(2,1)S(1)} %get-tuple-element.167), channel_id=1, source_target_pairs={{0,2},{1,3},{2,0},{3,1},{4,6},{5,7},{6,4},{7,5},{8,10},{9,11},{10,... | collective-permute-start | bytes 4202504 | tf_op jit(solution)/shard_map/ppermute | solution.py:664
  641.9 41.2 %collective-permute-start.11 = (bf16[6,29184]{1,0:T(8,128)(2,1)}, bf16[6,29184]{1,0:T(8,128)(2,1)}, u32[]{:S(2)}, u32[]{:S(2)}) collective-permute-start(bf16[6,29184]{1,0:T(8,128)(2,1)} %copy-done.42), channel_id=1, source_target_pairs={{0,1},{1,0},{2,3},{3,2},{4,5},{5,4},{6,7},{7,6},{8,9},{9,8},{10,11... | collective-permute-start | bytes 1050632 | tf_op jit(solution)/shard_map/ppermute | solution.py:664
  643.2 91.1 %collective-permute-start.12 = (bf16[6,29184]{1,0:T(8,128)(2,1)}, bf16[6,29184]{1,0:T(8,128)(2,1)}, u32[]{:S(2)}, u32[]{:S(2)}) collective-permute-start(bf16[6,29184]{1,0:T(8,128)(2,1)} %copy-done.41), channel_id=1, source_target_pairs={{0,2},{1,3},{2,0},{3,1},{4,6},{5,7},{6,4},{7,5},{8,10},{9,11},{10,... | collective-permute-start | bytes 1050632 | tf_op jit(solution)/shard_map/ppermute | solution.py:664
  643.7 90.6 %collective-permute-start.13 = (bf16[6,29184]{1,0:T(8,128)(2,1)}, bf16[6,29184]{1,0:T(8,128)(2,1)}, u32[]{:S(2)}, u32[]{:S(2)}) collective-permute-start(bf16[6,29184]{1,0:T(8,128)(2,1)} %copy-done.40), channel_id=1, source_target_pairs={{0,3},{1,2},{2,1},{3,0},{4,7},{5,6},{6,5},{7,4},{8,11},{9,10},{10,... | collective-permute-start | bytes 1050632 | tf_op jit(solution)/shard_map/ppermute | solution.py:664
  738.3 148.9 %all-to-all-start.8 = ((bf16[32,36,768]{2,1,0:T(8,128)(2,1)}), bf16[32,36,768]{2,1,0:T(8,128)(2,1)}, u32[]{:S(2)}, u32[]{:S(2)}) async-start(bf16[32,36,768]{2,1,0:T(8,128)(2,1)} %synthesis.3), calls=%async_computation.8 | async-start | bytes 3932160 | tf_op jit(solution)/shard_map/all_to_all | solution.py:593
  887.2 85.1 %all-to-all-start.9 = ((bf16[8,576,768]{2,1,0:T(8,128)(2,1)}), bf16[8,576,768]{2,1,0:T(8,128)(2,1)}, u32[]{:S(2)}, u32[]{:S(2)}) async-start(bf16[8,576,768]{2,1,0:T(8,128)(2,1)} %bitcast.79), calls=%async_computation.9 | async-start | bytes 14155776 | tf_op jit(solution)/shard_map/all_to_all | solution.py:593
  901.7 54.5 %collective-permute-start.10 = (bf16[24,29184]{1,0:T(8,128)(2,1)}, bf16[24,29184]{1,0:T(8,128)(2,1)}, u32[]{:S(2)}, u32[]{:S(2)}) collective-permute-start(bf16[24,29184]{1,0:T(8,128)(2,1)} %pad.60), channel_id=1, source_target_pairs={{0,3},{1,2},{2,1},{3,0},{4,7},{5,6},{6,5},{7,4},{8,11},{9,10},{10,... | collective-permute-start | bytes 4202504 | tf_op jit(solution)/shard_map/ppermute | solution.py:664
  905.2 61.7 %collective-permute-start.9 = (bf16[24,29184]{1,0:T(8,128)(2,1)}, bf16[24,29184]{1,0:T(8,128)(2,1)}, u32[]{:S(2)}, u32[]{:S(2)}) collective-permute-start(bf16[24,29184]{1,0:T(8,128)(2,1)} %pad.58), channel_id=1, source_target_pairs={{0,1},{1,0},{2,3},{3,2},{4,5},{5,4},{6,7},{7,6},{8,9},{9,8},{10,11... | collective-permute-start | bytes 4202504 | tf_op jit(solution)/shard_map/ppermute | solution.py:664
  972.3 48.7 %all-to-all-start.10 = ((bf16[32,36,768]{2,1,0:T(8,128)(2,1)}), bf16[32,36,768]{2,1,0:T(8,128)(2,1)}, u32[]{:S(2)}, u32[]{:S(2)}) async-start(bf16[32,36,768]{2,1,0:T(8,128)(2,1)} %get-tuple-element.194), calls=%async_computation.10 | async-start | bytes 3932160 | tf_op jit(solution)/shard_map/all_to_all | solution.py:593
  1021.0 103.2 %all-to-all-start.11 = ((bf16[8,576,768]{2,1,0:T(8,128)(2,1)}), bf16[8,576,768]{2,1,0:T(8,128)(2,1)}, u32[]{:S(2)}, u32[]{:S(2)}) async-start(bf16[8,576,768]{2,1,0:T(8,128)(2,1)} %synthesis_back.2), calls=%async_computation.11 | async-start | bytes 14155776 | tf_op jit(solution)/shard_map/all_to_all | solution.py:593
  1025.9 243.8 %reduce-scatter.18.cloned.1.call-start = ((), (), s32[]{:S(2)}) async-start(), calls=%async_computation.29 | async-start | bytes 5308416
  1058.7 64.4 %collective-permute-start.14 = (bf16[24,29184]{1,0:T(8,128)(2,1)}, bf16[24,29184]{1,0:T(8,128)(2,1)S(1)}, u32[]{:S(2)}, u32[]{:S(2)}) collective-permute-start(bf16[24,29184]{1,0:T(8,128)(2,1)} %pad.59), channel_id=1, source_target_pairs={{0,2},{1,3},{2,0},{3,1},{4,6},{5,7},{6,4},{7,5},{8,10},{9,11},{10,... | collective-permute-start | bytes 4202504 | tf_op jit(solution)/shard_map/ppermute | solution.py:664
  1124.2 28.3 %all-to-all-start.12 = ((bf16[8,144,768]{2,1,0:T(8,128)(2,1)}), bf16[8,144,768]{2,1,0:T(8,128)(2,1)}, u32[]{:S(2)}, u32[]{:S(2)}) async-start(bf16[8,144,768]{2,1,0:T(8,128)(2,1)} %synthesis_back.3), calls=%async_computation.12 | async-start | bytes 3538944 | tf_op jit(solution)/shard_map/all_to_all | solution.py:593
  1128.7 66.1 %collective-permute-start.15 = (bf16[6,29184]{1,0:T(8,128)(2,1)}, bf16[6,29184]{1,0:T(8,128)(2,1)S(1)}, u32[]{:S(2)}, u32[]{:S(2)}) collective-permute-start(bf16[6,29184]{1,0:T(8,128)(2,1)} %pad.62), channel_id=1, source_target_pairs={{0,1},{1,0},{2,3},{3,2},{4,5},{5,4},{6,7},{7,6},{8,9},{9,8},{10,11... | collective-permute-start | bytes 1050632 | tf_op jit(solution)/shard_map/ppermute | solution.py:664
  1128.8 66.0 %collective-permute-start.16 = (bf16[6,29184]{1,0:T(8,128)(2,1)}, bf16[6,29184]{1,0:T(8,128)(2,1)S(1)}, u32[]{:S(2)}, u32[]{:S(2)}) collective-permute-start(bf16[6,29184]{1,0:T(8,128)(2,1)} %pad.63), channel_id=1, source_target_pairs={{0,2},{1,3},{2,0},{3,1},{4,6},{5,7},{6,4},{7,5},{8,10},{9,11},{10,... | collective-permute-start | bytes 1050632 | tf_op jit(solution)/shard_map/ppermute | solution.py:664
  1132.0 62.8 %collective-permute-start.17 = (bf16[6,29184]{1,0:T(8,128)(2,1)}, bf16[6,29184]{1,0:T(8,128)(2,1)S(1)}, u32[]{:S(2)}, u32[]{:S(2)}) collective-permute-start(bf16[6,29184]{1,0:T(8,128)(2,1)} %pad.64), channel_id=1, source_target_pairs={{0,3},{1,2},{2,1},{3,0},{4,7},{5,6},{6,5},{7,4},{8,11},{9,10},{10,... | collective-permute-start | bytes 1050632 | tf_op jit(solution)/shard_map/ppermute | solution.py:664
  1152.5 84.9 %all-to-all-start.13 = ((bf16[8,576,768]{2,1,0:T(8,128)(2,1)}), bf16[8,576,768]{2,1,0:T(8,128)(2,1)}, u32[]{:S(2)}, u32[]{:S(2)}) async-start(bf16[8,576,768]{2,1,0:T(8,128)(2,1)} %get-tuple-element.198), calls=%async_computation.13 | async-start | bytes 14155776 | tf_op jit(solution)/shard_map/all_to_all | solution.py:593
  1157.3 147.4 %reduce-scatter.10.cloned.1.call-start = ((), (), s32[]{:S(2)}) async-start(), calls=%async_computation.23 | async-start | bytes 7741440 | tf_op jit(solution)/shard_map/reduce_scatter | solution.py:755
  1237.3 27.5 %all-to-all-start.14 = ((bf16[8,144,768]{2,1,0:T(8,128)(2,1)}), bf16[8,144,768]{2,1,0:T(8,128)(2,1)}, u32[]{:S(2)}, u32[]{:S(2)}) async-start(bf16[8,144,768]{2,1,0:T(8,128)(2,1)} %get-tuple-element.205), calls=%async_computation.14 | async-start | bytes 3538944 | tf_op jit(solution)/shard_map/all_to_all | solution.py:593
  1264.8 84.9 %all-to-all-start.15 = ((bf16[8,576,768]{2,1,0:T(8,128)(2,1)}), bf16[8,576,768]{2,1,0:T(8,128)(2,1)}, u32[]{:S(2)}, u32[]{:S(2)}) async-start(bf16[8,576,768]{2,1,0:T(8,128)(2,1)} %analysis_back.2), calls=%async_computation.15 | async-start | bytes 14155776 | tf_op jit(solution)/shard_map/all_to_all | solution.py:593
  1269.6 80.0 %reduce-scatter.14.cloned.1.call-start = ((), (), s32[]{:S(2)}) async-start(), calls=%async_computation.25 | async-start | bytes 737280 | tf_op jit(solution)/shard_map/reduce_scatter | solution.py:775
  1274.1 148.9 %all-gather.8.cloned.1.call-start = ((), (), s32[]{:S(2)}) async-start(), calls=%async_computation.26 | async-start | bytes 1327104 | tf_op jit(solution)/shard_map/all_gather | solution.py:776
  1349.7 215.0 %reduce-scatter.12.cloned.1.call-start = ((), (), s32[]{:S(2)}) async-start(), calls=%async_computation.24 | async-start | bytes 7741440 | tf_op jit(solution)/shard_map/reduce_scatter | solution.py:755
  1354.8 121.5 %all-to-all-start.16 = ((bf16[32,36,768]{2,1,0:T(8,128)(2,1)}), bf16[32,36,768]{2,1,0:T(8,128)(2,1)}, u32[]{:S(2)}, u32[]{:S(2)}) async-start(bf16[32,36,768]{2,1,0:T(8,128)(2,1)} %analysis_back.3), calls=%async_computation.17 | async-start | bytes 3932160 | tf_op jit(solution)/shard_map/all_to_all | solution.py:593
  1389.3 231.7 %collective-permute-start.20 = (bf16[24,29184]{1,0:T(8,128)(2,1)}, bf16[24,29184]{1,0:T(8,128)(2,1)}, u32[]{:S(2)}, u32[]{:S(2)}) collective-permute-start(bf16[24,29184]{1,0:T(8,128)(2,1)} %pad.70), channel_id=1, source_target_pairs={{0,3},{1,2},{2,1},{3,0},{4,7},{5,6},{6,5},{7,4},{8,11},{9,10},{10,... | collective-permute-start | bytes 4202504 | tf_op jit(solution)/shard_map/ppermute | solution.py:664
  1422.3 263.7 %collective-permute-start.19 = (bf16[24,29184]{1,0:T(8,128)(2,1)}, bf16[24,29184]{1,0:T(8,128)(2,1)}, u32[]{:S(2)}, u32[]{:S(2)}) collective-permute-start(bf16[24,29184]{1,0:T(8,128)(2,1)} %pad.69), channel_id=1, source_target_pairs={{0,2},{1,3},{2,0},{3,1},{4,6},{5,7},{6,4},{7,5},{8,10},{9,11},{10,... | collective-permute-start | bytes 4202504 | tf_op jit(solution)/shard_map/ppermute | solution.py:664
  1422.3 263.7 %collective-permute-start.18 = (bf16[24,29184]{1,0:T(8,128)(2,1)}, bf16[24,29184]{1,0:T(8,128)(2,1)}, u32[]{:S(2)}, u32[]{:S(2)}) collective-permute-start(bf16[24,29184]{1,0:T(8,128)(2,1)} %pad.68), channel_id=1, source_target_pairs={{0,1},{1,0},{2,3},{3,2},{4,5},{5,4},{6,7},{7,6},{8,9},{9,8},{10,11... | collective-permute-start | bytes 4202504 | tf_op jit(solution)/shard_map/ppermute | solution.py:664
  1581.3 104.7 %collective-permute-start.23 = (bf16[6,29184]{1,0:T(8,128)(2,1)}, bf16[6,29184]{1,0:T(8,128)(2,1)S(1)}, u32[]{:S(2)}, u32[]{:S(2)}) collective-permute-start(bf16[6,29184]{1,0:T(8,128)(2,1)} %pad.74), channel_id=1, source_target_pairs={{0,3},{1,2},{2,1},{3,0},{4,7},{5,6},{6,5},{7,4},{8,11},{9,10},{10,... | collective-permute-start | bytes 1050632 | tf_op jit(solution)/shard_map/ppermute | solution.py:664
  1582.0 104.0 %collective-permute-start.22 = (bf16[6,29184]{1,0:T(8,128)(2,1)}, bf16[6,29184]{1,0:T(8,128)(2,1)S(1)}, u32[]{:S(2)}, u32[]{:S(2)}) collective-permute-start(bf16[6,29184]{1,0:T(8,128)(2,1)} %pad.73), channel_id=1, source_target_pairs={{0,2},{1,3},{2,0},{3,1},{4,6},{5,7},{6,4},{7,5},{8,10},{9,11},{10,... | collective-permute-start | bytes 1050632 | tf_op jit(solution)/shard_map/ppermute | solution.py:664
  1621.0 65.0 %collective-permute-start.21 = (bf16[6,29184]{1,0:T(8,128)(2,1)}, bf16[6,29184]{1,0:T(8,128)(2,1)S(1)}, u32[]{:S(2)}, u32[]{:S(2)}) collective-permute-start(bf16[6,29184]{1,0:T(8,128)(2,1)} %pad.72), channel_id=1, source_target_pairs={{0,1},{1,0},{2,3},{3,2},{4,5},{5,4},{6,7},{7,6},{8,9},{9,8},{10,11... | collective-permute-start | bytes 1050632 | tf_op jit(solution)/shard_map/ppermute | solution.py:664
  (61 other events, 1715.9 us)
Sparse Core Ops, SparseCore 0:
  136.4 318.2 all-gather.9
  1353.5 211.1 reduce-scatter.11
Sparse Core Ops, SparseCore 1:
  398.4 69.1 reduce-scatter.15
  641.9 72.9 all-gather.5
  1051.1 76.6 reduce-scatter.17
  1194.9 109.7 reduce-scatter.9
  1307.0 22.4 reduce-scatter.13
  1349.8 23.9 all-gather.7

commit v4 on v3

--- a/solution.py
+++ b/solution.py
@@ -385,9 +385,9 @@
     )(coef, weights)
 
 
-def weight_grads(grads, coefs, n_tp, wrows):
+def weight_grads(grads, coefs, n_tp, wrows, first, own):
     n = len(grads)
-    own, _, cp = grads[0].shape
+    cp = grads[0].shape[2]
     csh = cp // n_tp
 
     def body(*refs):
@@ -401,7 +401,9 @@
     return pl.pallas_call(
         body,
         grid=(own,),
-        in_specs=[pl.BlockSpec((1,) + v.shape[1:], lambda q: (q, 0, 0)) for v in grads + coefs],
+        in_specs=[
+            pl.BlockSpec((1,) + v.shape[1:], lambda q: (q + first, 0, 0)) for v in grads + coefs
+        ],
         out_specs=pl.BlockSpec((n_tp, 1, wrows, cp), lambda q: (0, q, 0, 0)),
         out_shape=jax.ShapeDtypeStruct((n_tp, own, wrows, cp), BF),
         compiler_params=params(48),
@@ -710,11 +712,14 @@
     w_out = dense[2:].reshape(2 * cp, cp)
     main, left = after((ahead, left), mixed[0])
     main, left = even(main), send_all(left)
+    cots = [cut(ahead[d]) if d % 2 or d == 0 else cut(a) for d, a in enumerate(main)]
+    if n > 1:
+        mixed[1] = after(mixed[1], [c for d, c in enumerate(cots) if d % 2 or d == 0])
     synth = []
     for i, ck in enumerate(chunks):
         g = legendre(ck, mixed[i], table(ck, syn_j), ck.nd, True, "synthesis")
         synth.append(ck.grid_coef(swap_next(g, ck.axes, *((main, left) if i else ()))))
-    cot5 = [[cut(a) for a in main], [cut(a) for a in left]]
+    cot5 = [cots, [cut(a) for a in left]]
     outs, rest, dgs = [], [], []
     for i, ck in enumerate(chunks):
         o, r = grid_block(
@@ -745,17 +750,18 @@
         grad_q.append(g)
     pieces_out = [(0, main)] + ([(-1, left)] if left else [])
     result = unpack_rows(pieces_out, me, plan, flat, valid, lanes, tile)
-    dws = weight_grads(grad_q, coef_q, n_tp, CROWS)
-    das[0] = after(das[0], dws)
+    half = own // 2
+    dws_a = weight_grads(grad_q, coef_q, n_tp, CROWS, 0, half)
+    dws_b = weight_grads(grad_q, coef_q, n_tp, CROWS, half, own - half)
+    das[0] = after(das[0], dws_a, dws_b)
     dfs = []
     for ck, a in zip(chunks, das):
         g = legendre(ck, a, table(ck, ana_j), ck.nd, True, "analysis_back")
         dfs.append(swap_next(g, ck.axes))
-    half = own // 2
     scatter = lambda v: lax.psum_scatter(v, "tp", scatter_dimension=0, tiled=False)
-    spec_a = scatter(after(dws[:, :half], pieces_out))
+    spec_a = scatter(after(dws_a, pieces_out))
     dfs[0] = after(dfs[0], spec_a)
-    spec_b = scatter(after(dws[:, half:], spec_a))
+    spec_b = scatter(after(dws_b, spec_a))
     dfs[-1] = after(dfs[-1], spec_b)
     spec_g = jnp.concatenate([spec_a, spec_b], axis=0)
     pieces, gg_a = [], 0.0

time: 1720 us -> 1700 us (0.988)
    unnamed x124 -> x148, local copies, waits for them, and re-layouts: 56 us -> 61 us
  transfers between devices with their start and end apart: 49 -> 49, of which waited for: 24 -> 26; matrix products, arithmetic and copies ran while one was open for 12% -> 12% of each run, Pallas kernels for 20% -> 20%
where the time goes in v4:
time: 1700 us; the launch traced here: 1690 us
  waiting for transfers between devices  782 us (46%)
  Pallas kernels  358 us (21%)
  starting transfers between devices  209 us (12%)
  local copies, waits for them, and re-layouts  200 us (12%)
  blocking collectives  68 us (4%)
  other arithmetic  47.7 us (3%)
  between operations  20 us (1%)
    all_to_all x17, waiting for transfers between devices, swap(): return lax.all_to_all(value, axis, split_axis=0, concat_axis=0, tiled=True)  338 us
    ppermute x24, waiting for transfers between devices, local(): lax.ppermute(a, 'tp', [(i, i ^ d) for i in range(n_tp)])  315 us
    pallas_call x2, Pallas kernels, grid_block(): pl.pallas_call(body, grid=ck.grid, in_specs=[SMEM, ck.coef_spec(rows_s, c...  143 us
    reduce_scatter x2, waiting for transfers between devices, local(): lax.psum_scatter(v, 'tp', scatter_dimension=0, tiled=False)  127 us
    all_to_all x17, starting transfers between devices, swap(): return lax.all_to_all(value, axis, split_axis=0, concat_axis=0, tiled=True)  114 us
    ppermute x24, starting transfers between devices, local(): lax.ppermute(a, 'tp', [(i, i ^ d) for i in range(n_tp)])  94.7 us
    unnamed x148, local copies, waits for them, and re-layouts  61 us
    pallas_call x8, Pallas kernels, legendre(): pl.pallas_call(body, grid=(cp // tile,), in_specs=[pl.BlockSpec((n_src, r...  59.3 us
  transfers between devices with their start and end apart: 49, of which 26 were waited for; matrix products, arithmetic and copies ran while one was open for 12% of the time, Pallas kernels for 20%

profile of v4, /device:TPU:0, one launch (start us, length us, event | category | flops | bytes accessed | tf_op | source)
XLA Modules:
  0.0 1687.6 jit_solution(1932794907461500388)
XLA Ops:
  9.3 6.3 all-to-all-start
  48.0 41.5 %collective-permute-done = bf16[24,29184]{1,0:T(8,128)(2,1)} collective-permute-done((bf16[24,29184]{1,0:T(8,128)(2,1)}, bf16[24,29184]{1,0:T(8,128)(2,1)}, u32[]{:S(2)}, u32[]{:S(2)}) %collective-permute-start) | collective-permute-done | bytes 1400864 | tf_op jit(solution)/shard_map/ppermute | solution.py:666
  95.1 29.9 %collective-permute-done.1 = bf16[24,29184]{1,0:T(8,128)(2,1)} collective-permute-done((bf16[24,29184]{1,0:T(8,128)(2,1)}, bf16[24,29184]{1,0:T(8,128)(2,1)}, u32[]{:S(2)}, u32[]{:S(2)}) %collective-permute-start.1) | collective-permute-done | bytes 1400864 | tf_op jit(solution)/shard_map/ppermute | solution.py:666
  142.9 17.7 %fourier.2 = (bf16[8,12,2,24,768]{4,3,2,1,0:T(8,128)(2,1)}, bf16[24,180,768]{2,1,0:T(8,128)(2,1)}) custom-call(s32[1]{0:T(128)} %bitcast.me_ref, bf16[192,180]{1,0:T(8,128)(2,1)S(1)} %copy-done.35, bf16[180,180]{1,0:T(8,128)(2,1)S(1)} %copy-done.12, f32[1,768]{1,0:T(1,128)S(1)} %slice.111.g_ref, f32[1,768]{1,0:T(1,128)S(1)} %compare_convert_fusion.cm_ref, ...), custom_call_target="tpu_custom_call" | custom-call | tf_op jit(solution)/shard_map/fourier/pallas_call | solution.py:282
  165.8 23.2 %collective-permute-start.3 = (bf16[6,29184]{1,0:T(8,128)(2,1)S(1)}, bf16[6,29184]{1,0:T(8,128)(2,1)}, u32[]{:S(2)}, u32[]{:S(2)}) collective-permute-start(bf16[6,29184]{1,0:T(8,128)(2,1)S(1)} %copy-done.48), channel_id=1, source_target_pairs={{0,1},{1,0},{2,3},{3,2},{4,5},{5,4},{6,7},{7,6},{8,9},{9,8},{10,11... | collective-permute-start | bytes 1050632 | tf_op jit(solution)/shard_map/ppermute | solution.py:666
  194.4 34.5 %collective-permute-done.3 = bf16[6,29184]{1,0:T(8,128)(2,1)} collective-permute-done((bf16[6,29184]{1,0:T(8,128)(2,1)S(1)}, bf16[6,29184]{1,0:T(8,128)(2,1)}, u32[]{:S(2)}, u32[]{:S(2)}) %collective-permute-start.3) | collective-permute-done | bytes 350240 | tf_op jit(solution)/shard_map/ppermute | solution.py:666
  230.8 10.3 collective-permute-done.4
  243.1 9.8 collective-permute-done.5
  261.2 33.3 %all-to-all-start.2 = ((bf16[32,36,768]{2,1,0:T(8,128)(2,1)}), bf16[32,36,768]{2,1,0:T(8,128)(2,1)S(1)}, u32[]{:S(2)}, u32[]{:S(2)}) async-start(bf16[32,36,768]{2,1,0:T(8,128)(2,1)} %copy-done.16), calls=%async_computation.2 | async-start | bytes 3932160 | tf_op jit(solution)/shard_map/all_to_all | solution.py:595
  296.7 10.5 analysis.2
  307.2 76.4 %all-to-all-done.2.x_ref = bf16[32,36,768]{2,1,0:T(8,128)(2,1)S(1)} async-done(((bf16[32,36,768]{2,1,0:T(8,128)(2,1)}), bf16[32,36,768]{2,1,0:T(8,128)(2,1)S(1)}, u32[]{:S(2)}, u32[]{:S(2)}) %all-to-all-start.2) | async-done | bytes 1769504 | tf_op jit(solution)/shard_map/all_to_all | solution.py:595
  403.6 70.9 %all-to-all-done.3.x_ref = bf16[8,576,768]{2,1,0:T(8,128)(2,1)} async-done(((bf16[8,576,768]{2,1,0:T(8,128)(2,1)}), bf16[8,576,768]{2,1,0:T(8,128)(2,1)}, u32[]{:S(2)}, u32[]{:S(2)}) %all-to-all-start.3) | async-done | bytes 7077920 | tf_op jit(solution)/shard_map/all_to_all | solution.py:595
  479.6 19.1 %mix_forward.2 = (bf16[8,576,768]{2,1,0:T(8,128)(2,1)}, bf16[12,384,768]{2,1,0:T(8,128)(2,1)}) custom-call(bf16[8,576,768]{2,1,0:T(8,128)(2,1)} %all-to-all-done.3.x_ref, bf16[4,12,168,768]{3,2,1,0:T(8,128)(2,1)} %bitcast.69), custom_call_target="tpu_custom_call" | custom-call | tf_op jit(solution)/shard_map/mix_forward/pallas_call | solution.py:363
  507.6 27.2 %all-gather.1 = bf16[4,96,768]{2,1,0:T(8,128)(2,1)} all-gather(bf16[4,24,768]{2,1,0:T(8,128)(2,1)S(1)} %copy.54), channel_id=3, replica_groups=mesh['sp'=8,'tp'=4] {'tp'}, dimensions={1}, use_global_device_ids=true | all-gather | bytes 737280 | tf_op jit(solution)/shard_map/all_gather | solution.py:701
  548.0 10.0 mix_forward.3
  558.0 19.7 %collective-permute-done.6 = bf16[24,29184]{1,0:T(8,128)(2,1)S(1)} collective-permute-done((bf16[24,29184]{1,0:T(8,128)(2,1)S(1)}, bf16[24,29184]{1,0:T(8,128)(2,1)S(1)}, u32[]{:S(2)}, u32[]{:S(2)}) %collective-permute-start.6) | collective-permute-done | bytes 1400864 | tf_op jit(solution)/shard_map/ppermute | solution.py:666
  578.8 28.4 %collective-permute-done.7 = bf16[24,29184]{1,0:T(8,128)(2,1)} collective-permute-done((bf16[24,29184]{1,0:T(8,128)(2,1)S(1)}, bf16[24,29184]{1,0:T(8,128)(2,1)}, u32[]{:S(2)}, u32[]{:S(2)}) %collective-permute-start.7) | collective-permute-done | bytes 1400864 | tf_op jit(solution)/shard_map/ppermute | solution.py:666
  615.2 10.5 synthesis.2
  625.7 8.9 all-to-all-done.6.x_ref
  669.5 13.8 collective-permute-done.11
  683.3 51.2 %collective-permute-done.12 = bf16[6,29184]{1,0:T(8,128)(2,1)} collective-permute-done((bf16[6,29184]{1,0:T(8,128)(2,1)}, bf16[6,29184]{1,0:T(8,128)(2,1)}, u32[]{:S(2)}, u32[]{:S(2)}) %collective-permute-start.12) | collective-permute-done | bytes 350240 | tf_op jit(solution)/shard_map/ppermute | solution.py:666
  738.4 10.1 all-to-all-start.8
  761.2 110.7 %grid_block.2 = (bf16[24,161,180]{2,1,0:T(8,128)(2,1)}, bf16[24,161,180]{2,1,0:T(8,128)(2,1)}, bf16[24,161,180]{2,1,0:T(8,128)(2,1)}, bf16[24,161,180]{2,1,0:T(8...) custom-call(s32[1]{0:T(128)} %bitcast.me_ref, ...), custom_call_target="tpu_custom_call" | custom-call | tf_op jit(solution)/shard_map/grid_block/pallas_call | solution.py:481
  911.0 32.7 %grid_block.3 = (bf16[6,161,180]{2,1,0:T(8,128)(2,1)}, bf16[6,161,180]{2,1,0:T(8,128)(2,1)}, bf16[6,161,180]{2,1,0:T(8,128)(2,1)}, bf16[6,161,180]{2,1,0:T(8,128...) custom-call(s32[1]{0:T(128)} %bitcast.me_ref, ...), custom_call_target="tpu_custom_call" | custom-call | tf_op jit(solution)/shard_map/grid_block/pallas_call | solution.py:481
  943.7 7.7 collective-permute-done.9.refs_1_
  961.3 10.5 synthesis_back.2
  971.7 34.0 %all-to-all-done.10.x_ref = bf16[32,36,768]{2,1,0:T(8,128)(2,1)} async-done(((bf16[32,36,768]{2,1,0:T(8,128)(2,1)}), bf16[32,36,768]{2,1,0:T(8,128)(2,1)}, u32[]{:S(2)}, u32[]{:S(2)}) %all-to-all-start.10) | async-done | bytes 1769504 | tf_op jit(solution)/shard_map/all_to_all | solution.py:595
  1010.6 7.4 fusion.5
  1018.5 5.8 copy.60
  1024.4 8.2 reshape.673
  1046.9 57.4 %collective-permute-done.14.refs_2_ = bf16[24,29184]{1,0:T(8,128)(2,1)S(1)} collective-permute-done((bf16[24,29184]{1,0:T(8,128)(2,1)S(1)}, bf16[24,29184]{1,0:T(8,128)(2,1)S(1)}, u32[]{:S(2)}, u32[]{:S(2)}) %collective-permute-start.14) | collective-permute-done | bytes 1400864 | tf_op jit(solution)/shard_map/ppermute | solution.py:666
  1109.5 19.4 %mix_backward.2 = (bf16[8,576,768]{2,1,0:T(8,128)(2,1)}, bf16[12,384,768]{2,1,0:T(8,128)(2,1)}) custom-call(bf16[8,576,768]{2,1,0:T(8,128)(2,1)} %all-to-all-done.11.x_ref, bf16[4,12,168,768]{3,2,1,0:T(8,128)(2,1)} %bitcast.71), custom_call_target="tpu_custom_call" | custom-call | tf_op jit(solution)/shard_map/mix_backward/pallas_call | solution.py:363
  1143.2 9.1 mix_backward.3
  1153.8 9.0 weight_grads.2
  1163.5 11.0 collective-permute-done.16.refs_6_
  1176.1 42.6 %all-to-all-done.13.x_ref = bf16[8,576,768]{2,1,0:T(8,128)(2,1)} async-done(((bf16[8,576,768]{2,1,0:T(8,128)(2,1)}), bf16[8,576,768]{2,1,0:T(8,128)(2,1)}, u32[]{:S(2)}, u32[]{:S(2)}) %all-to-all-start.13) | async-done | bytes 7077920 | tf_op jit(solution)/shard_map/all_to_all | solution.py:595
  1223.1 9.1 weight_grads.3
  1232.2 10.6 analysis_back.2
  1253.7 39.0 %reduce-scatter.10.cloned.1.call-done = bf16[1,6,168,768]{3,2,1,0:T(8,128)(2,1)} async-done(((bf16[4,6,168,768]{3,2,1,0:T(8,128)(2,1)}), bf16[1,6,168,768]{3,2,1,0:T(8,128)(2,1)}) %reduce-scatter.10.cloned.1.call-update) | async-done | bytes 1548304 | tf_op jit(solution)/shard_map/reduce_scatter | solution.py:761
  1292.8 38.3 %all-to-all-done.15 = bf16[8,576,768]{2,1,0:T(8,128)(2,1)} async-done(((bf16[8,576,768]{2,1,0:T(8,128)(2,1)}), bf16[8,576,768]{2,1,0:T(8,128)(2,1)}, u32[]{:S(2)}, u32[]{:S(2)}) %all-to-all-start.15) | async-done | bytes 7077920 | tf_op jit(solution)/shard_map/all_to_all | solution.py:595
  1340.1 20.7 %grid_final.2 = (bf16[24,161,180]{2,1,0:T(8,128)(2,1)S(1)}, bf16[24,161,180]{2,1,0:T(8,128)(2,1)S(1)}, bf16[24,161,180]{2,1,0:T(8,128)(2,1)}, bf16[24,161,180]{2,1,0:T(8,128)(2,1)}, f32[1,768]{1,0:T(1,128)S(1)}) custom-call(s32[1]{0:T(128)} %bitcast.me_ref, bf16[8,2,288,768]{3,2,1,0:T(8,128)(2,1)} %bitcast.31.c_ref, ...), custom_call_target="tpu_custom_call" | custom-call | tf_op jit(solution)/shard_map/grid_final/pallas_call | solution.py:559
  1381.3 11.7 unpack_rows.2
  1409.6 47.8 %all-to-all-done.16 = bf16[32,36,768]{2,1,0:T(8,128)(2,1)} async-done(((bf16[32,36,768]{2,1,0:T(8,128)(2,1)}), bf16[32,36,768]{2,1,0:T(8,128)(2,1)}, u32[]{:S(2)}, u32[]{:S(2)}) %all-to-all-start.16) | async-done | bytes 1769504 | tf_op jit(solution)/shard_map/all_to_all | solution.py:595
  1457.3 88.4 %reduce-scatter.12.cloned.1.call-done = bf16[1,6,168,768]{3,2,1,0:T(8,128)(2,1)} async-done(((bf16[4,6,168,768]{3,2,1,0:T(8,128)(2,1)}), bf16[1,6,168,768]{3,2,1,0:T(8,128)(2,1)}) %reduce-scatter.12.cloned.1.call-update) | async-done | bytes 1548304 | tf_op jit(solution)/shard_map/reduce_scatter | solution.py:761
  1562.9 39.1 %collective-permute-start.22 = (bf16[6,29184]{1,0:T(8,128)(2,1)}, bf16[6,29184]{1,0:T(8,128)(2,1)S(1)}, u32[]{:S(2)}, u32[]{:S(2)}) collective-permute-start(bf16[6,29184]{1,0:T(8,128)(2,1)} %pad.73), channel_id=1, source_target_pairs={{0,2},{1,3},{2,0},{3,1},{4,6},{5,7},{6,4},{7,5},{8,10},{9,11},{10,... | collective-permute-start | bytes 1050632 | tf_op jit(solution)/shard_map/ppermute | solution.py:666
  1602.0 20.8 %fusion.38 = (bf16[12,192,768]{2,1,0:T(8,128)(2,1)}, f32[12,192,768]{2,1,0:T(8,128)}, f32[12,192,768]{2,1,0:T(8,128)}, f32[12,192,768]{2,1,0:T(8,128)}) fusion(f32[12,192,768]{2,1,0:T(8,128)} %param.23, bf16[6,168,768]{2,1,0:T(8,128)(2,1)} %bitcast.90, bf16[6,168,768]{2,1,0:T(8,128)(2,1)} %bitcast.89, f32[192,768]{1,0:T(8,128)} %get-tuple-element.249, ...), kind=kLoop, calls=%fused_computation.99 | loop fusion | flops 46006272 | bytes 51462192 | tf_op jit(solution)/shard_map/convert_element_type | solution.py:796
  1625.5 40.8 %psum.7 = f32[2,768]{1,0:T(2,128)S(1)} all-reduce(f32[2,768]{1,0:T(2,128)S(1)} %pad_maximum_fusion.2), channel_id=1, replica_groups=mesh['sp'=8,'tp'=4] {'sp','tp'}, use_global_device_ids=true, to_apply=%region_5.6 | all-reduce | flops 1536 | bytes 12288 | tf_op jit(solution)/shard_map/psum | solution.py:789
  1667.0 12.9 unpack_rows.3
  (356 shorter events, 359.7 us)
Async XLA Ops:
  15.6 458.9 %all-gather.10.cloned.1.call-start = ((), (), s32[]{:S(2)}) async-start(), calls=%async_computation.27 | async-start | bytes 15482880 | tf_op jit(solution)/shard_map/all_gather | solution.py:682
  28.1 61.4 %collective-permute-start = (bf16[24,29184]{1,0:T(8,128)(2,1)}, bf16[24,29184]{1,0:T(8,128)(2,1)}, u32[]{:S(2)}, u32[]{:S(2)}) collective-permute-start(bf16[24,29184]{1,0:T(8,128)(2,1)} %copy-done.42), channel_id=1, source_target_pairs={{0,1},{1,0},{2,3},{3,2},{4,5},{5,4},{6,7},{7,6},{8,9},{9,8},{10,11... | collective-permute-start | bytes 4202504 | tf_op jit(solution)/shard_map/ppermute | solution.py:666
  30.1 94.9 %collective-permute-start.1 = (bf16[24,29184]{1,0:T(8,128)(2,1)}, bf16[24,29184]{1,0:T(8,128)(2,1)}, u32[]{:S(2)}, u32[]{:S(2)}) collective-permute-start(bf16[24,29184]{1,0:T(8,128)(2,1)} %copy-done.41), channel_id=1, source_target_pairs={{0,2},{1,3},{2,0},{3,1},{4,6},{5,7},{6,4},{7,5},{8,10},{9,11},{10,... | collective-permute-start | bytes 4202504 | tf_op jit(solution)/shard_map/ppermute | solution.py:666
  32.5 98.2 %collective-permute-start.2 = (bf16[24,29184]{1,0:T(8,128)(2,1)S(1)}, bf16[24,29184]{1,0:T(8,128)(2,1)}, u32[]{:S(2)}, u32[]{:S(2)}) collective-permute-start(bf16[24,29184]{1,0:T(8,128)(2,1)S(1)} %get-tuple-element.127), channel_id=1, source_target_pairs={{0,3},{1,2},{2,1},{3,0},{4,7},{5,6},{6,5},{7,4},{8,11},{9,10},{10,... | collective-permute-start | bytes 4202504 | tf_op jit(solution)/shard_map/ppermute | solution.py:666
  160.6 100.6 %all-to-all-start.1 = ((bf16[8,576,768]{2,1,0:T(8,128)(2,1)}), bf16[8,576,768]{2,1,0:T(8,128)(2,1)}, u32[]{:S(2)}, u32[]{:S(2)}) async-start(bf16[8,576,768]{2,1,0:T(8,128)(2,1)} %bitcast.80), calls=%async_computation.1 | async-start | bytes 14155776 | tf_op jit(solution)/shard_map/all_to_all | solution.py:595
  165.8 63.0 %collective-permute-start.3 = (bf16[6,29184]{1,0:T(8,128)(2,1)S(1)}, bf16[6,29184]{1,0:T(8,128)(2,1)}, u32[]{:S(2)}, u32[]{:S(2)}) collective-permute-start(bf16[6,29184]{1,0:T(8,128)(2,1)S(1)} %copy-done.48), channel_id=1, source_target_pairs={{0,1},{1,0},{2,3},{3,2},{4,5},{5,4},{6,7},{7,6},{8,9},{9,8},{10,11... | collective-permute-start | bytes 1050632 | tf_op jit(solution)/shard_map/ppermute | solution.py:666
  189.1 52.1 %collective-permute-start.4 = (bf16[6,29184]{1,0:T(8,128)(2,1)S(1)}, bf16[6,29184]{1,0:T(8,128)(2,1)}, u32[]{:S(2)}, u32[]{:S(2)}) collective-permute-start(bf16[6,29184]{1,0:T(8,128)(2,1)S(1)} %copy-done.46), channel_id=1, source_target_pairs={{0,2},{1,3},{2,0},{3,1},{4,6},{5,7},{6,4},{7,5},{8,10},{9,11},{10,... | collective-permute-start | bytes 1050632 | tf_op jit(solution)/shard_map/ppermute | solution.py:666
  190.0 62.8 %collective-permute-start.5 = (bf16[6,29184]{1,0:T(8,128)(2,1)S(1)}, bf16[6,29184]{1,0:T(8,128)(2,1)}, u32[]{:S(2)}, u32[]{:S(2)}) collective-permute-start(bf16[6,29184]{1,0:T(8,128)(2,1)S(1)} %copy-done.44), channel_id=1, source_target_pairs={{0,3},{1,2},{2,1},{3,0},{4,7},{5,6},{6,5},{7,4},{8,11},{9,10},{10,... | collective-permute-start | bytes 1050632 | tf_op jit(solution)/shard_map/ppermute | solution.py:666
  261.2 122.4 %all-to-all-start.2 = ((bf16[32,36,768]{2,1,0:T(8,128)(2,1)}), bf16[32,36,768]{2,1,0:T(8,128)(2,1)S(1)}, u32[]{:S(2)}, u32[]{:S(2)}) async-start(bf16[32,36,768]{2,1,0:T(8,128)(2,1)} %copy-done.16), calls=%async_computation.2 | async-start | bytes 3932160 | tf_op jit(solution)/shard_map/all_to_all | solution.py:595
  384.9 89.6 %all-to-all-start.3 = ((bf16[8,576,768]{2,1,0:T(8,128)(2,1)}), bf16[8,576,768]{2,1,0:T(8,128)(2,1)}, u32[]{:S(2)}, u32[]{:S(2)}) async-start(bf16[8,576,768]{2,1,0:T(8,128)(2,1)} %analysis.2), calls=%async_computation.3 | async-start | bytes 14155776 | tf_op jit(solution)/shard_map/all_to_all | solution.py:595
  389.7 88.8 %reduce-scatter.16.cloned.1.call-start = ((), (), s32[]{:S(2)}) async-start(), calls=%async_computation.28 | async-start | bytes 1327104
  474.5 27.1 %all-to-all-start.4 = ((bf16[8,144,768]{2,1,0:T(8,128)(2,1)}), bf16[8,144,768]{2,1,0:T(8,128)(2,1)S(1)}, u32[]{:S(2)}, u32[]{:S(2)}) async-start(bf16[8,144,768]{2,1,0:T(8,128)(2,1)} %analysis.3), calls=%async_computation.4 | async-start | bytes 3538944 | tf_op jit(solution)/shard_map/all_to_all | solution.py:595
  502.8 104.4 %all-to-all-start.5 = ((bf16[8,576,768]{2,1,0:T(8,128)(2,1)}), bf16[8,576,768]{2,1,0:T(8,128)(2,1)}, u32[]{:S(2)}, u32[]{:S(2)}) async-start(bf16[8,576,768]{2,1,0:T(8,128)(2,1)} %get-tuple-element.146), calls=%async_computation.5 | async-start | bytes 14155776 | tf_op jit(solution)/shard_map/all_to_all | solution.py:595
  544.4 33.3 %collective-permute-start.6 = (bf16[24,29184]{1,0:T(8,128)(2,1)S(1)}, bf16[24,29184]{1,0:T(8,128)(2,1)S(1)}, u32[]{:S(2)}, u32[]{:S(2)}) collective-permute-start(bf16[24,29184]{1,0:T(8,128)(2,1)S(1)} %get-tuple-element.150), channel_id=1, source_target_pairs={{0,1},{1,0},{2,3},{3,2},{4,5},{5,4},{6,7},{7,6},{8,9},{9,8},{10,11... | collective-permute-start | bytes 4202504 | tf_op jit(solution)/shard_map/ppermute | solution.py:666
  546.0 61.2 %collective-permute-start.7 = (bf16[24,29184]{1,0:T(8,128)(2,1)S(1)}, bf16[24,29184]{1,0:T(8,128)(2,1)}, u32[]{:S(2)}, u32[]{:S(2)}) collective-permute-start(bf16[24,29184]{1,0:T(8,128)(2,1)S(1)} %get-tuple-element.152), channel_id=1, source_target_pairs={{0,3},{1,2},{2,1},{3,0},{4,7},{5,6},{6,5},{7,4},{8,11},{9,10},{10,... | collective-permute-start | bytes 4202504 | tf_op jit(solution)/shard_map/ppermute | solution.py:666
  607.2 27.5 %all-to-all-start.6 = ((bf16[8,144,768]{2,1,0:T(8,128)(2,1)}), bf16[8,144,768]{2,1,0:T(8,128)(2,1)}, u32[]{:S(2)}, u32[]{:S(2)}) async-start(bf16[8,144,768]{2,1,0:T(8,128)(2,1)} %get-tuple-element.155), calls=%async_computation.6 | async-start | bytes 3538944 | tf_op jit(solution)/shard_map/all_to_all | solution.py:595
  634.6 103.8 %all-to-all-start.7 = ((bf16[8,576,768]{2,1,0:T(8,128)(2,1)}), bf16[8,576,768]{2,1,0:T(8,128)(2,1)}, u32[]{:S(2)}, u32[]{:S(2)}) async-start(bf16[8,576,768]{2,1,0:T(8,128)(2,1)} %synthesis.2), calls=%async_computation.7 | async-start | bytes 14155776 | tf_op jit(solution)/shard_map/all_to_all | solution.py:595
  639.5 116.8 %all-gather.6.cloned.1.call-start = ((), (), s32[]{:S(2)}) async-start(), calls=%async_computation.22 | async-start | bytes 5308416 | tf_op jit(solution)/shard_map/all_gather | solution.py:710
  640.1 94.4 %collective-permute-start.8 = (bf16[24,29184]{1,0:T(8,128)(2,1)S(1)}, bf16[24,29184]{1,0:T(8,128)(2,1)}, u32[]{:S(2)}, u32[]{:S(2)}) collective-permute-start(bf16[24,29184]{1,0:T(8,128)(2,1)S(1)} %get-tuple-element.163), channel_id=1, source_target_pairs={{0,2},{1,3},{2,0},{3,1},{4,6},{5,7},{6,4},{7,5},{8,10},{9,11},{10,... | collective-permute-start | bytes 4202504 | tf_op jit(solution)/shard_map/ppermute | solution.py:666
  642.0 41.2 %collective-permute-start.11 = (bf16[6,29184]{1,0:T(8,128)(2,1)}, bf16[6,29184]{1,0:T(8,128)(2,1)}, u32[]{:S(2)}, u32[]{:S(2)}) collective-permute-start(bf16[6,29184]{1,0:T(8,128)(2,1)} %copy-done.51), channel_id=1, source_target_pairs={{0,1},{1,0},{2,3},{3,2},{4,5},{5,4},{6,7},{7,6},{8,9},{9,8},{10,11... | collective-permute-start | bytes 1050632 | tf_op jit(solution)/shard_map/ppermute | solution.py:666
  643.3 91.1 %collective-permute-start.12 = (bf16[6,29184]{1,0:T(8,128)(2,1)}, bf16[6,29184]{1,0:T(8,128)(2,1)}, u32[]{:S(2)}, u32[]{:S(2)}) collective-permute-start(bf16[6,29184]{1,0:T(8,128)(2,1)} %copy-done.50), channel_id=1, source_target_pairs={{0,2},{1,3},{2,0},{3,1},{4,6},{5,7},{6,4},{7,5},{8,10},{9,11},{10,... | collective-permute-start | bytes 1050632 | tf_op jit(solution)/shard_map/ppermute | solution.py:666
  643.8 90.6 %collective-permute-start.13 = (bf16[6,29184]{1,0:T(8,128)(2,1)}, bf16[6,29184]{1,0:T(8,128)(2,1)}, u32[]{:S(2)}, u32[]{:S(2)}) collective-permute-start(bf16[6,29184]{1,0:T(8,128)(2,1)} %copy-done.49), channel_id=1, source_target_pairs={{0,3},{1,2},{2,1},{3,0},{4,7},{5,6},{6,5},{7,4},{8,11},{9,10},{10,... | collective-permute-start | bytes 1050632 | tf_op jit(solution)/shard_map/ppermute | solution.py:666
  738.4 133.5 %all-to-all-start.8 = ((bf16[32,36,768]{2,1,0:T(8,128)(2,1)}), bf16[32,36,768]{2,1,0:T(8,128)(2,1)}, u32[]{:S(2)}, u32[]{:S(2)}) async-start(bf16[32,36,768]{2,1,0:T(8,128)(2,1)} %synthesis.3), calls=%async_computation.8 | async-start | bytes 3932160 | tf_op jit(solution)/shard_map/all_to_all | solution.py:595
  871.9 84.9 %all-to-all-start.9 = ((bf16[8,576,768]{2,1,0:T(8,128)(2,1)}), bf16[8,576,768]{2,1,0:T(8,128)(2,1)}, u32[]{:S(2)}, u32[]{:S(2)}) async-start(bf16[8,576,768]{2,1,0:T(8,128)(2,1)} %bitcast.79), calls=%async_computation.9 | async-start | bytes 14155776 | tf_op jit(solution)/shard_map/all_to_all | solution.py:595
  886.1 57.6 %collective-permute-start.10 = (bf16[24,29184]{1,0:T(8,128)(2,1)}, bf16[24,29184]{1,0:T(8,128)(2,1)}, u32[]{:S(2)}, u32[]{:S(2)}) collective-permute-start(bf16[24,29184]{1,0:T(8,128)(2,1)} %pad.60), channel_id=1, source_target_pairs={{0,3},{1,2},{2,1},{3,0},{4,7},{5,6},{6,5},{7,4},{8,11},{9,10},{10,... | collective-permute-start | bytes 4202504 | tf_op jit(solution)/shard_map/ppermute | solution.py:666
  889.9 61.6 %collective-permute-start.9 = (bf16[24,29184]{1,0:T(8,128)(2,1)}, bf16[24,29184]{1,0:T(8,128)(2,1)S(1)}, u32[]{:S(2)}, u32[]{:S(2)}) collective-permute-start(bf16[24,29184]{1,0:T(8,128)(2,1)} %pad.58), channel_id=1, source_target_pairs={{0,1},{1,0},{2,3},{3,2},{4,5},{5,4},{6,7},{7,6},{8,9},{9,8},{10,11... | collective-permute-start | bytes 4202504 | tf_op jit(solution)/shard_map/ppermute | solution.py:666
  956.8 48.9 %all-to-all-start.10 = ((bf16[32,36,768]{2,1,0:T(8,128)(2,1)}), bf16[32,36,768]{2,1,0:T(8,128)(2,1)}, u32[]{:S(2)}, u32[]{:S(2)}) async-start(bf16[32,36,768]{2,1,0:T(8,128)(2,1)} %get-tuple-element.190), calls=%async_computation.10 | async-start | bytes 3932160 | tf_op jit(solution)/shard_map/all_to_all | solution.py:595
  1005.7 99.7 %all-to-all-start.11 = ((bf16[8,576,768]{2,1,0:T(8,128)(2,1)}), bf16[8,576,768]{2,1,0:T(8,128)(2,1)}, u32[]{:S(2)}, u32[]{:S(2)}) async-start(bf16[8,576,768]{2,1,0:T(8,128)(2,1)} %synthesis_back.2), calls=%async_computation.11 | async-start | bytes 14155776 | tf_op jit(solution)/shard_map/all_to_all | solution.py:595
  1010.6 240.6 %reduce-scatter.18.cloned.1.call-start = ((), (), s32[]{:S(2)}) async-start(), calls=%async_computation.29 | async-start | bytes 5308416
  1040.1 64.2 %collective-permute-start.14 = (bf16[24,29184]{1,0:T(8,128)(2,1)S(1)}, bf16[24,29184]{1,0:T(8,128)(2,1)S(1)}, u32[]{:S(2)}, u32[]{:S(2)}) collective-permute-start(bf16[24,29184]{1,0:T(8,128)(2,1)S(1)} %copy-done.57), channel_id=1, source_target_pairs={{0,2},{1,3},{2,0},{3,1},{4,6},{5,7},{6,4},{7,5},{8,10},{9,11},{10,... | collective-permute-start | bytes 4202504 | tf_op jit(solution)/shard_map/ppermute | solution.py:666
  1105.4 27.2 %all-to-all-start.12 = ((bf16[8,144,768]{2,1,0:T(8,128)(2,1)}), bf16[8,144,768]{2,1,0:T(8,128)(2,1)S(1)}, u32[]{:S(2)}, u32[]{:S(2)}) async-start(bf16[8,144,768]{2,1,0:T(8,128)(2,1)} %synthesis_back.3), calls=%async_computation.12 | async-start | bytes 3538944 | tf_op jit(solution)/shard_map/all_to_all | solution.py:595
  1133.8 84.9 %all-to-all-start.13 = ((bf16[8,576,768]{2,1,0:T(8,128)(2,1)}), bf16[8,576,768]{2,1,0:T(8,128)(2,1)}, u32[]{:S(2)}, u32[]{:S(2)}) async-start(bf16[8,576,768]{2,1,0:T(8,128)(2,1)} %get-tuple-element.194), calls=%async_computation.13 | async-start | bytes 14155776 | tf_op jit(solution)/shard_map/all_to_all | solution.py:595
  1138.7 154.1 %reduce-scatter.10.cloned.1.call-start = ((), (), s32[]{:S(2)}) async-start(), calls=%async_computation.23 | async-start | bytes 7741440 | tf_op jit(solution)/shard_map/reduce_scatter | solution.py:761
  1138.8 24.0 %collective-permute-start.15 = (bf16[6,29184]{1,0:T(8,128)(2,1)}, bf16[6,29184]{1,0:T(8,128)(2,1)S(1)}, u32[]{:S(2)}, u32[]{:S(2)}) collective-permute-start(bf16[6,29184]{1,0:T(8,128)(2,1)} %pad.62), channel_id=1, source_target_pairs={{0,1},{1,0},{2,3},{3,2},{4,5},{5,4},{6,7},{7,6},{8,9},{9,8},{10,11... | collective-permute-start | bytes 1050632 | tf_op jit(solution)/shard_map/ppermute | solution.py:666
  1139.8 34.7 %collective-permute-start.16 = (bf16[6,29184]{1,0:T(8,128)(2,1)}, bf16[6,29184]{1,0:T(8,128)(2,1)S(1)}, u32[]{:S(2)}, u32[]{:S(2)}) collective-permute-start(bf16[6,29184]{1,0:T(8,128)(2,1)} %pad.63), channel_id=1, source_target_pairs={{0,2},{1,3},{2,0},{3,1},{4,6},{5,7},{6,4},{7,5},{8,10},{9,11},{10,... | collective-permute-start | bytes 1050632 | tf_op jit(solution)/shard_map/ppermute | solution.py:666
  1142.3 33.1 %collective-permute-start.17 = (bf16[6,29184]{1,0:T(8,128)(2,1)}, bf16[6,29184]{1,0:T(8,128)(2,1)S(1)}, u32[]{:S(2)}, u32[]{:S(2)}) collective-permute-start(bf16[6,29184]{1,0:T(8,128)(2,1)} %pad.64), channel_id=1, source_target_pairs={{0,3},{1,2},{2,1},{3,0},{4,7},{5,6},{6,5},{7,4},{8,11},{9,10},{10,... | collective-permute-start | bytes 1050632 | tf_op jit(solution)/shard_map/ppermute | solution.py:666
  1218.7 27.5 %all-to-all-start.14 = ((bf16[8,144,768]{2,1,0:T(8,128)(2,1)}), bf16[8,144,768]{2,1,0:T(8,128)(2,1)}, u32[]{:S(2)}, u32[]{:S(2)}) async-start(bf16[8,144,768]{2,1,0:T(8,128)(2,1)} %get-tuple-element.201), calls=%async_computation.14 | async-start | bytes 3538944 | tf_op jit(solution)/shard_map/all_to_all | solution.py:595
  1246.2 84.9 %all-to-all-start.15 = ((bf16[8,576,768]{2,1,0:T(8,128)(2,1)}), bf16[8,576,768]{2,1,0:T(8,128)(2,1)}, u32[]{:S(2)}, u32[]{:S(2)}) async-start(bf16[8,576,768]{2,1,0:T(8,128)(2,1)} %analysis_back.2), calls=%async_computation.15 | async-start | bytes 14155776 | tf_op jit(solution)/shard_map/all_to_all | solution.py:595
  1251.1 80.0 %reduce-scatter.14.cloned.1.call-start = ((), (), s32[]{:S(2)}) async-start(), calls=%async_computation.25 | async-start | bytes 737280 | tf_op jit(solution)/shard_map/reduce_scatter | solution.py:781
  1253.7 152.9 %all-gather.8.cloned.1.call-start = ((), (), s32[]{:S(2)}) async-start(), calls=%async_computation.26 | async-start | bytes 1327104 | tf_op jit(solution)/shard_map/all_gather | solution.py:782
  1331.1 214.6 %reduce-scatter.12.cloned.1.call-start = ((), (), s32[]{:S(2)}) async-start(), calls=%async_computation.24 | async-start | bytes 7741440 | tf_op jit(solution)/shard_map/reduce_scatter | solution.py:761
  1336.3 121.1 %all-to-all-start.16 = ((bf16[32,36,768]{2,1,0:T(8,128)(2,1)}), bf16[32,36,768]{2,1,0:T(8,128)(2,1)}, u32[]{:S(2)}, u32[]{:S(2)}) async-start(bf16[32,36,768]{2,1,0:T(8,128)(2,1)} %analysis_back.3), calls=%async_computation.17 | async-start | bytes 3932160 | tf_op jit(solution)/shard_map/all_to_all | solution.py:595
  1370.5 231.5 %collective-permute-start.20 = (bf16[24,29184]{1,0:T(8,128)(2,1)}, bf16[24,29184]{1,0:T(8,128)(2,1)}, u32[]{:S(2)}, u32[]{:S(2)}) collective-permute-start(bf16[24,29184]{1,0:T(8,128)(2,1)} %pad.70), channel_id=1, source_target_pairs={{0,3},{1,2},{2,1},{3,0},{4,7},{5,6},{6,5},{7,4},{8,11},{9,10},{10,... | collective-permute-start | bytes 4202504 | tf_op jit(solution)/shard_map/ppermute | solution.py:666
  1405.9 261.1 %collective-permute-start.19 = (bf16[24,29184]{1,0:T(8,128)(2,1)}, bf16[24,29184]{1,0:T(8,128)(2,1)}, u32[]{:S(2)}, u32[]{:S(2)}) collective-permute-start(bf16[24,29184]{1,0:T(8,128)(2,1)} %pad.69), channel_id=1, source_target_pairs={{0,2},{1,3},{2,0},{3,1},{4,6},{5,7},{6,4},{7,5},{8,10},{9,11},{10,... | collective-permute-start | bytes 4202504 | tf_op jit(solution)/shard_map/ppermute | solution.py:666
  1405.9 261.1 %collective-permute-start.18 = (bf16[24,29184]{1,0:T(8,128)(2,1)}, bf16[24,29184]{1,0:T(8,128)(2,1)}, u32[]{:S(2)}, u32[]{:S(2)}) collective-permute-start(bf16[24,29184]{1,0:T(8,128)(2,1)} %pad.68), channel_id=1, source_target_pairs={{0,1},{1,0},{2,3},{3,2},{4,5},{5,4},{6,7},{7,6},{8,9},{9,8},{10,11... | collective-permute-start | bytes 4202504 | tf_op jit(solution)/shard_map/ppermute | solution.py:666
  1562.3 104.7 %collective-permute-start.23 = (bf16[6,29184]{1,0:T(8,128)(2,1)}, bf16[6,29184]{1,0:T(8,128)(2,1)S(1)}, u32[]{:S(2)}, u32[]{:S(2)}) collective-permute-start(bf16[6,29184]{1,0:T(8,128)(2,1)} %pad.74), channel_id=1, source_target_pairs={{0,3},{1,2},{2,1},{3,0},{4,7},{5,6},{6,5},{7,4},{8,11},{9,10},{10,... | collective-permute-start | bytes 1050632 | tf_op jit(solution)/shard_map/ppermute | solution.py:666
  1562.9 104.1 %collective-permute-start.22 = (bf16[6,29184]{1,0:T(8,128)(2,1)}, bf16[6,29184]{1,0:T(8,128)(2,1)S(1)}, u32[]{:S(2)}, u32[]{:S(2)}) collective-permute-start(bf16[6,29184]{1,0:T(8,128)(2,1)} %pad.73), channel_id=1, source_target_pairs={{0,2},{1,3},{2,0},{3,1},{4,6},{5,7},{6,4},{7,5},{8,10},{9,11},{10,... | collective-permute-start | bytes 1050632 | tf_op jit(solution)/shard_map/ppermute | solution.py:666
  1602.0 65.0 %collective-permute-start.21 = (bf16[6,29184]{1,0:T(8,128)(2,1)}, bf16[6,29184]{1,0:T(8,128)(2,1)S(1)}, u32[]{:S(2)}, u32[]{:S(2)}) collective-permute-start(bf16[6,29184]{1,0:T(8,128)(2,1)} %pad.72), channel_id=1, source_target_pairs={{0,1},{1,0},{2,3},{3,2},{4,5},{5,4},{6,7},{7,6},{8,9},{9,8},{10,11... | collective-permute-start | bytes 1050632 | tf_op jit(solution)/shard_map/ppermute | solution.py:666
  (73 other events, 2449.8 us)
Sparse Core Ops, SparseCore 0:
  136.4 318.2 all-gather.9
  1334.4 211.2 reduce-scatter.11
Sparse Core Ops, SparseCore 1:
  398.2 69.2 reduce-scatter.15
  642.0 72.9 all-gather.5
  1032.7 79.7 reduce-scatter.17
  1176.2 116.5 reduce-scatter.9
  1295.6 22.4 reduce-scatter.13
  1331.2 24.0 all-gather.7
